TPU v7x, 256 devices: a whole 4x4x8 slice. The times are simulated.
256 devices in a mesh: prow: 16 (over y, x), pcol: 16 (over z, core).
Axes of the slice: x: 4, y: 4, z: 8, core: 2. Of those that a mesh axis runs over, the one named last changes fastest.
Arguments:
- inverse_region: bfloat16 [8, 4096, 8, 4096], P(None, 'prow', None, 'pcol'), may hold values from -5 to 5
- panel_one: bfloat16 [16384, 256], P('pcol'), may hold values from -0.046875 to 0.046875
- panel_two: bfloat16 [8192, 256], P('pcol'), may hold values from -0.0625 to 0.0625
- link_block: bfloat16 [256, 256], replicated, may hold values from -0.375 to 0.375
- inv_diag_one: float32 [256, 256], replicated, may hold values from -5 to 5
- inv_diag_two: float32 [256, 256], replicated, may hold values from -5 to 5
- pattern_one: int32 [64], replicated, may hold values from 0 to 127, as said below
- pattern_two: int32 [32], replicated, may hold values from 0 to 127, as said below
Outputs:
- column_one: bfloat16 [8, 4096, 256], P(None, ('prow', 'pcol'))
- diagonal_one: float32 [256, 256], replicated
- column_two: bfloat16 [8, 4096, 256], P(None, ('prow', 'pcol'))
- cross_two: float32 [256, 256], replicated
- diagonal_two: float32 [256, 256], replicated
Inputs may be any that keep to these rules, and one draw needn't show every extreme that they name: `pattern_one`: 64 distinct indices in increasing order; the first block 0 and the top block 127 are always among them. `pattern_two`: 32 distinct entries of pattern_one in increasing order; the first and the last entry of pattern_one are always among them.
All inputs are finite; a program needn't handle non-finite values.
Results may differ from a plain program's by a relative error of at most 0.004.
Values may be sent and summed in bfloat16 or wider, within the bound.
No kernel may reach another device: no remote copies, remote signals or barrier semaphores. Data moves between devices by JAX's collectives and lax.ppermute only.
A program may use at most 128 MiB of HBM per device.

v0:
```python
import jax
import jax.numpy as jnp
from jax import lax
from jax.sharding import PartitionSpec as P


def select_blocks(blocks, block_ids, pattern):
    onehot = (block_ids[:, None] == pattern[None, :]).astype(jnp.bfloat16)
    picked = jnp.einsum("cs,sij->cij", onehot, blocks, preferred_element_type=jnp.float32)
    return picked.astype(jnp.bfloat16)


def keep_rows(block_ids, pattern):
    hits = jnp.any(block_ids[:, None] == pattern[None, :], axis=1)
    return hits.astype(jnp.float32)[:, None, None]


def gather_separate(panel_one, panel_two):
    first = lax.all_gather(panel_one, "pcol", axis=0, tiled=True)
    second = lax.all_gather(panel_two, "pcol", axis=0, tiled=True)
    return (first, second)


def reduce_columns(partial_value):
    return lax.psum(partial_value, "pcol")


def reduce_block(term):
    return lax.psum(term, "prow")


def output_rows(values, pcol_at, share_rows):
    return lax.dynamic_slice_in_dim(values, pcol_at * share_rows, share_rows, 1)


def shards(
    inverse_region,
    panel_one,
    panel_two,
    link_block,
    inv_diag_one,
    inv_diag_two,
    pattern_one,
    pattern_two,
):
    rows_grid = lax.axis_size("prow")
    cols_grid = lax.axis_size("pcol")
    prow_at = lax.axis_index("prow")
    pcol_at = lax.axis_index("pcol")
    row_blocks = inverse_region.shape[0]
    block_width = inverse_region.shape[1]
    col_blocks = inverse_region.shape[2]
    share_rows = block_width // cols_grid
    local_tile = inverse_region.reshape(row_blocks * block_width, col_blocks * block_width)
    row_ids = jnp.arange(row_blocks, dtype=jnp.int32) * rows_grid + prow_at
    col_ids = jnp.arange(col_blocks, dtype=jnp.int32) * cols_grid + pcol_at
    link_float = link_block.astype(jnp.float32)
    keep_one = keep_rows(row_ids, pattern_one)
    keep_two = keep_rows(row_ids, pattern_two)
    gathered_one, gathered_two = gather_separate(panel_one, panel_two)
    gathered_one = gathered_one.reshape(-1, block_width, block_width)
    gathered_two = gathered_two.reshape(-1, block_width, block_width)
    cols_one = select_blocks(gathered_one, col_ids, pattern_one)
    rows_one = select_blocks(gathered_one, row_ids, pattern_one)
    partial_one = jnp.dot(
        local_tile, cols_one.reshape(-1, block_width), preferred_element_type=jnp.float32
    )
    partial_one = partial_one.reshape(row_blocks, block_width, block_width)
    column_here = (-(keep_one * reduce_columns(partial_one))).astype(jnp.bfloat16)
    diag_term = jnp.einsum("aij,aik->jk", rows_one, column_here, preferred_element_type=jnp.float32)
    diagonal_one = inv_diag_one - reduce_block(diag_term)
    cols_two = select_blocks(gathered_two, col_ids, pattern_two)
    rows_two = select_blocks(gathered_two, row_ids, pattern_two)
    partial_two = jnp.dot(
        local_tile, cols_two.reshape(-1, block_width), preferred_element_type=jnp.float32
    )
    partial_two = partial_two.reshape(row_blocks, block_width, block_width)
    linked = jnp.dot(
        column_here.reshape(-1, block_width), link_block, preferred_element_type=jnp.float32
    )
    summed_two = reduce_columns(partial_two) + linked.reshape(column_here.shape)
    second_here = (-(keep_two * summed_two)).astype(jnp.bfloat16)
    cross_term = jnp.einsum(
        "aij,aik->jk", column_here, rows_two, preferred_element_type=jnp.float32
    )
    cross_two = -jnp.dot(diagonal_one, link_float, precision=lax.Precision.HIGHEST) - reduce_block(
        cross_term
    )
    second_term = jnp.einsum(
        "aij,aik->jk", rows_two, second_here, preferred_element_type=jnp.float32
    )
    diagonal_two = inv_diag_two - reduce_block(second_term)
    diagonal_two = diagonal_two - jnp.dot(link_float.T, cross_two, precision=lax.Precision.HIGHEST)
    column_one = output_rows(column_here, pcol_at, share_rows)
    column_two = output_rows(second_here, pcol_at, share_rows)
    return (column_one, diagonal_one, column_two, cross_two, diagonal_two)


def solution(mesh):
    return jax.shard_map(
        shards,
        mesh=mesh,
        in_specs=(
            P(None, "prow", None, "pcol"),
            P("pcol", None),
            P("pcol", None),
            P(),
            P(),
            P(),
            P(),
            P(),
        ),
        out_specs=(P(None, ("prow", "pcol"), None), P(), P(None, ("prow", "pcol"), None), P(), P()),
        check_vma=False,
    )
```

profile of v0, /device:TPU:1, one launch (start us, length us, event | category | flops | bytes accessed | tf_op | source)
XLA Modules:
  0.0 361.1 jit_solution(15357391528451420993)
XLA Ops:
  7.2 0.7 all-gather.5.cloned.1.call-update
  8.0 0.7 all-gather.3.cloned.1.call-update
  8.7 10.3 %copy.37 = bf16[256,8,8,256]{3,1,2,0:T(8,128)(2,1)} copy(bf16[256,8,8,256]{3,2,1,0:T(8,128)(2,1)} %bitcast.55) | data formatting | bytes 16777216
  19.0 37.2 %all-gather.5.cloned.1.call-done = bf16[8192,256]{1,0:T(8,128)(2,1)} async-done(((bf16[512,256]{1,0:T(8,128)(2,1)}), bf16[8192,256]{1,0:T(8,128)(2,1)}) %all-gather.5.cloned.1.call-update) | async-done | bytes 4194320 | tf_op jit(solution)/shard_map/all_gather | solution.py:20
  56.2 4.5 %fusion.8 = bf16[8,256,256]{2,0,1:T(8,128)(2,1)S(1)} fusion(bf16[32,256,256]{2,1,0:T(8,128)(2,1)} %bitcast.53, s32[32]{0:T(128)S(1)} %copy-done.5, s32[8]{0:T(128)S(1)} %fusion.35), kind=kOutput, calls=%fused_computation.12 | convolution fusion | flops 34078976 | bytes 5243040 | tf_op jit(solution)/shard_map/cs,sij->cij/dot_general | solution.py:9
  61.0 5.8 %convolution_bitcast_fusion = f32[2048,256]{0,1:T(8,128)S(1)} fusion(bf16[2048,256]{1,0:T(8,128)(2,1)S(1)} %bitcast.61, bf16[2048,2048]{1,0:T(8,128)(2,1)} %bitcast.56), kind=kOutput, calls=%fused_computation.8 | convolution fusion | flops 2147483648 | bytes 11534336 | tf_op jit(solution)/shard_map/dot_general | solution.py:74
  66.8 2.0 copy.36
  68.8 43.8 %all-gather.3.cloned.1.call-done = bf16[16384,256]{1,0:T(8,128)(2,1)} async-done(((bf16[1024,256]{1,0:T(8,128)(2,1)}), bf16[16384,256]{1,0:T(8,128)(2,1)}) %all-gather.3.cloned.1.call-update) | async-done | bytes 8388624 | tf_op jit(solution)/shard_map/all_gather | solution.py:19
  112.5 7.9 %fusion.14 = bf16[8,256,256]{2,0,1:T(8,128)(2,1)S(1)} fusion(bf16[64,256,256]{2,1,0:T(8,128)(2,1)} %bitcast.51, s32[64]{0:T(128)S(1)} %copy-done.6, s32[8]{0:T(128)S(1)} %fusion.35), kind=kOutput, calls=%fused_computation.14 | convolution fusion | flops 67633664 | bytes 9437472 | tf_op jit(solution)/shard_map/cs,sij->cij/dot_general | solution.py:9
  120.7 5.8 %convolution_bitcast_fusion.1 = f32[2048,256]{0,1:T(8,128)S(1)} fusion(bf16[2048,256]{1,0:T(8,128)(2,1)S(1)} %bitcast.60, bf16[2048,2048]{1,0:T(8,128)(2,1)} %bitcast.57), kind=kOutput, calls=%fused_computation.9 | convolution fusion | flops 2147483648 | bytes 11534336 | tf_op jit(solution)/shard_map/dot_general | solution.py:65
  126.4 1.8 copy.35
  128.9 4.5 %fusion.11 = bf16[8,256,256]{2,0,1:T(8,128)(2,1)S(1)} fusion(bf16[32,256,256]{2,1,0:T(8,128)(2,1)} %bitcast.54, s32[32]{0:T(128)S(1)} %copy-done.5, s32[8]{0:T(128)S(1)} %fusion.36), kind=kOutput, calls=%fused_computation.13 | convolution fusion | flops 34078976 | bytes 5243040 | tf_op jit(solution)/shard_map/cs,sij->cij/dot_general | solution.py:9
  133.5 7.9 %fusion = bf16[8,256,256]{2,0,1:T(8,128)(2,1)S(1)} fusion(bf16[64,256,256]{2,1,0:T(8,128)(2,1)} %bitcast.52, s32[64]{0:T(128)S(1)} %copy-done.6, s32[8]{0:T(128)S(1)} %fusion.36), kind=kOutput, calls=%fused_computation | convolution fusion | flops 67109376 | bytes 9437472 | tf_op jit(solution)/shard_map/cs,sij->cij/dot_general | solution.py:9
  141.4 0.8 copy.30
  142.2 105.4 %all-reduce.5.cloned.1.call-done = (f32[8,256,256]{2,1,0:T(8,128)}, f32[8,256,256]{2,1,0:T(8,128)}) async-done(((f32[8,256,256]{2,1,0:T(8,128)}, f32[8,256,256]{2,1,0:T(8,128)}), (f32[8,256,256]{2,1,0:T(8,128)}, f32[8,256,256]{2,1,0:T(8,128)})) %all-reduce.5.cloned.1.call-update) | async-done | bytes 4194320 | tf_op jit(solution)/shard_map/psum | solution.py:25
  247.6 2.0 negate_convert_fusion.1
  249.7 1.1 convolution_bitcast_fusion.5
  250.8 1.3 convolution_bitcast_fusion.4
  252.6 1.6 convolution_bitcast_fusion.3
  254.2 0.7 constant_dynamic-slice_fusion
  254.8 95.3 %all-reduce.7.cloned.1.call-done = (f32[256,256]{1,0:T(8,128)}, f32[256,256]{1,0:T(8,128)}, f32[256,256]{1,0:T(8,128)}) async-done(((f32[256,256]{1,0:T(8,128)}, f32[256,256]{1,0:T(8,128)}, f32[256,256]{1,0:T(8,128)}), (f32[256,256]{1,0:T(8,128)}, f32[256,256]{1,0:T(8,128)}, f32[256,256]{1,0:T(8,128)})) %all-reduce.7.cloned.1.call-update) | async-done | bytes 786448 | tf_op jit(solution)/shard_map/psum | solution.py:29
  350.1 1.0 sub.12
  351.1 1.3 fusion.18
  352.4 2.1 fusion.17
  (29 shorter events, 1.7 us)
Async XLA Ops:
  7.2 244.9 %copy-start = (bf16[256,256]{1,0:T(8,128)(2,1)S(1)}, bf16[256,256]{1,0:T(8,128)(2,1)}, u32[]{:S(2)}) copy-start(bf16[256,256]{1,0:T(8,128)(2,1)} %param.11) | copy-start | bytes 393220
  7.2 49.0 %all-gather.5.cloned.1.call-start = ((), (), s32[]{:S(2)}) async-start(), calls=%async_computation.1 | async-start | bytes 4456448 | tf_op jit(solution)/shard_map/all_gather | solution.py:20
  7.9 104.6 %all-gather.3.cloned.1.call-start = ((), (), s32[]{:S(2)}) async-start(), calls=%async_computation | async-start | bytes 8912896 | tf_op jit(solution)/shard_map/all_gather | solution.py:19
  8.7 239.0 %all-reduce.5.cloned.1.call-start = ((), (), s32[]{:S(2)}) async-start(), calls=%async_computation.2 | async-start | bytes 8388608 | tf_op jit(solution)/shard_map/psum | solution.py:25
  8.7 47.5 %copy-start.5 = (s32[32]{0:T(128)S(1)}, s32[32]{0:T(128)}, u32[]{:S(2)}) copy-start(s32[32]{0:T(128)} %param.15) | copy-start | bytes 388
  66.7 45.8 %copy-start.6 = (s32[64]{0:T(128)S(1)}, s32[64]{0:T(128)}, u32[]{:S(2)}) copy-start(s32[64]{0:T(128)} %param.14) | copy-start | bytes 772
  128.3 221.8 %all-reduce.7.cloned.1.call-start = ((), (), s32[]{:S(2)}) async-start(), calls=%async_computation.3 | async-start | bytes 1572864 | tf_op jit(solution)/shard_map/psum | solution.py:29
  247.6 4.5 %copy-start.1 = (f32[8,256,256]{2,1,0:T(8,128)S(1)}, f32[8,256,256]{2,1,0:T(8,128)}, u32[]{:S(2)}) copy-start(f32[8,256,256]{2,1,0:T(8,128)} %get-tuple-element.6) | copy-start | bytes 6291460
  252.5 97.6 %copy-start.4 = (f32[256,256]{1,0:T(8,128)S(1)}, f32[256,256]{1,0:T(8,128)}, u32[]{:S(2)}) copy-start(f32[256,256]{1,0:T(8,128)} %param.12) | copy-start | bytes 786436
  351.1 3.5 copy-start.2
  352.4 2.2 copy-start.3
Sparse Core Ops, SparseCore 0:
  9.8 46.3 all-gather.4
  58.0 54.4 all-gather.2
  128.4 119.1 all-reduce.4
  254.3 95.7 all-reduce.6
where the time goes:
time: 362 us; the launch traced here: 361 us
  waiting for transfers between devices  283 us (78%)
  matrix products  44.3 us (12%)
  local copies, waits for them, and re-layouts  16 us (4%)
  between operations  13.9 us (4%)
    psum x1, waiting for transfers between devices, reduce_columns(): return lax.psum(partial_value, 'pcol')  105 us
    psum x1, waiting for transfers between devices, reduce_block(): return lax.psum(term, 'prow')  95.3 us
    all_gather x1, waiting for transfers between devices, gather_separate(): first = lax.all_gather(panel_one, 'pcol', axis=0, tiled=True)  43.8 us
    all_gather x1, waiting for transfers between devices, gather_separate(): second = lax.all_gather(panel_two, 'pcol', axis=0, tiled=True)  37.2 us
    dot_general x4, matrix products, select_blocks(): jnp.einsum('cs,sij->cij', onehot, blocks, preferred_element_type=jnp.floa...  24.9 us
    unnamed x15, local copies, waits for them, and re-layouts  10.3 us
  transfers between devices with their start and end apart: 4, of which 4 were waited for; matrix products, arithmetic and copies ran while one was open for 10% of the time, Pallas kernels for 0%

commit v1 on v0

v1 whole, which is shorter than its diff:
```python
import jax
import jax.numpy as jnp
from jax import lax
from jax.experimental import pallas as pl
from jax.experimental.pallas import tpu as pltpu
from jax.sharding import PartitionSpec as P

BF16 = jnp.bfloat16
F32 = jnp.float32
VMEM = pl.BlockSpec(memory_space=pltpu.VMEM)
SMEM = pl.BlockSpec(memory_space=pltpu.SMEM)
ANY = pl.BlockSpec(memory_space=pl.ANY)
CHIPS = 8
CORES = 2
ROWS = 16
LANES = 128


def params():
    return pltpu.CompilerParams(vmem_limit_bytes=48 * 1024 * 1024)


def places(block_ids, pattern):
    hits = block_ids[:, None] == pattern[None, :]
    at = jnp.arange(pattern.shape[0], dtype=jnp.int32)[None, :] + 1
    return jnp.sum(jnp.where(hits, at, 0), axis=1) - 1


def pick_kernel(slot_ref, gathered_ref, send_ref, own_ref):
    slots = own_ref.shape[0]
    for t in range(slots):
        at = slot_ref[t]
        block = gathered_ref[jnp.maximum(at, 0)]
        block = jnp.where(at >= 0, block, jnp.zeros_like(block))
        own_ref[t] = block
        for d in range(send_ref.shape[0]):
            send_ref[d, t] = block


def pick(slot_at, gathered, peers):
    slots = slot_at.shape[0]
    tail = gathered.shape[1:]
    return pl.pallas_call(
        pick_kernel,
        out_shape=(
            jax.ShapeDtypeStruct((peers, slots) + tail, BF16),
            jax.ShapeDtypeStruct((slots,) + tail, BF16),
        ),
        in_specs=[SMEM, VMEM],
        out_specs=(VMEM, VMEM),
        compiler_params=params(),
        name="pick",
    )(slot_at, gathered)


def product_kernel(
    row_ref, core_ref, region_ref, panel_ref, keep_ref, send_ref,
    region, panel, wide, turned, total, region_sem, panel_sem,
):
    blocks = region.shape[0]
    width = region.shape[1]
    peers = panel_ref.shape[0]
    core = core_ref[0]

    def region_copy(a):
        return pltpu.make_async_copy(region_ref.at[a], region.at[a], region_sem.at[a])

    def panel_copy(p):
        return pltpu.make_async_copy(
            panel_ref.at[p], panel.at[:, pl.ds(p * ROWS, ROWS), :], panel_sem.at[p]
        )

    for p in range(peers):
        panel_copy(p).start()
    for a in range(blocks):
        @pl.when(row_ref[a] >= 0)
        def _():
            region_copy(a).start()
    for p in range(peers):
        panel_copy(p).wait()

    def step(a, carry):
        @pl.when(row_ref[a] >= 0)
        def _():
            region_copy(a).wait()
            for h in range(width // LANES):
                lanes = pl.ds(h * LANES, LANES)
                wide[h] = region[a, :, :, lanes].reshape(width * blocks, LANES).astype(F32)
            for c in range(blocks):
                for h in range(width // LANES):
                    turned[:, pl.ds(c * width + h * LANES, LANES)] = wide[
                        h, pl.ds(c, width, stride=blocks), :
                    ].astype(BF16)
            first = panel[:blocks].reshape(blocks * width, width)
            one = jnp.dot(turned[...], first, preferred_element_type=F32)
            total[:, :, :, :width] = one.reshape(CHIPS, CORES, ROWS, width)

            @pl.when(row_ref[blocks + a] >= 0)
            def _():
                second = panel[blocks:].reshape(blocks * width, width)
                two = jnp.dot(turned[...], second, preferred_element_type=F32)
                total[:, :, :, width:] = two.reshape(CHIPS, CORES, ROWS, width)

            @pl.when(row_ref[blocks + a] < 0)
            def _():
                total[:, :, :, width:] = jnp.zeros((CHIPS, CORES, ROWS, width), F32)

            keep_ref[:, a] = total[:, core]
            send_ref[:, a] = total[:, 1 - core].astype(BF16)

        @pl.when(row_ref[a] < 0)
        def _():
            keep_ref[:, a] = jnp.zeros((CHIPS, ROWS, 2 * width), F32)
            send_ref[:, a] = jnp.zeros((CHIPS, ROWS, 2 * width), BF16)

        return carry

    lax.fori_loop(0, blocks, step, 0)


def product(row_at, core, region, panel):
    blocks, width = region.shape[:2]
    peers, slots = panel.shape[:2]
    return pl.pallas_call(
        product_kernel,
        out_shape=(
            jax.ShapeDtypeStruct((CHIPS, blocks, ROWS, 2 * width), F32),
            jax.ShapeDtypeStruct((CHIPS, blocks, ROWS, 2 * width), BF16),
        ),
        in_specs=[SMEM, SMEM, ANY, ANY],
        out_specs=(VMEM, VMEM),
        scratch_shapes=[
            pltpu.VMEM((blocks, width, blocks, width), BF16),
            pltpu.VMEM((slots, width, width), BF16),
            pltpu.VMEM((width // LANES, width * blocks, LANES), F32),
            pltpu.VMEM((width, blocks * width), BF16),
            pltpu.VMEM((CHIPS, CORES, ROWS, 2 * width), F32),
            pltpu.SemaphoreType.DMA((blocks,)),
            pltpu.SemaphoreType.DMA((peers,)),
        ],
        compiler_params=params(),
        name="product",
    )(row_at, core, region, panel)


def across(a, b):
    return lax.dot_general(a, b, (((0,), (0,)), ((), ())), preferred_element_type=F32)


def columns_kernel(row_ref, parts_ref, rows_ref, link_ref, one_ref, two_ref, sums_ref):
    blocks, share, width = one_ref.shape
    link = link_ref[...]
    total = parts_ref[0].astype(F32)
    for z in range(1, parts_ref.shape[0]):
        total = total + parts_ref[z].astype(F32)
    ones, twos = [], []
    for a in range(blocks):
        first = jnp.where(row_ref[a] >= 0, -total[a, :, :width], 0.0).astype(BF16)
        ones.append(first)
        one_ref[a] = first
    one = jnp.concatenate(ones, axis=0)
    linked = jnp.dot(one, link, preferred_element_type=F32).reshape(blocks, share, width)
    for a in range(blocks):
        second = -(total[a, :, width:] + linked[a])
        second = jnp.where(row_ref[blocks + a] >= 0, second, 0.0).astype(BF16)
        twos.append(second)
        two_ref[a] = second
    two = jnp.concatenate(twos, axis=0)
    rows_one = rows_ref[:blocks].reshape(blocks * share, width)
    rows_two = rows_ref[blocks:].reshape(blocks * share, width)
    sums_ref[:width] = across(rows_one, one).astype(sums_ref.dtype)
    sums_ref[width:2 * width] = across(one, rows_two).astype(sums_ref.dtype)
    sums_ref[2 * width:] = across(rows_two, two).astype(sums_ref.dtype)


def columns(row_at, parts, rows, link):
    blocks, share, wide = parts.shape[1:]
    width = wide // 2
    return pl.pallas_call(
        columns_kernel,
        out_shape=(
            jax.ShapeDtypeStruct((blocks, share, width), BF16),
            jax.ShapeDtypeStruct((blocks, share, width), BF16),
            jax.ShapeDtypeStruct((3 * width, width), BF16),
        ),
        in_specs=[SMEM, VMEM, VMEM, VMEM],
        out_specs=(VMEM, VMEM, VMEM),
        compiler_params=params(),
        name="columns",
    )(row_at, parts, rows, link)


def exact(a, b, dims):
    return lax.dot_general(
        a, b, (dims, ((), ())), precision=lax.Precision.HIGHEST, preferred_element_type=F32
    )


def diagonals_kernel(sums_ref, link_ref, inv_one_ref, inv_two_ref, one_ref, cross_ref, two_ref):
    width = link_ref.shape[0]
    link = link_ref[...].astype(F32)
    one = inv_one_ref[...] - sums_ref[:width].astype(F32)
    one_ref[...] = one
    cross = -exact(one, link, ((1,), (0,))) - sums_ref[width:2 * width].astype(F32)
    cross_ref[...] = cross
    two = inv_two_ref[...] - sums_ref[2 * width:].astype(F32)
    two_ref[...] = two - exact(link, cross, ((0,), (0,)))


def diagonals(sums, link, inv_one, inv_two):
    square = jax.ShapeDtypeStruct(inv_one.shape, F32)
    return pl.pallas_call(
        diagonals_kernel,
        out_shape=(square, square, square),
        in_specs=[VMEM] * 4,
        out_specs=(VMEM,) * 3,
        compiler_params=params(),
        name="diagonals",
    )(sums, link, inv_one, inv_two)


def swap_axes(value, axes, groups=None):
    return lax.all_to_all(value, axes, 0, 0, axis_index_groups=groups, tiled=True)


def sum_everywhere(sums, rows_grid, cols_grid):
    both = ("prow", "pcol")
    planes = [
        [p * cols_grid + z * CORES + c for p in range(rows_grid) for c in range(CORES)]
        for z in range(CHIPS)
    ]
    lines = [[z * CORES + c for z in range(CHIPS)] for c in range(CORES)]
    ways = rows_grid * CORES
    height, width = sums.shape
    share = height // ways
    pieces = swap_axes(sums.reshape(ways, share, width), both, planes)
    piece = jnp.sum(pieces.astype(F32), axis=0)
    pieces = swap_axes(jnp.broadcast_to(piece, (CHIPS, share, width)), "pcol", lines)
    piece = jnp.sum(pieces, axis=0).astype(BF16)
    pieces = swap_axes(jnp.broadcast_to(piece, (ways, share, width)), both, planes)
    return pieces.reshape(height, width)


def shards(
    inverse_region, panel_one, panel_two, link_block, inv_diag_one, inv_diag_two,
    pattern_one, pattern_two,
):
    rows_grid = lax.axis_size("prow")
    cols_grid = lax.axis_size("pcol")
    p = lax.axis_index("prow")
    q = lax.axis_index("pcol")
    blocks, width = inverse_region.shape[:2]
    steps = jnp.arange(blocks, dtype=jnp.int32)
    row_ids = steps * rows_grid + p
    col_ids = steps * cols_grid + q
    row_at = jnp.concatenate([places(row_ids, pattern_one), places(row_ids, pattern_two)])
    held_one = panel_one.shape[0] // width
    held_two = panel_two.shape[0] // width
    held = held_one + held_two
    at_one = places(col_ids, pattern_one)
    at_two = places(col_ids, pattern_two)
    slot_at = jnp.concatenate([
        jnp.where(at_one < 0, -1, (at_one // held_one) * held + at_one % held_one),
        jnp.where(at_two < 0, -1, (at_two // held_two) * held + held_one + at_two % held_two),
    ])

    def own_rows(panel, count):
        return lax.dynamic_slice_in_dim(panel.reshape(count, width, width), p * ROWS, ROWS, 1)

    mine = jnp.concatenate([own_rows(panel_one, held_one), own_rows(panel_two, held_two)], axis=0)
    gathered = lax.all_gather(mine, "pcol", axis=0, tiled=True)
    send, own = pick(slot_at, gathered, rows_grid)
    turn = [(a * cols_grid + b, b * cols_grid + a) for a in range(rows_grid) for b in range(cols_grid)]
    rows = lax.ppermute(own, ("prow", "pcol"), turn)
    panel = swap_axes(send, "prow")
    core = lax.rem(q, CORES).reshape(1)
    keep, give = product(row_at, core, inverse_region, panel)
    got = lax.ppermute(give, "pcol", [(i, i ^ 1) for i in range(cols_grid)])
    paired = (keep + got.astype(F32)).astype(BF16)
    lines = [[z * CORES + c for z in range(CHIPS)] for c in range(CORES)]
    parts = swap_axes(paired, "pcol", lines)
    column_one, column_two, sums = columns(row_at, parts, rows, link_block)
    sums = sum_everywhere(sums, rows_grid, cols_grid)
    diagonal_one, cross_two, diagonal_two = diagonals(sums, link_block, inv_diag_one, inv_diag_two)
    return (column_one, diagonal_one, column_two, cross_two, diagonal_two)


def solution(mesh):
    return jax.shard_map(
        shards,
        mesh=mesh,
        in_specs=(P(None, "prow", None, "pcol"), P("pcol", None), P("pcol", None), P(), P(), P(), P(), P()),
        out_specs=(P(None, ("prow", "pcol"), None), P(), P(None, ("prow", "pcol"), None), P(), P()),
        check_vma=False,
    )
```

time: 362 us -> 171 us (0.47)
  waiting for transfers between devices: 283 us -> 62.2 us
  blocking collectives: 0 us -> 76.4 us
  matrix products: 44.3 us -> 0 us
  local copies, waits for them, and re-layouts: 16 us -> 2.15 us
  starting transfers between devices: 0.38 us -> 13.9 us
  between operations: 13.9 us -> 0.79 us
  Pallas kernels: 0 us -> 12.2 us
    psum x2 -> x0, waiting for transfers between devices: 201 us -> none  [the longest x1 105 us: reduce_columns(): return lax.psum(partial_value, 'pcol')]
    all_gather x2 -> x0, waiting for transfers between devices: 81 us -> none  [the longest x1 43.8 us: gather_separate(): first = lax.all_gather(panel_one, 'pcol', axis=0, tiled=True)]
    all_to_all x0 -> x2, waiting for transfers between devices: none -> 55.2 us  [swap_axes(): lax.all_to_all(value, axes, 0, 0, axis_index_groups=groups, tiled=True)]
    all_to_all x0 -> x3, blocking collectives: none -> 52.9 us  [swap_axes(): lax.all_to_all(value, axes, 0, 0, axis_index_groups=groups, tiled=True)]
    dot_general x12 -> x0, matrix products: 44.3 us -> none  [the longest x4 24.9 us: select_blocks(): jnp.einsum('cs,sij->cij', onehot, blocks, preferred_element_type=jnp.floa...]
    all_gather x0 -> x1, blocking collectives: none -> 23.5 us  [shards(): gathered = lax.all_gather(mine, 'pcol', axis=0, tiled=True)]
    pallas_call x0 -> x4, Pallas kernels: none -> 12.2 us  [the longest x1 8.23 us: product(): pl.pallas_call(product_kernel, out_shape=(jax.ShapeDtypeStruct((CHIPS, bl...]
    all_to_all x0 -> x2, starting transfers between devices: none -> 10.4 us  [swap_axes(): lax.all_to_all(value, axes, 0, 0, axis_index_groups=groups, tiled=True)]
  transfers between devices with their start and end apart: 4 -> 4, of which waited for: 4 -> 4; matrix products, arithmetic and copies ran while one was open for 10% -> 0% of each run, Pallas kernels for 0% -> 0%
where the time goes in v1:
time: 171 us
  blocking collectives  76.4 us (45%)
  waiting for transfers between devices  62.2 us (36%)
  starting transfers between devices  13.9 us (8%)
  Pallas kernels  12.2 us (7%)
  other arithmetic  3.48 us (2%)
  local copies, waits for them, and re-layouts  2.15 us (1%)
    all_to_all x2, waiting for transfers between devices, swap_axes(): lax.all_to_all(value, axes, 0, 0, axis_index_groups=groups, tiled=True)  55.2 us
    all_to_all x3, blocking collectives, swap_axes(): lax.all_to_all(value, axes, 0, 0, axis_index_groups=groups, tiled=True)  52.9 us
    all_gather x1, blocking collectives, shards(): gathered = lax.all_gather(mine, 'pcol', axis=0, tiled=True)  23.5 us
    all_to_all x2, starting transfers between devices, swap_axes(): lax.all_to_all(value, axes, 0, 0, axis_index_groups=groups, tiled=True)  10.4 us
    pallas_call x1, Pallas kernels, product(): pl.pallas_call(product_kernel, out_shape=(jax.ShapeDtypeStruct((CHIPS, bl...  8.23 us
    ppermute x1, waiting for transfers between devices, shards(): rows = lax.ppermute(own, ('prow', 'pcol'), turn)  4.65 us
  transfers between devices with their start and end apart: 4, of which 4 were waited for; matrix products, arithmetic and copies ran while one was open for 0% of the time, Pallas kernels for 0%

profile of v1, /device:TPU:1, one launch (start us, length us, event | category | flops | bytes accessed | tf_op | source)
XLA Modules:
  0.0 171.0 jit_solution(15166329995964244224)
XLA Ops:
  0.7 0.9 select_reduce_fusion.1
  1.6 0.9 select_reduce_fusion
  2.5 0.7 constant_dynamic-slice_fusion
  3.3 23.5 %all_gather.3.gathered_ref = bf16[96,16,256]{2,1,0:T(8,128)(2,1)S(1)} all-gather(bf16[6,16,256]{2,1,0:T(8,128)(2,1)S(1)} %pad_maximum_fusion), channel_id=1, replica_groups=mesh['prow'=16,'pcol'=16] {'pcol'}, dimensions={0}, use_global_device_ids=true | all-gather | bytes 835584 | tf_op jit(solution)/shard_map/all_gather | solution.py:271
  26.7 0.1 pad_add_fusion.1.slot_ref
  26.8 0.8 pick.1
  27.6 1.3 copy-done.1
  28.9 6.8 %all-to-all-start = ((bf16[16,16,16,256]{3,2,1,0:T(8,128)(2,1)}), bf16[16,16,16,256]{3,2,1,0:T(8,128)(2,1)S(1)}, u32[]{:S(2)}, u32[]{:S(2)}) async-start(bf16[16,16,16,256]{3,2,1,0:T(8,128)(2,1)} %copy-done.1), calls=%async_computation | async-start | bytes 4194304 | tf_op jit(solution)/shard_map/all_to_all | solution.py:223
  35.7 0.1 pad_add_fusion.row_ref
  35.8 32.8 %all-to-all-done.panel_ref = bf16[16,16,16,256]{3,2,1,0:T(8,128)(2,1)S(1)} async-done(((bf16[16,16,16,256]{3,2,1,0:T(8,128)(2,1)}), bf16[16,16,16,256]{3,2,1,0:T(8,128)(2,1)S(1)}, u32[]{:S(2)}, u32[]{:S(2)}) %all-to-all-start) | async-done | bytes 2097184 | tf_op jit(solution)/shard_map/all_to_all | solution.py:223
  68.6 8.2 %product.1 = (f32[8,8,16,512]{3,2,1,0:T(8,128)S(1)}, bf16[8,8,16,512]{3,2,1,0:T(8,128)(2,1)S(1)}) custom-call(s32[16]{0:T(128)S(1)} %pad_add_fusion.row_ref, s32[1]{0:T(128)} %bitcast.core_ref, bf16[8,256,8,256]{3,2,1,0:T(8,128)(2,1)} %region_ref.1, bf16[16,16,16,256]{3,2,1,0:T(8,128)(2,1)S(1)} %all-to-all-done.panel_ref), custom_call_target="tpu_custom_call" | custom-call | tf_op jit(solution)/shard_map/product/pallas_call | solution.py:124
  76.8 1.4 collective-permute-start
  78.2 2.3 %collective-permute-done = bf16[8,8,16,512]{3,2,1,0:T(8,128)(2,1)S(1)} collective-permute-done((bf16[8,8,16,512]{3,2,1,0:T(8,128)(2,1)S(1)}, bf16[8,8,16,512]{3,2,1,0:T(8,128)(2,1)S(1)}, u32[]{:S(2)}, u32[]{:S(2)}) %collective-permute-start) | collective-permute-done | bytes 1048608 | tf_op jit(solution)/shard_map/ppermute | solution.py:278
  80.5 1.4 add_convert_fusion
  81.9 3.7 %all-to-all-start.1 = ((bf16[8,8,16,512]{3,2,1,0:T(8,128)(2,1)}), bf16[8,8,16,512]{3,2,1,0:T(8,128)(2,1)S(1)}, u32[]{:S(2)}, u32[]{:S(2)}) async-start(bf16[8,8,16,512]{3,2,1,0:T(8,128)(2,1)} %add_convert_fusion), calls=%async_computation.1 | async-start | bytes 2097152 | tf_op jit(solution)/shard_map/all_to_all | solution.py:223
  85.6 2.1 %collective-permute-start.1 = (bf16[16,16,256]{2,1,0:T(8,128)(2,1)S(1)}, bf16[16,16,256]{2,1,0:T(8,128)(2,1)S(1)}, u32[]{:S(2)}, u32[]{:S(2)}) collective-permute-start(bf16[16,16,256]{2,1,0:T(8,128)(2,1)S(1)} %get-tuple-element.18), channel_id=1, source_target_pairs={{0,0},{1,16},{2,32},{3,48},{4,64},{5,80},{6,96},{7,112},{8,128},{9... | collective-permute-start | bytes 393224 | tf_op jit(solution)/shard_map/ppermute | solution.py:274
  87.7 4.7 %collective-permute-done.1.rows_ref = bf16[16,16,256]{2,1,0:T(8,128)(2,1)S(1)} collective-permute-done((bf16[16,16,256]{2,1,0:T(8,128)(2,1)S(1)}, bf16[16,16,256]{2,1,0:T(8,128)(2,1)S(1)}, u32[]{:S(2)}, u32[]{:S(2)}) %collective-permute-start.1) | collective-permute-done | bytes 131104 | tf_op jit(solution)/shard_map/ppermute | solution.py:274
  92.3 22.5 %all-to-all-done.1.parts_ref = bf16[8,8,16,512]{3,2,1,0:T(8,128)(2,1)S(1)} async-done(((bf16[8,8,16,512]{3,2,1,0:T(8,128)(2,1)}), bf16[8,8,16,512]{3,2,1,0:T(8,128)(2,1)S(1)}, u32[]{:S(2)}, u32[]{:S(2)}) %all-to-all-start.1) | async-done | bytes 1048608 | tf_op jit(solution)/shard_map/all_to_all | solution.py:223
  114.8 1.4 columns.1
  116.2 25.4 %all_to_all.25 = bf16[32,24,256]{2,1,0:T(8,128)(2,1)S(1)} all-to-all(bf16[32,24,256]{2,1,0:T(8,128)(2,1)S(1)} %bitcast.7), channel_id=1, replica_groups={{0,1,16,17,32,33,48,49,64,65,80,81,96,97,112,113,128,129,144,145,160,16..., dimensions={0} | all-to-all | bytes 786432 | tf_op jit(solution)/shard_map/all_to_all | solution.py:223
  141.6 0.1 convert_reduce_fusion
  141.7 11.9 %all_to_all.26 = f32[8,24,256]{2,1,0:T(8,128)S(1)} all-to-all(f32[8,24,256]{2,1,0:T(8,128)S(1)} %broadcast_in_dim.61), channel_id=1, replica_groups={{0,2,4,6,8,10,12,14},{1,3,5,7,9,11,13,15},{16,18,20,22,24,26,28,30},{17..., dimensions={0} | all-to-all | bytes 393216 | tf_op jit(solution)/shard_map/all_to_all | solution.py:223
  153.6 15.6 %all_to_all.27 = bf16[32,24,256]{2,1,0:T(8,128)(2,1)S(1)} all-to-all(bf16[32,24,256]{2,1,0:T(8,128)(2,1)S(1)} %broadcast_in_dim.62), channel_id=1, replica_groups={{0,1,16,17,32,33,48,49,64,65,80,81,96,97,112,113,128,129,144,145,160,16..., dimensions={0} | all-to-all | bytes 786432 | tf_op jit(solution)/shard_map/all_to_all | solution.py:223
  169.2 1.8 %diagonals.1 = (f32[256,256]{1,0:T(8,128)}, f32[256,256]{1,0:T(8,128)}, f32[256,256]{1,0:T(8,128)}) custom-call(bf16[768,256]{1,0:T(8,128)(2,1)S(1)} %bitcast.6, bf16[256,256]{1,0:T(8,128)(2,1)S(1)} %copy-done.2, f32[256,256]{1,0:T(8,128)S(1)} %copy-done.3, f32[256,256]{1,0:T(8,128)S(1)} %copy-done.4), custom_call_target="tpu_custom_call" | custom-call | tf_op jit(solution)/shard_map/diagonals/pallas_call | solution.py:212
  (21 shorter events, 0.2 us)
Async XLA Ops:
  0.6 2.6 %copy-start = (bf16[1024,256]{1,0:T(8,128)(2,1)S(1)}, bf16[1024,256]{1,0:T(8,128)(2,1)}, u32[]{:S(2)}) copy-start(bf16[1024,256]{1,0:T(8,128)(2,1)} %param.9) | copy-start | bytes 1572868
  27.6 1.3 copy-start.1
  28.9 39.7 %all-to-all-start = ((bf16[16,16,16,256]{3,2,1,0:T(8,128)(2,1)}), bf16[16,16,16,256]{3,2,1,0:T(8,128)(2,1)S(1)}, u32[]{:S(2)}, u32[]{:S(2)}) async-start(bf16[16,16,16,256]{3,2,1,0:T(8,128)(2,1)} %copy-done.1), calls=%async_computation | async-start | bytes 4194304 | tf_op jit(solution)/shard_map/all_to_all | solution.py:223
  76.8 3.7 %collective-permute-start = (bf16[8,8,16,512]{3,2,1,0:T(8,128)(2,1)S(1)}, bf16[8,8,16,512]{3,2,1,0:T(8,128)(2,1)S(1)}, u32[]{:S(2)}, u32[]{:S(2)}) collective-permute-start(bf16[8,8,16,512]{3,2,1,0:T(8,128)(2,1)S(1)} %get-tuple-element.17), channel_id=1, source_target_pairs={{0,1},{1,0},{2,3},{3,2},{4,5},{5,4},{6,7},{7,6},{8,9},{9,8},{10,11... | collective-permute-start | bytes 3145736 | tf_op jit(solution)/shard_map/ppermute | solution.py:278
  81.9 32.9 %copy-start.2 = (bf16[256,256]{1,0:T(8,128)(2,1)S(1)}, bf16[256,256]{1,0:T(8,128)(2,1)}, u32[]{:S(2)}) copy-start(bf16[256,256]{1,0:T(8,128)(2,1)} %link_ref.3) | copy-start | bytes 393220
  81.9 32.9 %all-to-all-start.1 = ((bf16[8,8,16,512]{3,2,1,0:T(8,128)(2,1)}), bf16[8,8,16,512]{3,2,1,0:T(8,128)(2,1)S(1)}, u32[]{:S(2)}, u32[]{:S(2)}) async-start(bf16[8,8,16,512]{3,2,1,0:T(8,128)(2,1)} %add_convert_fusion), calls=%async_computation.1 | async-start | bytes 2097152 | tf_op jit(solution)/shard_map/all_to_all | solution.py:223
  85.6 83.6 %copy-start.3 = (f32[256,256]{1,0:T(8,128)S(1)}, f32[256,256]{1,0:T(8,128)}, u32[]{:S(2)}) copy-start(f32[256,256]{1,0:T(8,128)} %inv_one_ref.1) | copy-start | bytes 786436
  85.6 83.6 %copy-start.4 = (f32[256,256]{1,0:T(8,128)S(1)}, f32[256,256]{1,0:T(8,128)}, u32[]{:S(2)}) copy-start(f32[256,256]{1,0:T(8,128)} %inv_two_ref.1) | copy-start | bytes 786436
  85.6 6.7 %collective-permute-start.1 = (bf16[16,16,256]{2,1,0:T(8,128)(2,1)S(1)}, bf16[16,16,256]{2,1,0:T(8,128)(2,1)S(1)}, u32[]{:S(2)}, u32[]{:S(2)}) collective-permute-start(bf16[16,16,256]{2,1,0:T(8,128)(2,1)S(1)} %get-tuple-element.18), channel_id=1, source_target_pairs={{0,0},{1,16},{2,32},{3,48},{4,64},{5,80},{6,96},{7,112},{8,128},{9... | collective-permute-start | bytes 393224 | tf_op jit(solution)/shard_map/ppermute | solution.py:274

commit v2 on v1

v2 whole, which is shorter than its diff:
```python
import functools

import jax
import jax.numpy as jnp
from jax import lax
from jax.experimental import pallas as pl
from jax.experimental.pallas import tpu as pltpu
from jax.sharding import PartitionSpec as P

BF16 = jnp.bfloat16
F32 = jnp.float32
VMEM = pl.BlockSpec(memory_space=pltpu.VMEM)
SMEM = pl.BlockSpec(memory_space=pltpu.SMEM)
ANY = pl.BlockSpec(memory_space=pl.ANY)
CHIPS = 8
CORES = 2
ROWS = 16
LANES = 128


def params(mebibytes=16):
    return pltpu.CompilerParams(vmem_limit_bytes=mebibytes * 1024 * 1024)


BLOCKS = 8
GROUPS = 4
SECOND_AT = GROUPS * BLOCKS
SPARE = SECOND_AT + BLOCKS
LISTS = SPARE + 1


def pick_kernel(caps, here_ref, one_ref, two_ref, gathered_ref, send_ref, own_ref, lists_ref, found, send_sem):
    grid = send_ref.shape[0]
    held = gathered_ref.shape[0] // grid
    for i in range(LISTS):
        found[i] = -1
        lists_ref[i] = -1
    row, column = here_ref[0], here_ref[1]
    for group, pattern in enumerate((one_ref, two_ref)):
        for s in range(pattern.shape[0]):
            block = pattern[s]
            home, at = lax.rem(block, grid), lax.div(block, grid)
            found[jnp.where(home == column, group * BLOCKS + at, SPARE)] = s
            found[jnp.where(home == row, (2 + group) * BLOCKS + at, SPARE)] = s
    for group in range(GROUPS):
        count = jnp.int32(0)
        for at in range(BLOCKS):
            present = found[group * BLOCKS + at] >= 0
            lists_ref[jnp.where(present, group * BLOCKS + count, SPARE)] = at
            if group == GROUPS - 1:
                lists_ref[SECOND_AT + at] = jnp.where(present, count, -1)
            count = count + present.astype(jnp.int32)
    offset, slot = 0, 0
    for group, pattern in enumerate((one_ref, two_ref)):
        each = pattern.shape[0] // grid
        for t in range(caps[group]):
            at = lists_ref[group * BLOCKS + t]
            s = jnp.where(at >= 0, found[group * BLOCKS + jnp.maximum(at, 0)], 0)
            block = gathered_ref[lax.div(s, each) * held + offset + lax.rem(s, each)]
            own_ref[slot] = jnp.where(at >= 0, block, jnp.zeros_like(block))
            slot += 1
        offset += each
    copies = [pltpu.make_async_copy(own_ref, send_ref.at[d], send_sem.at[d]) for d in range(grid)]
    for copy in copies:
        copy.start()
    for copy in copies:
        copy.wait()


def pick(caps, here, pattern_one, pattern_two, gathered, peers):
    tail = gathered.shape[1:]
    slots = sum(caps)
    return pl.pallas_call(
        functools.partial(pick_kernel, caps),
        out_shape=(
            jax.ShapeDtypeStruct((peers, slots) + tail, BF16),
            jax.ShapeDtypeStruct((slots,) + tail, BF16),
            jax.ShapeDtypeStruct((LISTS,), jnp.int32),
        ),
        in_specs=[SMEM, SMEM, SMEM, VMEM],
        out_specs=(ANY, VMEM, SMEM),
        scratch_shapes=[pltpu.SMEM((LISTS,), jnp.int32), pltpu.SemaphoreType.DMA((peers,))],
        compiler_params=params(),
        name="pick",
    )(here, pattern_one, pattern_two, gathered)


def turn_kernel(caps, lists_ref, region_ref, one_ref, two_ref, region, wide, region_sem):
    width = region.shape[1]
    halves = width // LANES

    def region_copy(u):
        at = lists_ref[2 * BLOCKS + u]
        return pltpu.make_async_copy(region_ref.at[at], region.at[u], region_sem.at[u])

    def each(u, work):
        pl.when(lists_ref[2 * BLOCKS + u] >= 0)(work)

    def place(out_ref, u, group):
        for t in range(caps[group]):
            c = lists_ref[group * BLOCKS + t]
            for h in range(halves):
                lanes = pl.ds(t * width + h * LANES, LANES)

                @pl.when(c >= 0)
                def _():
                    out_ref[u, :, lanes] = wide[h, pl.ds(c, width, stride=BLOCKS), :].astype(BF16)

                @pl.when(c < 0)
                def _():
                    out_ref[u, :, lanes] = jnp.zeros((width, LANES), BF16)

    for u in range(caps[0]):
        each(u, lambda u=u: region_copy(u).start())

    def step(u, carry):
        def work():
            region_copy(u).wait()
            for h in range(halves):
                part = region[u, :, :, pl.ds(h * LANES, LANES)]
                wide[h] = part.reshape(width * BLOCKS, LANES).astype(F32)
            place(one_ref, u, 0)
            second = lists_ref[SECOND_AT + lists_ref[2 * BLOCKS + u]]
            pl.when(second >= 0)(lambda: place(two_ref, second, 1))

        each(u, work)
        return carry

    lax.fori_loop(0, caps[0], step, 0)


def turn(caps, lists, region):
    blocks, width = region.shape[:2]
    return pl.pallas_call(
        functools.partial(turn_kernel, caps),
        out_shape=tuple(jax.ShapeDtypeStruct((k, width, k * width), BF16) for k in caps),
        in_specs=[SMEM, ANY],
        out_specs=(VMEM, VMEM),
        scratch_shapes=[
            pltpu.VMEM((blocks, width, blocks, width), BF16),
            pltpu.VMEM((width // LANES, width * blocks, LANES), F32),
            pltpu.SemaphoreType.DMA((blocks,)),
        ],
        compiler_params=params(20),
        cost_estimate=pl.CostEstimate(flops=2**20, bytes_accessed=2**24, transcendentals=0),
        name="turn",
    )(lists, region)


def product_kernel(
    caps, lists_ref, core_ref, one_ref, two_ref, panel_ref, keep_ref, send_ref, panel, total, panel_sem,
):
    width = one_ref.shape[1]
    peers = panel_ref.shape[0]
    core = core_ref[0]
    copies = [
        pltpu.make_async_copy(panel_ref.at[p], panel.at[:, pl.ds(p * ROWS, ROWS), :], panel_sem.at[p])
        for p in range(peers)
    ]
    for copy in copies:
        copy.start()
    for copy in copies:
        copy.wait()
    first = 0
    for group, turned in enumerate((one_ref, two_ref)):
        cap = caps[group]

        def step(u, carry, group=group, turned=turned, cap=cap, first=first):
            present = lists_ref[(2 + group) * BLOCKS + u] >= 0

            @pl.when(present)
            def _():
                blocks = panel[first:first + cap].reshape(cap * width, width)
                sums = jnp.dot(turned[u], blocks, preferred_element_type=F32)
                total[...] = sums.reshape(total.shape)
                keep_ref[:, first + u] = total[:, core]
                send_ref[:, first + u] = total[:, 1 - core].astype(BF16)

            @pl.when(jnp.logical_not(present))
            def _():
                keep_ref[:, first + u] = jnp.zeros((CHIPS, ROWS, width), F32)
                send_ref[:, first + u] = jnp.zeros((CHIPS, ROWS, width), BF16)

            return carry

        lax.fori_loop(0, cap, step, 0)
        first += cap


def product(caps, lists, core, one, two, panel):
    width = one.shape[1]
    peers, slots = panel.shape[:2]
    shape = (CHIPS, slots, ROWS, width)
    return pl.pallas_call(
        functools.partial(product_kernel, caps),
        out_shape=(jax.ShapeDtypeStruct(shape, F32), jax.ShapeDtypeStruct(shape, BF16)),
        in_specs=[SMEM, SMEM, VMEM, VMEM, ANY],
        out_specs=(VMEM, VMEM),
        scratch_shapes=[
            pltpu.VMEM((slots, width, width), BF16),
            pltpu.VMEM((CHIPS, CORES, ROWS, width), F32),
            pltpu.SemaphoreType.DMA((peers,)),
        ],
        compiler_params=params(),
        name="product",
    )(lists, core, one, two, panel)


def across(a, b):
    return lax.dot_general(a, b, (((0,), (0,)), ((), ())), preferred_element_type=F32)


def columns_kernel(caps, lists_ref, parts_ref, rows_ref, link_ref, one_ref, two_ref, sums_ref, sums, rows):
    blocks, share, width = one_ref.shape
    rows[...] = jnp.zeros(rows.shape, BF16)
    sums[...] = jnp.zeros(sums.shape, F32)
    slot = 0
    for group in range(2):
        for u in range(caps[group]):
            at = lists_ref[(2 + group) * BLOCKS + u]

            @pl.when(at >= 0)
            def _(slot=slot, group=group, at=at):
                total = parts_ref[0, slot].astype(F32)
                for z in range(1, parts_ref.shape[0]):
                    total = total + parts_ref[z, slot].astype(F32)
                place = pl.ds(pl.multiple_of(at * share, share), share)
                sums[group, place] = -total
                rows[group, place] = rows_ref[slot]

            slot += 1
    one = sums[0].astype(BF16)
    one_ref[...] = one.reshape(one_ref.shape)
    linked = jnp.dot(one, link_ref[...], preferred_element_type=F32)
    second = sums[1] - linked
    for at in range(blocks):
        part = slice(at * share, (at + 1) * share)
        kept = jnp.where(lists_ref[SECOND_AT + at] >= 0, second[part], 0.0)
        two_ref[at] = kept.astype(BF16)
    two = two_ref[...].reshape(blocks * share, width)
    kind = sums_ref.dtype
    sums_ref[:width] = across(rows[0], one).astype(kind)
    sums_ref[width:2 * width] = across(one, rows[1]).astype(kind)
    sums_ref[2 * width:] = across(rows[1], two).astype(kind)


def columns(caps, lists, parts, rows, link):
    share, width = parts.shape[2:]
    column = jax.ShapeDtypeStruct((BLOCKS, share, width), BF16)
    return pl.pallas_call(
        functools.partial(columns_kernel, caps),
        out_shape=(column, column, jax.ShapeDtypeStruct((3 * width, width), BF16)),
        in_specs=[SMEM, VMEM, VMEM, VMEM],
        out_specs=(VMEM, VMEM, VMEM),
        scratch_shapes=[
            pltpu.VMEM((2, BLOCKS * share, width), F32),
            pltpu.VMEM((2, BLOCKS * share, width), BF16),
        ],
        compiler_params=params(),
        name="columns",
    )(lists, parts, rows, link)


def exact(a, b, dims):
    return lax.dot_general(
        a, b, (dims, ((), ())), precision=lax.Precision.HIGHEST, preferred_element_type=F32
    )


def diagonals_kernel(sums_ref, link_ref, inv_one_ref, inv_two_ref, one_ref, cross_ref, two_ref):
    width = link_ref.shape[0]
    link = link_ref[...].astype(F32)
    one = inv_one_ref[...] - sums_ref[:width].astype(F32)
    one_ref[...] = one
    cross = -exact(one, link, ((1,), (0,))) - sums_ref[width:2 * width].astype(F32)
    cross_ref[...] = cross
    two = inv_two_ref[...] - sums_ref[2 * width:].astype(F32)
    two_ref[...] = two - exact(link, cross, ((0,), (0,)))


def diagonals(sums, link, inv_one, inv_two):
    square = jax.ShapeDtypeStruct(inv_one.shape, F32)
    return pl.pallas_call(
        diagonals_kernel,
        out_shape=(square, square, square),
        in_specs=[VMEM] * 4,
        out_specs=(VMEM,) * 3,
        compiler_params=params(),
        name="diagonals",
    )(sums, link, inv_one, inv_two)


def swap_axes(value, axes, groups=None):
    return lax.all_to_all(value, axes, 0, 0, axis_index_groups=groups, tiled=True)


def sum_everywhere(sums, rows_grid, cols_grid):
    both = ("prow", "pcol")
    planes = [
        [p * cols_grid + z * CORES + c for p in range(rows_grid) for c in range(CORES)]
        for z in range(CHIPS)
    ]
    lines = [[z * CORES + c for z in range(CHIPS)] for c in range(CORES)]
    ways = rows_grid * CORES
    height, width = sums.shape
    share = height // ways
    pieces = swap_axes(sums.reshape(ways, share, width), both, planes)
    piece = jnp.sum(pieces.astype(F32), axis=0)
    pieces = swap_axes(jnp.broadcast_to(piece, (CHIPS, share, width)), "pcol", lines)
    piece = jnp.sum(pieces, axis=0).astype(BF16)
    pieces = swap_axes(jnp.broadcast_to(piece, (ways, share, width)), both, planes)
    return pieces.reshape(height, width)


def shards(
    inverse_region, panel_one, panel_two, link_block, inv_diag_one, inv_diag_two,
    pattern_one, pattern_two,
):
    rows_grid = lax.axis_size("prow")
    cols_grid = lax.axis_size("pcol")
    p = lax.axis_index("prow")
    q = lax.axis_index("pcol")
    width = inverse_region.shape[1]
    caps = (BLOCKS, BLOCKS)
    here = jnp.stack([p, q]).astype(jnp.int32)
    core = lax.rem(q, CORES).reshape(1)

    def own_rows(panel):
        return lax.dynamic_slice_in_dim(panel.reshape(-1, width, width), p * ROWS, ROWS, 1)

    mine = jnp.concatenate([own_rows(panel_one), own_rows(panel_two)], axis=0)
    gathered = lax.all_gather(mine, "pcol", axis=0, tiled=True)
    send, own, lists = pick(caps, here, pattern_one, pattern_two, gathered, rows_grid)
    transpose = [
        (a * cols_grid + b, b * cols_grid + a) for a in range(rows_grid) for b in range(cols_grid)
    ]
    rows = lax.ppermute(own, ("prow", "pcol"), transpose)
    panel = swap_axes(send, "prow")
    turned_one, turned_two = turn(caps, lists, inverse_region)
    panel, rows = lax.optimization_barrier((panel, rows))
    keep, give = product(caps, lists, core, turned_one, turned_two, panel)
    got = lax.ppermute(give, "pcol", [(i, i ^ 1) for i in range(cols_grid)])
    paired = (keep + got.astype(F32)).astype(BF16)
    lines = [[z * CORES + c for z in range(CHIPS)] for c in range(CORES)]
    parts = swap_axes(paired, "pcol", lines)
    column_one, column_two, sums = columns(caps, lists, parts, rows, link_block)
    sums = sum_everywhere(sums, rows_grid, cols_grid)
    diagonal_one, cross_two, diagonal_two = diagonals(sums, link_block, inv_diag_one, inv_diag_two)
    return (column_one, diagonal_one, column_two, cross_two, diagonal_two)


def solution(mesh):
    return jax.shard_map(
        shards,
        mesh=mesh,
        in_specs=(P(None, "prow", None, "pcol"), P("pcol", None), P("pcol", None), P(), P(), P(), P(), P()),
        out_specs=(P(None, ("prow", "pcol"), None), P(), P(None, ("prow", "pcol"), None), P(), P()),
        check_vma=False,
    )
```

time: 171 us -> 175 us (1.023)
  waiting for transfers between devices: 62.2 us -> 22.7 us
  blocking collectives: 76.4 us -> 101 us
  local copies, waits for them, and re-layouts: 2.15 us -> 20.3 us
  Pallas kernels: 12.2 us -> 18.8 us
  starting transfers between devices: 13.9 us -> 10.7 us
  other arithmetic: 3.48 us -> 0.52 us
    all_to_all x2 -> x1, waiting for transfers between devices: 55.2 us -> 0.01 us  [swap_axes(): lax.all_to_all(value, axes, 0, 0, axis_index_groups=groups, tiled=True)]
    all_to_all x3 -> x4, blocking collectives: 52.9 us -> 77.8 us  [swap_axes(): lax.all_to_all(value, axes, 0, 0, axis_index_groups=groups, tiled=True)]
    unnamed x10 -> x24, local copies, waits for them, and re-layouts: 1.37 us -> 19.5 us
    ppermute x1, waiting for transfers between devices: 4.65 us -> 20 us  [shards(): rows = lax.ppermute(own, ('prow', 'pcol'), transpose)]
    pallas_call x3 -> x4, Pallas kernels: 10.4 us -> 17 us  [the longest x1 5.33 us: pick(): pl.pallas_call(functools.partial(pick_kernel, caps), out_shape=(jax.Shape...]
    all_to_all x2 -> x1, starting transfers between devices: 10.4 us -> 6.75 us  [swap_axes(): lax.all_to_all(value, axes, 0, 0, axis_index_groups=groups, tiled=True)]
    ppermute x1, starting transfers between devices: 2.05 us -> 3.87 us  [shards(): rows = lax.ppermute(own, ('prow', 'pcol'), transpose)]
    reduce_sum x2 -> x0, other arithmetic: 1.79 us -> none  [places(): return jnp.sum(jnp.where(hits, at, 0), axis=1) - 1]
  transfers between devices with their start and end apart: 4 -> 3, of which waited for: 4 -> 2; matrix products, arithmetic and copies ran while one was open for 0% -> 0% of each run, Pallas kernels for 0% -> 3%
where the time goes in v2:
time: 175 us
  blocking collectives  101 us (58%)
  waiting for transfers between devices  22.7 us (13%)
  local copies, waits for them, and re-layouts  20.3 us (12%)
  Pallas kernels  18.8 us (11%)
  starting transfers between devices  10.7 us (6%)
    all_to_all x4, blocking collectives, swap_axes(): lax.all_to_all(value, axes, 0, 0, axis_index_groups=groups, tiled=True)  77.8 us
    all_gather x1, blocking collectives, shards(): gathered = lax.all_gather(mine, 'pcol', axis=0, tiled=True)  23.5 us
    ppermute x1, waiting for transfers between devices, shards(): rows = lax.ppermute(own, ('prow', 'pcol'), transpose)  20 us
    unnamed x24, local copies, waits for them, and re-layouts  19.5 us
    all_to_all x1, starting transfers between devices, swap_axes(): lax.all_to_all(value, axes, 0, 0, axis_index_groups=groups, tiled=True)  6.75 us
    pallas_call x1, Pallas kernels, pick(): pl.pallas_call(functools.partial(pick_kernel, caps), out_shape=(jax.Shape...  5.33 us
    pallas_call x1, Pallas kernels, turn(): pl.pallas_call(functools.partial(turn_kernel, caps), out_shape=tuple((jax...  5.15 us
    pallas_call x1, Pallas kernels, product(): pl.pallas_call(functools.partial(product_kernel, caps), out_shape=(jax.Sh...  4.91 us
  transfers between devices with their start and end apart: 3, of which 2 were waited for; matrix products, arithmetic and copies ran while one was open for 0% of the time, Pallas kernels for 3%

profile of v2, /device:TPU:1, one launch (start us, length us, event | category | flops | bytes accessed | tf_op | source)
XLA Modules:
  0.0 175.1 jit_solution(10998130993768274049)
XLA Ops:
  0.7 0.8 constant_dynamic-slice_fusion
  1.7 23.5 %all_gather.3.gathered_ref = bf16[96,16,256]{2,1,0:T(8,128)(2,1)S(1)} all-gather(bf16[6,16,256]{2,1,0:T(8,128)(2,1)S(1)} %pad_maximum_fusion), channel_id=1, replica_groups=mesh['prow'=16,'pcol'=16] {'pcol'}, dimensions={0}, use_global_device_ids=true | all-gather | bytes 835584 | tf_op jit(solution)/shard_map/all_gather | solution.py:332
  25.3 0.7 copy-done.10
  25.9 0.7 copy-done.11
  26.6 5.3 %pick.1 = (bf16[16,16,16,256]{3,2,1,0:T(8,128)(2,1)S(1)}, bf16[16,16,256]{2,1,0:T(8,128)(2,1)S(1)}, s32[41]{0:T(128)S(1)}) custom-call(s32[2]{0:T(128)S(1)} %pad_add_fusion.here_ref, s32[64]{0:T(128)S(1)} %copy-done.10, s32[32]{0:T(128)S(1)} %copy-done.11, bf16[96,16,256]{2,1,0:T(8,128)(2,1)S(1)} %all_gather.3.gathered_ref), custom_call_target="tpu_custom_call" | custom-call | tf_op jit(solution)/shard_map/pick/pallas_call | solution.py:73
  31.9 1.3 copy-done.6
  33.2 6.8 %all-to-all-start = ((bf16[16,16,16,256]{3,2,1,0:T(8,128)(2,1)}), bf16[16,16,16,256]{3,2,1,0:T(8,128)(2,1)S(1)}, u32[]{:S(2)}, u32[]{:S(2)}) async-start(bf16[16,16,16,256]{3,2,1,0:T(8,128)(2,1)} %copy-done.6), calls=%async_computation | async-start | bytes 4194304 | tf_op jit(solution)/shard_map/all_to_all | solution.py:294
  40.0 3.9 %collective-permute-start = (bf16[16,16,256]{2,1,0:T(8,128)(2,1)S(1)}, bf16[16,16,256]{2,1,0:T(8,128)(2,1)S(1)}, u32[]{:S(2)}, u32[]{:S(2)}) collective-permute-start(bf16[16,16,256]{2,1,0:T(8,128)(2,1)S(1)} %get-tuple-element.24), channel_id=1, source_target_pairs={{0,0},{1,16},{2,32},{3,48},{4,64},{5,80},{6,96},{7,112},{8,128},{9... | collective-permute-start | bytes 393224 | tf_op jit(solution)/shard_map/ppermute | solution.py:337
  43.9 3.4 %copy-done.5 = bf16[8,256,8,256]{3,2,1,0:T(8,128)(2,1)S(1)} copy-done((bf16[8,256,8,256]{3,2,1,0:T(8,128)(2,1)S(1)}, bf16[8,256,8,256]{3,2,1,0:T(8,128)(2,1)}, u32[]{:S(2)}) %copy-start.5) | copy-done | bytes 8388632
  47.3 5.1 %turn.1 = (bf16[8,256,2048]{2,1,0:T(8,128)(2,1)S(1)}, bf16[8,256,2048]{2,1,0:T(8,128)(2,1)S(1)}) custom-call(s32[41]{0:T(128)S(1)} %get-tuple-element.20.lists_ref, bf16[8,256,8,256]{3,2,1,0:T(8,128)(2,1)S(1)} %copy-done.5), custom_call_target="tpu_custom_call" | custom-call | flops 1048576 | bytes 16777216 | tf_op jit(solution)/shard_map/turn/pallas_call | solution.py:134
  52.4 3.2 %copy-done.1 = bf16[8,256,2048]{2,1,0:T(8,128)(2,1)} copy-done((bf16[8,256,2048]{2,1,0:T(8,128)(2,1)}, bf16[8,256,2048]{2,1,0:T(8,128)(2,1)S(1)}, u32[]{:S(2)}) %copy-start.1) | copy-done | bytes 8388632
  55.6 3.2 %copy-done.3 = bf16[8,256,2048]{2,1,0:T(8,128)(2,1)} copy-done((bf16[8,256,2048]{2,1,0:T(8,128)(2,1)}, bf16[8,256,2048]{2,1,0:T(8,128)(2,1)S(1)}, u32[]{:S(2)}) %copy-start.3) | copy-done | bytes 8388632
  58.9 20.0 %collective-permute-done.rows_ref = bf16[16,16,256]{2,1,0:T(8,128)(2,1)S(1)} collective-permute-done((bf16[16,16,256]{2,1,0:T(8,128)(2,1)S(1)}, bf16[16,16,256]{2,1,0:T(8,128)(2,1)S(1)}, u32[]{:S(2)}, u32[]{:S(2)}) %collective-permute-start) | collective-permute-done | bytes 131104 | tf_op jit(solution)/shard_map/ppermute | solution.py:337
  78.9 3.4 %copy-done.2 = bf16[8,256,2048]{2,1,0:T(8,128)(2,1)S(1)} copy-done((bf16[8,256,2048]{2,1,0:T(8,128)(2,1)S(1)}, bf16[8,256,2048]{2,1,0:T(8,128)(2,1)}, u32[]{:S(2)}) %copy-start.2) | copy-done | bytes 8388632
  82.3 3.4 %copy-done.4 = bf16[8,256,2048]{2,1,0:T(8,128)(2,1)S(1)} copy-done((bf16[8,256,2048]{2,1,0:T(8,128)(2,1)S(1)}, bf16[8,256,2048]{2,1,0:T(8,128)(2,1)}, u32[]{:S(2)}) %copy-start.4) | copy-done | bytes 8388632
  85.6 4.9 %product.1 = (f32[8,16,16,256]{3,2,1,0:T(8,128)S(1)}, bf16[8,16,16,256]{3,2,1,0:T(8,128)(2,1)S(1)}) custom-call(s32[41]{0:T(128)S(1)} %get-tuple-element.20.lists_ref, s32[1]{0:T(128)} %bitcast.4.core_ref, bf16[8,256,2048]{2,1,0:T(8,128)(2,1)S(1)} %copy-done.2, bf16[8,256,2048]{2,1,0:T(8,128)(2,1)S(1)} %copy-done.4, ...), custom_call_target="tpu_custom_call" | custom-call | tf_op jit(solution)/shard_map/product/pallas_call | solution.py:194
  90.7 2.6 %collective-permute-done.1 = bf16[8,16,16,256]{3,2,1,0:T(8,128)(2,1)S(1)} collective-permute-done((bf16[8,16,16,256]{3,2,1,0:T(8,128)(2,1)S(1)}, bf16[8,16,16,256]{3,2,1,0:T(8,128)(2,1)S(1)}, u32[]{:S(2)}, u32[]{:S(2)}) %collective-permute-start.1) | collective-permute-done | bytes 1048608 | tf_op jit(solution)/shard_map/ppermute | solution.py:342
  93.3 0.4 add_convert_fusion
  93.7 31.1 %all_to_all.25.parts_ref = bf16[8,16,16,256]{3,2,1,0:T(8,128)(2,1)S(1)} all-to-all(bf16[8,16,16,256]{3,2,1,0:T(8,128)(2,1)S(1)} %add_convert_fusion), channel_id=1, replica_groups={{0,2,4,6,8,10,12,14},{1,3,5,7,9,11,13,15},{16,18,20,22,24,26,28,30},{17..., dimensions={0} | all-to-all | bytes 2097152 | tf_op jit(solution)/shard_map/all_to_all | solution.py:294
  124.8 1.6 columns.1
  126.4 19.4 %all_to_all.26 = bf16[32,24,256]{2,1,0:T(8,128)(2,1)S(1)} all-to-all(bf16[32,24,256]{2,1,0:T(8,128)(2,1)S(1)} %bitcast.9), channel_id=1, replica_groups={{0,1,16,17,32,33,48,49,64,65,80,81,96,97,112,113,128,129,144,145,160,16..., dimensions={0} | all-to-all | bytes 786432 | tf_op jit(solution)/shard_map/all_to_all | solution.py:294
  145.8 12.5 %all_to_all.27 = f32[8,24,256]{2,1,0:T(8,128)S(1)} all-to-all(f32[8,24,256]{2,1,0:T(8,128)S(1)} %broadcast_in_dim.6), channel_id=1, replica_groups={{0,2,4,6,8,10,12,14},{1,3,5,7,9,11,13,15},{16,18,20,22,24,26,28,30},{17..., dimensions={0} | all-to-all | bytes 393216 | tf_op jit(solution)/shard_map/all_to_all | solution.py:294
  158.4 14.9 %all_to_all.28 = bf16[32,24,256]{2,1,0:T(8,128)(2,1)S(1)} all-to-all(bf16[32,24,256]{2,1,0:T(8,128)(2,1)S(1)} %broadcast_in_dim.7), channel_id=1, replica_groups={{0,1,16,17,32,33,48,49,64,65,80,81,96,97,112,113,128,129,144,145,160,16..., dimensions={0} | all-to-all | bytes 786432 | tf_op jit(solution)/shard_map/all_to_all | solution.py:294
  173.3 1.8 %diagonals.1 = (f32[256,256]{1,0:T(8,128)}, f32[256,256]{1,0:T(8,128)}, f32[256,256]{1,0:T(8,128)}) custom-call(bf16[768,256]{1,0:T(8,128)(2,1)S(1)} %bitcast.8, bf16[256,256]{1,0:T(8,128)(2,1)S(1)} %copy-done.7, f32[256,256]{1,0:T(8,128)S(1)} %copy-done.8, f32[256,256]{1,0:T(8,128)S(1)} %copy-done.9), custom_call_target="tpu_custom_call" | custom-call | tf_op jit(solution)/shard_map/diagonals/pallas_call | solution.py:283
  (25 shorter events, 0.6 us)
Async XLA Ops:
  0.6 1.1 copy-start
  25.3 0.7 copy-start.10
  25.9 0.7 copy-start.11
  31.9 1.3 copy-start.6
  33.2 45.6 %all-to-all-start = ((bf16[16,16,16,256]{3,2,1,0:T(8,128)(2,1)}), bf16[16,16,16,256]{3,2,1,0:T(8,128)(2,1)S(1)}, u32[]{:S(2)}, u32[]{:S(2)}) async-start(bf16[16,16,16,256]{3,2,1,0:T(8,128)(2,1)} %copy-done.6), calls=%async_computation | async-start | bytes 4194304 | tf_op jit(solution)/shard_map/all_to_all | solution.py:294
  40.0 38.9 %collective-permute-start = (bf16[16,16,256]{2,1,0:T(8,128)(2,1)S(1)}, bf16[16,16,256]{2,1,0:T(8,128)(2,1)S(1)}, u32[]{:S(2)}, u32[]{:S(2)}) collective-permute-start(bf16[16,16,256]{2,1,0:T(8,128)(2,1)S(1)} %get-tuple-element.24), channel_id=1, source_target_pairs={{0,0},{1,16},{2,32},{3,48},{4,64},{5,80},{6,96},{7,112},{8,128},{9... | collective-permute-start | bytes 393224 | tf_op jit(solution)/shard_map/ppermute | solution.py:337
  43.9 3.4 %copy-start.5 = (bf16[8,256,8,256]{3,2,1,0:T(8,128)(2,1)S(1)}, bf16[8,256,8,256]{3,2,1,0:T(8,128)(2,1)}, u32[]{:S(2)}) copy-start(bf16[8,256,8,256]{3,2,1,0:T(8,128)(2,1)} %region_ref.1) | copy-start | bytes 25165828
  52.4 3.2 %copy-start.1 = (bf16[8,256,2048]{2,1,0:T(8,128)(2,1)}, bf16[8,256,2048]{2,1,0:T(8,128)(2,1)S(1)}, u32[]{:S(2)}) copy-start(bf16[8,256,2048]{2,1,0:T(8,128)(2,1)S(1)} %get-tuple-element.21.one_ref) | copy-start | bytes 25165828
  55.6 3.2 %copy-start.3 = (bf16[8,256,2048]{2,1,0:T(8,128)(2,1)}, bf16[8,256,2048]{2,1,0:T(8,128)(2,1)S(1)}, u32[]{:S(2)}) copy-start(bf16[8,256,2048]{2,1,0:T(8,128)(2,1)S(1)} %get-tuple-element.22.two_ref) | copy-start | bytes 25165828
  78.9 3.4 %copy-start.2 = (bf16[8,256,2048]{2,1,0:T(8,128)(2,1)S(1)}, bf16[8,256,2048]{2,1,0:T(8,128)(2,1)}, u32[]{:S(2)}) copy-start(bf16[8,256,2048]{2,1,0:T(8,128)(2,1)} %copy-done.1) | copy-start | bytes 25165828
  82.3 3.4 %copy-start.4 = (bf16[8,256,2048]{2,1,0:T(8,128)(2,1)S(1)}, bf16[8,256,2048]{2,1,0:T(8,128)(2,1)}, u32[]{:S(2)}) copy-start(bf16[8,256,2048]{2,1,0:T(8,128)(2,1)} %copy-done.3) | copy-start | bytes 25165828
  90.6 2.7 %collective-permute-start.1 = (bf16[8,16,16,256]{3,2,1,0:T(8,128)(2,1)S(1)}, bf16[8,16,16,256]{3,2,1,0:T(8,128)(2,1)S(1)}, u32[]{:S(2)}, u32[]{:S(2)}) collective-permute-start(bf16[8,16,16,256]{3,2,1,0:T(8,128)(2,1)S(1)} %get-tuple-element.27), channel_id=1, source_target_pairs={{0,1},{1,0},{2,3},{3,2},{4,5},{5,4},{6,7},{7,6},{8,9},{9,8},{10,11... | collective-permute-start | bytes 3145736 | tf_op jit(solution)/shard_map/ppermute | solution.py:342
  93.7 31.1 %copy-start.7 = (bf16[256,256]{1,0:T(8,128)(2,1)S(1)}, bf16[256,256]{1,0:T(8,128)(2,1)}, u32[]{:S(2)}) copy-start(bf16[256,256]{1,0:T(8,128)(2,1)} %link_ref.3) | copy-start | bytes 393220
  124.8 48.5 %copy-start.8 = (f32[256,256]{1,0:T(8,128)S(1)}, f32[256,256]{1,0:T(8,128)}, u32[]{:S(2)}) copy-start(f32[256,256]{1,0:T(8,128)} %inv_one_ref.1) | copy-start | bytes 786436
  124.8 48.5 %copy-start.9 = (f32[256,256]{1,0:T(8,128)S(1)}, f32[256,256]{1,0:T(8,128)}, u32[]{:S(2)}) copy-start(f32[256,256]{1,0:T(8,128)} %inv_two_ref.1) | copy-start | bytes 786436

commit v3 on v1

v3 whole, which is shorter than its diff:
```python
import functools

import jax
import jax.numpy as jnp
from jax import lax
from jax.experimental import pallas as pl
from jax.experimental.pallas import tpu as pltpu
from jax.sharding import PartitionSpec as P

BF16 = jnp.bfloat16
F32 = jnp.float32
VMEM = pl.BlockSpec(memory_space=pltpu.VMEM)
SMEM = pl.BlockSpec(memory_space=pltpu.SMEM)
HBM = pl.BlockSpec(memory_space=pltpu.HBM)
ANY = pl.BlockSpec(memory_space=pl.ANY)
CHIPS = 8
CORES = 2
ROWS = 16
LANES = 128


def params(mebibytes=16):
    return pltpu.CompilerParams(vmem_limit_bytes=mebibytes * 1024 * 1024)


BLOCKS = 8


def places(block_ids, pattern_one, pattern_two):
    found = []
    for pattern in (pattern_one, pattern_two):
        hits = block_ids[:, None] == pattern[None, :]
        at = jnp.arange(pattern.shape[0], dtype=jnp.int32)[None, :] + 1
        found.append(jnp.sum(jnp.where(hits, at, 0), axis=1) - 1)
    return jnp.concatenate(found)


LIST = 4 * BLOCKS + 1


def compact(found_ref, list_ref):
    for i in range(2 * BLOCKS):
        list_ref[i] = -1
    count = jnp.int32(0)
    for code in range(2 * BLOCKS):
        present = found_ref[code] >= 0
        list_ref[jnp.where(present, count, LIST - 1)] = code
        list_ref[2 * BLOCKS + code] = jnp.where(present, count, -1)
        count = count + present.astype(jnp.int32)


SIDE = 4
FEW = 12


def source(code, s, each):
    one = lax.div(s, each[0]) * sum(each) + lax.rem(s, each[0])
    two = lax.div(s, each[1]) * sum(each) + each[0] + lax.rem(s, each[1])
    return jnp.where(code < BLOCKS, one, two)


def pick_kernel(each, found_ref, gathered_ref, own_ref, low_ref, high_ref, list_ref):
    compact(found_ref, list_ref)
    half = low_ref.shape[0]
    for slot in range(own_ref.shape[0]):
        code = list_ref[slot]
        s = jnp.maximum(found_ref[jnp.maximum(code, 0)], 0)
        block = gathered_ref[source(code, s, each)]
        block = jnp.where(code >= 0, block, jnp.zeros_like(block))
        own_ref[slot] = block
        if slot < half:
            low_ref[slot] = block
        else:
            high_ref[slot - half] = block


def pick(slots, each, found, gathered):
    tail = gathered.shape[1:]
    half = jax.ShapeDtypeStruct((slots // 2,) + tail, BF16)
    return pl.pallas_call(
        functools.partial(pick_kernel, each),
        out_shape=(
            jax.ShapeDtypeStruct((slots,) + tail, BF16), half, half,
            jax.ShapeDtypeStruct((LIST,), jnp.int32),
        ),
        in_specs=[SMEM, VMEM],
        out_specs=(VMEM, VMEM, VMEM, SMEM),
        compiler_params=params(),
        name="pick",
    )(found, gathered)


def product_kernel(rows_ref, cols_ref, here_ref, region_ref, *refs):
    low_refs, high_refs = refs[:SIDE], refs[SIDE:2 * SIDE]
    keep_ref, send_ref, list_ref, region, wide, turned, narrow, panel, total, region_sem, sem = refs[2 * SIDE:]
    width = region.shape[1]
    slots = narrow.shape[0]
    half = slots // 2
    core, depth, x, y = here_ref[0], here_ref[1], here_ref[2], here_ref[3]
    compact(rows_ref, list_ref)

    def region_copy(at):
        return pltpu.make_async_copy(region_ref.at[at], region.at[at], region_sem.at[at])

    def slot_of(code):
        slot = list_ref[2 * BLOCKS + code]
        return slot, (slot >= 0) & (slot < slots)

    copies = []
    for i, (low, high) in enumerate(zip(low_refs, high_refs)):
        for j in range(SIDE):
            for side, ref in enumerate((low, high)):
                dx, dy = (j, i) if side == 0 else (i, j)
                row = lax.rem(y + SIDE - dy, SIDE) * SIDE + lax.rem(x + SIDE - dx, SIDE)
                place = pl.ds(pl.multiple_of(row * ROWS, ROWS), ROWS)
                copies.append(pltpu.make_async_copy(
                    ref.at[j], narrow.at[pl.ds(side * half, half), place, :], sem.at[len(copies)]
                ))
    for copy in copies:
        copy.start()
    for at in range(BLOCKS):
        pl.when(slot_of(at)[1])(region_copy(at).start)
    panel[...] = jnp.zeros(panel.shape, BF16)
    for slot in range(slots):
        @pl.when(list_ref[slot] < 0)
        def _():
            keep_ref[:, slot] = jnp.zeros((CHIPS, ROWS, width), F32)
            send_ref[:, slot] = jnp.zeros((CHIPS, ROWS, width), BF16)

    for copy in copies:
        copy.wait()
    for slot in range(slots):
        code = cols_ref[slot]

        @pl.when(code >= 0)
        def _():
            panel[pl.ds(pl.multiple_of(code * width, width), width), :] = narrow[slot]

    deep = BLOCKS * width

    def multiply(group, slot):
        sums = jnp.dot(turned[...], panel[group * deep:(group + 1) * deep], preferred_element_type=F32)
        total[...] = sums.reshape(total.shape)
        for d in range(CHIPS):
            z = lax.rem(depth + d, CHIPS)
            keep_ref[d, slot] = total[z, core]
            send_ref[d, slot] = total[z, 1 - core].astype(BF16)

    def step(at, carry):
        first, present = slot_of(at)
        second, both = slot_of(BLOCKS + at)

        @pl.when(present)
        def _():
            region_copy(at).wait()
            for h in range(width // LANES):
                part = region[at, :, :, pl.ds(h * LANES, LANES)]
                wide[h] = part.reshape(width * BLOCKS, LANES).astype(F32)
            for c in range(BLOCKS):
                for h in range(width // LANES):
                    turned[:, pl.ds(c * width + h * LANES, LANES)] = wide[
                        h, pl.ds(c, width, stride=BLOCKS), :
                    ].astype(BF16)
            multiply(0, first)
            pl.when(both)(lambda: multiply(1, second))

        return carry

    lax.fori_loop(0, BLOCKS, step, 0)


def product(slots, rows, cols, here, region, lows, highs):
    blocks, width = region.shape[:2]
    shape = (CHIPS, slots, ROWS, width)
    return pl.pallas_call(
        product_kernel,
        out_shape=(
            jax.ShapeDtypeStruct(shape, F32), jax.ShapeDtypeStruct(shape, BF16),
            jax.ShapeDtypeStruct((LIST,), jnp.int32),
        ),
        in_specs=[SMEM, SMEM, SMEM, HBM] + [ANY] * (2 * SIDE),
        out_specs=(VMEM, VMEM, SMEM),
        scratch_shapes=[
            pltpu.VMEM((blocks, width, blocks, width), BF16),
            pltpu.VMEM((width // LANES, width * blocks, LANES), F32),
            pltpu.VMEM((width, blocks * width), BF16),
            pltpu.VMEM((slots, width, width), BF16),
            pltpu.VMEM((2 * blocks * width, width), BF16),
            pltpu.VMEM((CHIPS, CORES, ROWS, width), F32),
            pltpu.SemaphoreType.DMA((blocks,)),
            pltpu.SemaphoreType.DMA((2 * SIDE * SIDE,)),
        ],
        compiler_params=params(48),
        name="product",
    )(rows, cols, here, region, *lows, *highs)


def pair_kernel(keep_ref, got_ref, *out_refs):
    for d, out_ref in enumerate(out_refs):
        out_ref[...] = (keep_ref[d] + got_ref[d].astype(F32)).astype(BF16)


def pair(keep, got):
    share = jax.ShapeDtypeStruct(keep.shape[1:], BF16)
    return pl.pallas_call(
        pair_kernel,
        out_shape=(share,) * CHIPS,
        in_specs=[VMEM, VMEM],
        out_specs=(VMEM,) * CHIPS,
        compiler_params=params(),
        name="pair",
    )(keep, got)


def across(a, b):
    return lax.dot_general(a, b, (((0,), (0,)), ((), ())), preferred_element_type=F32)


def columns_kernel(list_ref, found_ref, rows_ref, link_ref, *refs):
    parts = refs[:CHIPS]
    one_ref, two_ref, sums_ref, sums, rows = refs[CHIPS:]
    blocks, share, width = one_ref.shape
    deep = blocks * share
    rows[...] = jnp.zeros(rows.shape, BF16)
    sums[...] = jnp.zeros(sums.shape, F32)
    for slot in range(parts[0].shape[0]):
        code = list_ref[slot]

        @pl.when(code >= 0)
        def _():
            total = parts[0][slot].astype(F32)
            for part in parts[1:]:
                total = total + part[slot].astype(F32)
            place = pl.ds(pl.multiple_of(code * share, share), share)
            sums[place] = -total
            rows[place] = rows_ref[slot]

    one = sums[:deep].astype(BF16)
    one_ref[...] = one.reshape(one_ref.shape)
    linked = jnp.dot(one, link_ref[...], preferred_element_type=F32)
    second = sums[deep:] - linked
    for at in range(blocks):
        part = slice(at * share, (at + 1) * share)
        kept = jnp.where(found_ref[BLOCKS + at] >= 0, second[part], 0.0)
        two_ref[at] = kept.astype(BF16)
    two = two_ref[...].reshape(deep, width)
    kind = sums_ref.dtype
    sums_ref[:width] = across(rows[:deep], one).astype(kind)
    sums_ref[width:2 * width] = across(one, rows[deep:]).astype(kind)
    sums_ref[2 * width:] = across(rows[deep:], two).astype(kind)


def columns(row_list, found, parts, rows, link):
    share, width = parts[0].shape[1:]
    column = jax.ShapeDtypeStruct((BLOCKS, share, width), BF16)
    return pl.pallas_call(
        columns_kernel,
        out_shape=(column, column, jax.ShapeDtypeStruct((3 * width, width), BF16)),
        in_specs=[SMEM, SMEM, VMEM, VMEM] + [VMEM] * CHIPS,
        out_specs=(VMEM, VMEM, VMEM),
        scratch_shapes=[
            pltpu.VMEM((2 * BLOCKS * share, width), F32),
            pltpu.VMEM((2 * BLOCKS * share, width), BF16),
        ],
        compiler_params=params(),
        name="columns",
    )(row_list, found, rows, link, *parts)


def times_link(value, link, dims):
    total = None
    for _ in range(3):
        part = value.astype(BF16)
        value = value - part.astype(F32)
        term = lax.dot_general(part, link, (dims, ((), ())), preferred_element_type=F32)
        total = term if total is None else total + term
    return total


def diagonals_kernel(sums_ref, link_ref, inv_one_ref, inv_two_ref, one_ref, cross_ref, two_ref):
    width = link_ref.shape[0]
    link = link_ref[...]
    one = inv_one_ref[...] - sums_ref[:width].astype(F32)
    one_ref[...] = one
    cross = -times_link(one, link, ((1,), (0,))) - sums_ref[width:2 * width].astype(F32)
    cross_ref[...] = cross
    two = inv_two_ref[...] - sums_ref[2 * width:].astype(F32)
    two_ref[...] = two - times_link(cross, link, ((0,), (0,))).T


def diagonals(sums, link, inv_one, inv_two):
    square = jax.ShapeDtypeStruct(inv_one.shape, F32)
    return pl.pallas_call(
        diagonals_kernel,
        out_shape=(square, square, square),
        in_specs=[VMEM] * 4,
        out_specs=(VMEM,) * 3,
        compiler_params=params(),
        name="diagonals",
    )(sums, link, inv_one, inv_two)


def swap_axes(value, axes, groups=None):
    return lax.all_to_all(value, axes, 0, 0, axis_index_groups=groups, tiled=True)


def sum_everywhere(sums, rows_grid, cols_grid):
    both = ("prow", "pcol")
    planes = [
        [p * cols_grid + z * CORES + c for p in range(rows_grid) for c in range(CORES)]
        for z in range(CHIPS)
    ]
    lines = [[z * CORES + c for z in range(CHIPS)] for c in range(CORES)]
    ways = rows_grid * CORES
    height, width = sums.shape
    share = height // ways
    pieces = swap_axes(sums.reshape(ways, share, width), both, planes)
    piece = jnp.sum(pieces.astype(F32), axis=0)
    pieces = swap_axes(jnp.broadcast_to(piece, (CHIPS, share, width)), "pcol", lines)
    piece = jnp.sum(pieces, axis=0).astype(BF16)
    pieces = swap_axes(jnp.broadcast_to(piece, (ways, share, width)), both, planes)
    return pieces.reshape(height, width)


def along_z(d):
    lines = [(z, c) for z in range(CHIPS) for c in range(CORES)]
    return [(z * CORES + c, (z + d) % CHIPS * CORES + c) for z, c in lines]


def along_plane(dy, dx):
    places = [(y, x) for y in range(SIDE) for x in range(SIDE)]
    return [(y * SIDE + x, (y + dy) % SIDE * SIDE + (x + dx) % SIDE) for y, x in places]


def spread_plane(low, high):
    hops = (1, SIDE - 1) + tuple(range(2, SIDE - 1))

    def around(value, turn):
        moved = {0: value}
        for d in hops:
            moved[d] = lax.ppermute(value, "prow", turn(d))
        return [moved[d] for d in range(SIDE)]

    def by_x(d):
        return along_plane(0, d)

    def by_y(d):
        return along_plane(d, 0)

    lows, highs = around(low, by_x), around(high, by_y)
    lows, highs = jnp.stack(lows), jnp.stack(highs)
    return around(lows, by_y), around(highs, by_x)


def shards(
    inverse_region, panel_one, panel_two, link_block, inv_diag_one, inv_diag_two,
    pattern_one, pattern_two,
):
    rows_grid = lax.axis_size("prow")
    cols_grid = lax.axis_size("pcol")
    p = lax.axis_index("prow")
    q = lax.axis_index("pcol")
    width = inverse_region.shape[1]
    here = jnp.stack([lax.rem(q, CORES), lax.div(q, CORES), lax.rem(p, SIDE), lax.div(p, SIDE)])
    steps = jnp.arange(BLOCKS, dtype=jnp.int32)
    panels = [panel.reshape(-1, width, width) for panel in (panel_one, panel_two)]
    each = tuple(panel.shape[0] for panel in panels)
    found_cols = places(steps * cols_grid + q, pattern_one, pattern_two)
    found_rows = places(steps * rows_grid + p, pattern_one, pattern_two)
    mine = jnp.concatenate(
        [lax.dynamic_slice_in_dim(panel, p * ROWS, ROWS, 1) for panel in panels], axis=0
    )
    gathered = lax.all_gather(mine, "pcol", axis=0, tiled=True)

    def invert(slots, gathered, found_cols, found_rows, region, link, inv_one, inv_two):
        own, low, high, col_list = pick(slots, each, found_cols, gathered)
        transpose = [
            (a * cols_grid + b, b * cols_grid + a) for a in range(rows_grid) for b in range(cols_grid)
        ]
        rows = lax.ppermute(own, ("prow", "pcol"), transpose)
        lows, highs = spread_plane(low, high)
        keep, give, row_list = product(slots, found_rows, col_list, here, region, lows, highs)
        got = lax.ppermute(give, "pcol", [(i, i ^ 1) for i in range(cols_grid)])
        shares = pair(keep, got)
        parts = [shares[0]]
        for d in (1, 7, 2, 6, 3, 5, 4):
            parts.append(lax.ppermute(shares[d], "pcol", along_z(d)))
        column_one, column_two, sums = columns(row_list, found_rows, parts, rows, link)
        sums = sum_everywhere(sums, rows_grid, cols_grid)
        diagonal_one, cross_two, diagonal_two = diagonals(sums, link, inv_one, inv_two)
        return (column_one, diagonal_one, column_two, cross_two, diagonal_two)

    classes = jnp.arange(rows_grid, dtype=jnp.int32)[:, None]
    members = sum(
        jnp.sum((lax.rem(pattern, rows_grid)[None, :] == classes).astype(jnp.int32), axis=1)
        for pattern in (pattern_one, pattern_two)
    )
    fits = jnp.all(members <= FEW)
    given = (gathered, found_cols, found_rows, inverse_region, link_block, inv_diag_one, inv_diag_two)
    return lax.cond(
        fits,
        lambda outs, *given: outs,
        lambda outs, *given: invert(2 * BLOCKS, *given),
        invert(FEW, *given), *given,
    )


def solution(mesh):
    return jax.shard_map(
        shards,
        mesh=mesh,
        in_specs=(P(None, "prow", None, "pcol"), P("pcol", None), P("pcol", None), P(), P(), P(), P(), P()),
        out_specs=(P(None, ("prow", "pcol"), None), P(), P(None, ("prow", "pcol"), None), P(), P()),
        check_vma=False,
    )
```

time: 171 us -> 146 us (0.85)
  blocking collectives: 76.4 us -> 41.3 us
  starting transfers between devices: 13.9 us -> 47.7 us
  waiting for transfers between devices: 62.2 us -> 39.5 us
    all_to_all x2, waiting for transfers between devices: 55.2 us -> 18.1 us  [swap_axes(): lax.all_to_all(value, axes, 0, 0, axis_index_groups=groups, tiled=True)]
    all_to_all x3 -> x1, blocking collectives: 52.9 us -> 17.8 us  [swap_axes(): lax.all_to_all(value, axes, 0, 0, axis_index_groups=groups, tiled=True)]
    ppermute x2 -> x21, starting transfers between devices: 3.43 us -> 37.2 us  [the longest x7 16.7 us: invert(): parts.append(lax.ppermute(shares[d], 'pcol', along_z(d)))]
    ppermute x2 -> x21, waiting for transfers between devices: 6.94 us -> 21.4 us  [the longest x7 10.9 us: invert(): parts.append(lax.ppermute(shares[d], 'pcol', along_z(d)))]
    pallas_call x3 -> x4, Pallas kernels: 10.4 us -> 9.12 us  [the longest x1 6.19 us: product(): pl.pallas_call(product_kernel, out_shape=(jax.ShapeDtypeStruct(shape, F32...]
  transfers between devices with their start and end apart: 4 -> 23, of which waited for: 4 -> 11; matrix products, arithmetic and copies ran while one was open for 0% -> 1% of each run, Pallas kernels for 0% -> 0%
where the time goes in v3:
time: 146 us
  starting transfers between devices  47.7 us (33%)
  blocking collectives  41.3 us (28%)
  waiting for transfers between devices  39.5 us (27%)
  Pallas kernels  10.6 us (7%)
  other arithmetic  3.08 us (2%)
  local copies, waits for them, and re-layouts  2.23 us (2%)
  between operations  1.47 us (1%)
    all_gather x1, blocking collectives, shards(): gathered = lax.all_gather(mine, 'pcol', axis=0, tiled=True)  23.5 us
    all_to_all x2, waiting for transfers between devices, swap_axes(): lax.all_to_all(value, axes, 0, 0, axis_index_groups=groups, tiled=True)  18.1 us
    all_to_all x1, blocking collectives, swap_axes(): lax.all_to_all(value, axes, 0, 0, axis_index_groups=groups, tiled=True)  17.8 us
    ppermute x7, starting transfers between devices, invert(): parts.append(lax.ppermute(shares[d], 'pcol', along_z(d)))  16.7 us
    ppermute x12, starting transfers between devices, around(): moved[d] = lax.ppermute(value, 'prow', turn(d))  13.4 us
    ppermute x7, waiting for transfers between devices, invert(): parts.append(lax.ppermute(shares[d], 'pcol', along_z(d)))  10.9 us
    all_to_all x2, starting transfers between devices, swap_axes(): lax.all_to_all(value, axes, 0, 0, axis_index_groups=groups, tiled=True)  10.5 us
    ppermute x12, waiting for transfers between devices, around(): moved[d] = lax.ppermute(value, 'prow', turn(d))  10.4 us
  transfers between devices with their start and end apart: 23, of which 11 were waited for; matrix products, arithmetic and copies ran while one was open for 1% of the time, Pallas kernels for 0%

profile of v3, /device:TPU:1, one launch (start us, length us, event | category | flops | bytes accessed | tf_op | source)
XLA Modules:
  0.0 145.9 jit_solution(13551494986529097474)
XLA Ops:
  3.2 23.5 %all_gather.3.gathered_ref = bf16[96,16,256]{2,1,0:T(8,128)(2,1)S(1)} all-gather(bf16[6,16,256]{2,1,0:T(8,128)(2,1)S(1)} %pad_maximum_fusion.4), channel_id=1, replica_groups=mesh['prow'=16,'pcol'=16] {'pcol'}, dimensions={0}, use_global_device_ids=true | all-gather | bytes 835584 | tf_op jit(solution)/shard_map/all_gather | solution.py:373
  28.1 2.6 %collective-permute-start.23 = (bf16[6,16,256]{2,1,0:T(8,128)(2,1)S(1)}, bf16[6,16,256]{2,1,0:T(8,128)(2,1)S(1)}, u32[]{:S(2)}, u32[]{:S(2)}) collective-permute-start(bf16[6,16,256]{2,1,0:T(8,128)(2,1)S(1)} %get-tuple-element.82), channel_id=1, source_target_pairs={{0,48},{16,0},{32,16},{48,32},{64,112},{80,64},{96,80},{112,96},{1... | collective-permute-start | bytes 147464 | tf_op jit(solution)/shard_map/ppermute | solution.py:341
  31.2 2.7 %collective-permute-start.29 = (bf16[6,16,256]{2,1,0:T(8,128)(2,1)S(1)}, bf16[6,16,256]{2,1,0:T(8,128)(2,1)S(1)}, u32[]{:S(2)}, u32[]{:S(2)}) collective-permute-start(bf16[6,16,256]{2,1,0:T(8,128)(2,1)S(1)} %get-tuple-element.83), channel_id=1, source_target_pairs={{0,192},{16,208},{32,224},{48,240},{64,0},{80,16},{96,32},{112,48}... | collective-permute-start | bytes 147464 | tf_op jit(solution)/shard_map/ppermute | solution.py:341
  35.7 2.7 %collective-permute-done.28 = bf16[6,16,256]{2,1,0:T(8,128)(2,1)S(1)} collective-permute-done((bf16[6,16,256]{2,1,0:T(8,128)(2,1)S(1)}, bf16[6,16,256]{2,1,0:T(8,128)(2,1)S(1)}, u32[]{:S(2)}, u32[]{:S(2)}) %collective-permute-start.28) | collective-permute-done | bytes 49184 | tf_op jit(solution)/shard_map/ppermute | solution.py:341
  39.8 1.7 %collective-permute-start.31 = (bf16[4,6,16,256]{3,2,1,0:T(8,128)(2,1)S(1)}, bf16[4,6,16,256]{3,2,1,0:T(8,128)(2,1)S(1)}, u32[]{:S(2)}, u32[]{:S(2)}) collective-permute-start(bf16[4,6,16,256]{3,2,1,0:T(8,128)(2,1)S(1)} %pad_maximum_fusion.3.refs_4_), channel_id=1, source_target_pairs={{0,32},{16,48},{32,0},{48,16},{64,96},{80,112},{96,64},{112,80},{1... | collective-permute-start | bytes 589832 | tf_op jit(solution)/shard_map/ppermute | solution.py:341
  45.9 4.9 %collective-permute-done.30.refs_5_ = bf16[4,6,16,256]{3,2,1,0:T(8,128)(2,1)S(1)} collective-permute-done((bf16[4,6,16,256]{3,2,1,0:T(8,128)(2,1)S(1)}, bf16[4,6,16,256]{3,2,1,0:T(8,128)(2,1)S(1)}, u32[]{:S(2)}, u32[]{:S(2)}) %collective-permute-start.30) | collective-permute-done | bytes 196640 | tf_op jit(solution)/shard_map/ppermute | solution.py:341
  52.1 6.2 %product.3 = (f32[8,12,16,256]{3,2,1,0:T(8,128)S(1)}, bf16[8,12,16,256]{3,2,1,0:T(8,128)(2,1)S(1)}, s32[33]{0:T(128)S(1)}) custom-call(s32[16]{0:T(128)S(1)} %pad_add_fusion.1.rows_ref.found_ref, s32[33]{0:T(128)S(1)} %get-tuple-element.81.cols_ref, s32[4]{0:T(128)S(1)} %pad_add_fusion.2.here_ref, bf16[8,256,8,256]{3,2,1,0:T(8,128)(2,1)} %region_ref.1, ...), custom_call_target="tpu_custom_call" | custom-call | tf_op jit(solution)/shard_map/product/pallas_call | solution.py:175
  58.3 4.0 %collective-permute-start.34 = (bf16[8,12,16,256]{3,2,1,0:T(8,128)(2,1)S(1)}, bf16[8,12,16,256]{3,2,1,0:T(8,128)(2,1)S(1)}, u32[]{:S(2)}, u32[]{:S(2)}) collective-permute-start(bf16[8,12,16,256]{3,2,1,0:T(8,128)(2,1)S(1)} %get-tuple-element.87), channel_id=1, source_target_pairs={{0,1},{1,0},{2,3},{3,2},{4,5},{5,4},{6,7},{7,6},{8,9},{9,8},{10,11... | collective-permute-start | bytes 2359304 | tf_op jit(solution)/shard_map/ppermute | solution.py:383
  62.3 3.2 %collective-permute-start.33 = (bf16[12,16,256]{2,1,0:T(8,128)(2,1)S(1)}, bf16[12,16,256]{2,1,0:T(8,128)(2,1)S(1)}, u32[]{:S(2)}, u32[]{:S(2)}) collective-permute-start(bf16[12,16,256]{2,1,0:T(8,128)(2,1)S(1)} %get-tuple-element.85), channel_id=1, source_target_pairs={{0,0},{1,16},{2,32},{3,48},{4,64},{5,80},{6,96},{7,112},{8,128},{9... | collective-permute-start | bytes 294920 | tf_op jit(solution)/shard_map/ppermute | solution.py:380
  65.7 2.5 %collective-permute-start.35 = (bf16[12,16,256]{2,1,0:T(8,128)(2,1)S(1)}, bf16[12,16,256]{2,1,0:T(8,128)(2,1)S(1)}, u32[]{:S(2)}, u32[]{:S(2)}) collective-permute-start(bf16[12,16,256]{2,1,0:T(8,128)(2,1)S(1)} %get-tuple-element.89), channel_id=1, source_target_pairs={{0,2},{1,3},{2,4},{3,5},{4,6},{5,7},{6,8},{7,9},{8,10},{9,11},{10,... | collective-permute-start | bytes 294920 | tf_op jit(solution)/shard_map/ppermute | solution.py:387
  68.2 1.6 %collective-permute-start.36 = (bf16[12,16,256]{2,1,0:T(8,128)(2,1)S(1)}, bf16[12,16,256]{2,1,0:T(8,128)(2,1)S(1)}, u32[]{:S(2)}, u32[]{:S(2)}) collective-permute-start(bf16[12,16,256]{2,1,0:T(8,128)(2,1)S(1)} %get-tuple-element.90), channel_id=1, source_target_pairs={{0,14},{1,15},{2,0},{3,1},{4,2},{5,3},{6,4},{7,5},{8,6},{9,7},{10,... | collective-permute-start | bytes 294920 | tf_op jit(solution)/shard_map/ppermute | solution.py:387
  69.8 2.9 %collective-permute-start.37 = (bf16[12,16,256]{2,1,0:T(8,128)(2,1)S(1)}, bf16[12,16,256]{2,1,0:T(8,128)(2,1)S(1)}, u32[]{:S(2)}, u32[]{:S(2)}) collective-permute-start(bf16[12,16,256]{2,1,0:T(8,128)(2,1)S(1)} %get-tuple-element.91), channel_id=1, source_target_pairs={{0,4},{1,5},{2,6},{3,7},{4,8},{5,9},{6,10},{7,11},{8,12},{9,13},{1... | collective-permute-start | bytes 294920 | tf_op jit(solution)/shard_map/ppermute | solution.py:387
  73.4 4.2 %collective-permute-start.39 = (bf16[12,16,256]{2,1,0:T(8,128)(2,1)S(1)}, bf16[12,16,256]{2,1,0:T(8,128)(2,1)S(1)}, u32[]{:S(2)}, u32[]{:S(2)}) collective-permute-start(bf16[12,16,256]{2,1,0:T(8,128)(2,1)S(1)} %get-tuple-element.93), channel_id=1, source_target_pairs={{0,6},{1,7},{2,8},{3,9},{4,10},{5,11},{6,12},{7,13},{8,14},{9,15},... | collective-permute-start | bytes 294920 | tf_op jit(solution)/shard_map/ppermute | solution.py:387
  77.6 3.3 %collective-permute-done.35.refs_1_ = bf16[12,16,256]{2,1,0:T(8,128)(2,1)S(1)} collective-permute-done((bf16[12,16,256]{2,1,0:T(8,128)(2,1)S(1)}, bf16[12,16,256]{2,1,0:T(8,128)(2,1)S(1)}, u32[]{:S(2)}, u32[]{:S(2)}) %collective-permute-start.35) | collective-permute-done | bytes 98336 | tf_op jit(solution)/shard_map/ppermute | solution.py:387
  81.0 4.7 %collective-permute-start.41 = (bf16[12,16,256]{2,1,0:T(8,128)(2,1)S(1)}, bf16[12,16,256]{2,1,0:T(8,128)(2,1)S(1)}, u32[]{:S(2)}, u32[]{:S(2)}) collective-permute-start(bf16[12,16,256]{2,1,0:T(8,128)(2,1)S(1)} %get-tuple-element.95), channel_id=1, source_target_pairs={{0,8},{1,9},{2,10},{3,11},{4,12},{5,13},{6,14},{7,15},{8,0},{9,1},... | collective-permute-start | bytes 294920 | tf_op jit(solution)/shard_map/ppermute | solution.py:387
  85.7 2.9 %collective-permute-done.39.refs_5_ = bf16[12,16,256]{2,1,0:T(8,128)(2,1)S(1)} collective-permute-done((bf16[12,16,256]{2,1,0:T(8,128)(2,1)S(1)}, bf16[12,16,256]{2,1,0:T(8,128)(2,1)S(1)}, u32[]{:S(2)}, u32[]{:S(2)}) %collective-permute-start.39) | collective-permute-done | bytes 98336 | tf_op jit(solution)/shard_map/ppermute | solution.py:387
  88.7 4.6 %collective-permute-done.41.refs_7_ = bf16[12,16,256]{2,1,0:T(8,128)(2,1)S(1)} collective-permute-done((bf16[12,16,256]{2,1,0:T(8,128)(2,1)S(1)}, bf16[12,16,256]{2,1,0:T(8,128)(2,1)S(1)}, u32[]{:S(2)}, u32[]{:S(2)}) %collective-permute-start.41) | collective-permute-done | bytes 98336 | tf_op jit(solution)/shard_map/ppermute | solution.py:387
  93.3 1.5 %columns.3 = (bf16[8,16,256]{2,1,0:T(8,128)(2,1)}, bf16[8,16,256]{2,1,0:T(8,128)(2,1)}, bf16[768,256]{1,0:T(8,128)(2,1)S(1)}) custom-call(s32[33]{0:T(128)S(1)} %get-tuple-element.84.list_ref, s32[16]{0:T(128)S(1)} %pad_add_fusion.1.rows_ref.found_ref, bf16[12,16,256]{2,1,0:T(8,128)(2,1)S(1)} %collective-permute-done.33.rows_ref, ...), custom_call_target="tpu_custom_call" | custom-call | tf_op jit(solution)/shard_map/columns/pallas_call | solution.py:256
  94.8 17.8 %all_to_all.30 = bf16[32,24,256]{2,1,0:T(8,128)(2,1)S(1)} all-to-all(bf16[32,24,256]{2,1,0:T(8,128)(2,1)S(1)} %bitcast.30), channel_id=1, replica_groups={{0,1,16,17,32,33,48,49,64,65,80,81,96,97,112,113,128,129,144,145,160,16..., dimensions={0} | all-to-all | bytes 786432 | tf_op jit(solution)/shard_map/all_to_all | solution.py:304
  113.4 4.9 %all-to-all-start.4 = ((f32[8,24,256]{2,1,0:T(8,128)}), f32[8,24,256]{2,1,0:T(8,128)S(1)}, u32[]{:S(2)}, u32[]{:S(2)}) async-start(f32[8,24,256]{2,1,0:T(8,128)} %broadcast_in_dim.67), calls=%async_computation.4 | async-start | bytes 393216 | tf_op jit(solution)/shard_map/all_to_all | solution.py:304
  118.4 9.4 %all-to-all-done.4 = f32[8,24,256]{2,1,0:T(8,128)S(1)} async-done(((f32[8,24,256]{2,1,0:T(8,128)}), f32[8,24,256]{2,1,0:T(8,128)S(1)}, u32[]{:S(2)}, u32[]{:S(2)}) %all-to-all-start.4) | async-done | bytes 196640 | tf_op jit(solution)/shard_map/all_to_all | solution.py:304
  128.6 5.6 %all-to-all-start.5 = ((bf16[32,24,256]{2,1,0:T(8,128)(2,1)}), bf16[32,24,256]{2,1,0:T(8,128)(2,1)S(1)}, u32[]{:S(2)}, u32[]{:S(2)}) async-start(bf16[32,24,256]{2,1,0:T(8,128)(2,1)} %broadcast_in_dim.68), calls=%async_computation.5 | async-start | bytes 786432 | tf_op jit(solution)/shard_map/all_to_all | solution.py:304
  135.7 8.7 %all-to-all-done.5 = bf16[32,24,256]{2,1,0:T(8,128)(2,1)S(1)} async-done(((bf16[32,24,256]{2,1,0:T(8,128)(2,1)}), bf16[32,24,256]{2,1,0:T(8,128)(2,1)S(1)}, u32[]{:S(2)}, u32[]{:S(2)}) %all-to-all-start.5) | async-done | bytes 393248 | tf_op jit(solution)/shard_map/all_to_all | solution.py:304
  144.4 1.5 %diagonals.3 = (f32[256,256]{1,0:T(8,128)}, f32[256,256]{1,0:T(8,128)}, f32[256,256]{1,0:T(8,128)}) custom-call(bf16[768,256]{1,0:T(8,128)(2,1)S(1)} %bitcast.27, bf16[256,256]{1,0:T(8,128)(2,1)S(1)} %copy-done.1, f32[256,256]{1,0:T(8,128)S(1)} %copy-done.2, f32[256,256]{1,0:T(8,128)S(1)} %copy-done.3), custom_call_target="tpu_custom_call" | custom-call | tf_op jit(solution)/shard_map/diagonals/pallas_call | solution.py:293
  (68 shorter events, 16.7 us)
Async XLA Ops:
  28.1 13.5 %collective-permute-start.23 = (bf16[6,16,256]{2,1,0:T(8,128)(2,1)S(1)}, bf16[6,16,256]{2,1,0:T(8,128)(2,1)S(1)}, u32[]{:S(2)}, u32[]{:S(2)}) collective-permute-start(bf16[6,16,256]{2,1,0:T(8,128)(2,1)S(1)} %get-tuple-element.82), channel_id=1, source_target_pairs={{0,48},{16,0},{32,16},{48,32},{64,112},{80,64},{96,80},{112,96},{1... | collective-permute-start | bytes 147464 | tf_op jit(solution)/shard_map/ppermute | solution.py:341
  30.6 11.7 %collective-permute-start.22 = (bf16[6,16,256]{2,1,0:T(8,128)(2,1)S(1)}, bf16[6,16,256]{2,1,0:T(8,128)(2,1)S(1)}, u32[]{:S(2)}, u32[]{:S(2)}) collective-permute-start(bf16[6,16,256]{2,1,0:T(8,128)(2,1)S(1)} %get-tuple-element.82), channel_id=1, source_target_pairs={{0,32},{16,48},{32,0},{48,16},{64,96},{80,112},{96,64},{112,80},{1... | collective-permute-start | bytes 147464 | tf_op jit(solution)/shard_map/ppermute | solution.py:341
  31.2 3.9 %collective-permute-start.29 = (bf16[6,16,256]{2,1,0:T(8,128)(2,1)S(1)}, bf16[6,16,256]{2,1,0:T(8,128)(2,1)S(1)}, u32[]{:S(2)}, u32[]{:S(2)}) collective-permute-start(bf16[6,16,256]{2,1,0:T(8,128)(2,1)S(1)} %get-tuple-element.83), channel_id=1, source_target_pairs={{0,192},{16,208},{32,224},{48,240},{64,0},{80,16},{96,32},{112,48}... | collective-permute-start | bytes 147464 | tf_op jit(solution)/shard_map/ppermute | solution.py:341
  33.9 4.5 %collective-permute-start.28 = (bf16[6,16,256]{2,1,0:T(8,128)(2,1)S(1)}, bf16[6,16,256]{2,1,0:T(8,128)(2,1)S(1)}, u32[]{:S(2)}, u32[]{:S(2)}) collective-permute-start(bf16[6,16,256]{2,1,0:T(8,128)(2,1)S(1)} %get-tuple-element.83), channel_id=1, source_target_pairs={{0,128},{16,144},{32,160},{48,176},{64,192},{80,208},{96,224},{112... | collective-permute-start | bytes 147464 | tf_op jit(solution)/shard_map/ppermute | solution.py:341
  34.2 4.6 %collective-permute-start.27 = (bf16[6,16,256]{2,1,0:T(8,128)(2,1)S(1)}, bf16[6,16,256]{2,1,0:T(8,128)(2,1)S(1)}, u32[]{:S(2)}, u32[]{:S(2)}) collective-permute-start(bf16[6,16,256]{2,1,0:T(8,128)(2,1)S(1)} %get-tuple-element.83), channel_id=1, source_target_pairs={{0,64},{16,80},{32,96},{48,112},{64,128},{80,144},{96,160},{112,17... | collective-permute-start | bytes 147464 | tf_op jit(solution)/shard_map/ppermute | solution.py:341
  35.1 7.2 %collective-permute-start.21 = (bf16[6,16,256]{2,1,0:T(8,128)(2,1)S(1)}, bf16[6,16,256]{2,1,0:T(8,128)(2,1)S(1)}, u32[]{:S(2)}, u32[]{:S(2)}) collective-permute-start(bf16[6,16,256]{2,1,0:T(8,128)(2,1)S(1)} %get-tuple-element.82), channel_id=1, source_target_pairs={{0,16},{16,32},{32,48},{48,0},{64,80},{80,96},{96,112},{112,64},{1... | collective-permute-start | bytes 147464 | tf_op jit(solution)/shard_map/ppermute | solution.py:341
  38.9 5.2 %collective-permute-start.32 = (bf16[4,6,16,256]{3,2,1,0:T(8,128)(2,1)S(1)}, bf16[4,6,16,256]{3,2,1,0:T(8,128)(2,1)S(1)}, u32[]{:S(2)}, u32[]{:S(2)}) collective-permute-start(bf16[4,6,16,256]{3,2,1,0:T(8,128)(2,1)S(1)} %pad_maximum_fusion.3.refs_4_), channel_id=1, source_target_pairs={{0,48},{16,0},{32,16},{48,32},{64,112},{80,64},{96,80},{112,96},{1... | collective-permute-start | bytes 589832 | tf_op jit(solution)/shard_map/ppermute | solution.py:341
  39.8 6.1 %collective-permute-start.31 = (bf16[4,6,16,256]{3,2,1,0:T(8,128)(2,1)S(1)}, bf16[4,6,16,256]{3,2,1,0:T(8,128)(2,1)S(1)}, u32[]{:S(2)}, u32[]{:S(2)}) collective-permute-start(bf16[4,6,16,256]{3,2,1,0:T(8,128)(2,1)S(1)} %pad_maximum_fusion.3.refs_4_), channel_id=1, source_target_pairs={{0,32},{16,48},{32,0},{48,16},{64,96},{80,112},{96,64},{112,80},{1... | collective-permute-start | bytes 589832 | tf_op jit(solution)/shard_map/ppermute | solution.py:341
  41.5 9.3 %collective-permute-start.30 = (bf16[4,6,16,256]{3,2,1,0:T(8,128)(2,1)S(1)}, bf16[4,6,16,256]{3,2,1,0:T(8,128)(2,1)S(1)}, u32[]{:S(2)}, u32[]{:S(2)}) collective-permute-start(bf16[4,6,16,256]{3,2,1,0:T(8,128)(2,1)S(1)} %pad_maximum_fusion.3.refs_4_), channel_id=1, source_target_pairs={{0,16},{16,32},{32,48},{48,0},{64,80},{80,96},{96,112},{112,64},{1... | collective-permute-start | bytes 589832 | tf_op jit(solution)/shard_map/ppermute | solution.py:341
  42.3 8.5 %collective-permute-start.26 = (bf16[4,6,16,256]{3,2,1,0:T(8,128)(2,1)S(1)}, bf16[4,6,16,256]{3,2,1,0:T(8,128)(2,1)S(1)}, u32[]{:S(2)}, u32[]{:S(2)}) collective-permute-start(bf16[4,6,16,256]{3,2,1,0:T(8,128)(2,1)S(1)} %pad_maximum_fusion.2.refs_0_), channel_id=1, source_target_pairs={{0,192},{16,208},{32,224},{48,240},{64,0},{80,16},{96,32},{112,48}... | collective-permute-start | bytes 589832 | tf_op jit(solution)/shard_map/ppermute | solution.py:341
  43.0 7.8 %collective-permute-start.25 = (bf16[4,6,16,256]{3,2,1,0:T(8,128)(2,1)S(1)}, bf16[4,6,16,256]{3,2,1,0:T(8,128)(2,1)S(1)}, u32[]{:S(2)}, u32[]{:S(2)}) collective-permute-start(bf16[4,6,16,256]{3,2,1,0:T(8,128)(2,1)S(1)} %pad_maximum_fusion.2.refs_0_), channel_id=1, source_target_pairs={{0,128},{16,144},{32,160},{48,176},{64,192},{80,208},{96,224},{112... | collective-permute-start | bytes 589832 | tf_op jit(solution)/shard_map/ppermute | solution.py:341
  44.1 8.0 %collective-permute-start.24 = (bf16[4,6,16,256]{3,2,1,0:T(8,128)(2,1)S(1)}, bf16[4,6,16,256]{3,2,1,0:T(8,128)(2,1)S(1)}, u32[]{:S(2)}, u32[]{:S(2)}) collective-permute-start(bf16[4,6,16,256]{3,2,1,0:T(8,128)(2,1)S(1)} %pad_maximum_fusion.2.refs_0_), channel_id=1, source_target_pairs={{0,64},{16,80},{32,96},{48,112},{64,128},{80,144},{96,160},{112,17... | collective-permute-start | bytes 589832 | tf_op jit(solution)/shard_map/ppermute | solution.py:341
  58.3 7.2 %collective-permute-start.34 = (bf16[8,12,16,256]{3,2,1,0:T(8,128)(2,1)S(1)}, bf16[8,12,16,256]{3,2,1,0:T(8,128)(2,1)S(1)}, u32[]{:S(2)}, u32[]{:S(2)}) collective-permute-start(bf16[8,12,16,256]{3,2,1,0:T(8,128)(2,1)S(1)} %get-tuple-element.87), channel_id=1, source_target_pairs={{0,1},{1,0},{2,3},{3,2},{4,5},{5,4},{6,7},{7,6},{8,9},{9,8},{10,11... | collective-permute-start | bytes 2359304 | tf_op jit(solution)/shard_map/ppermute | solution.py:383
  62.3 11.1 %collective-permute-start.33 = (bf16[12,16,256]{2,1,0:T(8,128)(2,1)S(1)}, bf16[12,16,256]{2,1,0:T(8,128)(2,1)S(1)}, u32[]{:S(2)}, u32[]{:S(2)}) collective-permute-start(bf16[12,16,256]{2,1,0:T(8,128)(2,1)S(1)} %get-tuple-element.85), channel_id=1, source_target_pairs={{0,0},{1,16},{2,32},{3,48},{4,64},{5,80},{6,96},{7,112},{8,128},{9... | collective-permute-start | bytes 294920 | tf_op jit(solution)/shard_map/ppermute | solution.py:380
  65.5 52.8 %copy-start.4 = (s32[64]{0:T(128)S(1)}, s32[64]{0:T(128)}, u32[]{:S(2)}) copy-start(s32[64]{0:T(128)} %param.16) | copy-start | bytes 772
  65.7 15.3 %collective-permute-start.35 = (bf16[12,16,256]{2,1,0:T(8,128)(2,1)S(1)}, bf16[12,16,256]{2,1,0:T(8,128)(2,1)S(1)}, u32[]{:S(2)}, u32[]{:S(2)}) collective-permute-start(bf16[12,16,256]{2,1,0:T(8,128)(2,1)S(1)} %get-tuple-element.89), channel_id=1, source_target_pairs={{0,2},{1,3},{2,4},{3,5},{4,6},{5,7},{6,8},{7,9},{8,10},{9,11},{10,... | collective-permute-start | bytes 294920 | tf_op jit(solution)/shard_map/ppermute | solution.py:387
  68.2 12.8 %collective-permute-start.36 = (bf16[12,16,256]{2,1,0:T(8,128)(2,1)S(1)}, bf16[12,16,256]{2,1,0:T(8,128)(2,1)S(1)}, u32[]{:S(2)}, u32[]{:S(2)}) collective-permute-start(bf16[12,16,256]{2,1,0:T(8,128)(2,1)S(1)} %get-tuple-element.90), channel_id=1, source_target_pairs={{0,14},{1,15},{2,0},{3,1},{4,2},{5,3},{6,4},{7,5},{8,6},{9,7},{10,... | collective-permute-start | bytes 294920 | tf_op jit(solution)/shard_map/ppermute | solution.py:387
  69.8 15.9 %collective-permute-start.37 = (bf16[12,16,256]{2,1,0:T(8,128)(2,1)S(1)}, bf16[12,16,256]{2,1,0:T(8,128)(2,1)S(1)}, u32[]{:S(2)}, u32[]{:S(2)}) collective-permute-start(bf16[12,16,256]{2,1,0:T(8,128)(2,1)S(1)} %get-tuple-element.91), channel_id=1, source_target_pairs={{0,4},{1,5},{2,6},{3,7},{4,8},{5,9},{6,10},{7,11},{8,12},{9,13},{1... | collective-permute-start | bytes 294920 | tf_op jit(solution)/shard_map/ppermute | solution.py:387
  72.7 13.0 %collective-permute-start.38 = (bf16[12,16,256]{2,1,0:T(8,128)(2,1)S(1)}, bf16[12,16,256]{2,1,0:T(8,128)(2,1)S(1)}, u32[]{:S(2)}, u32[]{:S(2)}) collective-permute-start(bf16[12,16,256]{2,1,0:T(8,128)(2,1)S(1)} %get-tuple-element.92), channel_id=1, source_target_pairs={{0,12},{1,13},{2,14},{3,15},{4,0},{5,1},{6,2},{7,3},{8,4},{9,5},{1... | collective-permute-start | bytes 294920 | tf_op jit(solution)/shard_map/ppermute | solution.py:387
  73.4 15.3 %collective-permute-start.39 = (bf16[12,16,256]{2,1,0:T(8,128)(2,1)S(1)}, bf16[12,16,256]{2,1,0:T(8,128)(2,1)S(1)}, u32[]{:S(2)}, u32[]{:S(2)}) collective-permute-start(bf16[12,16,256]{2,1,0:T(8,128)(2,1)S(1)} %get-tuple-element.93), channel_id=1, source_target_pairs={{0,6},{1,7},{2,8},{3,9},{4,10},{5,11},{6,12},{7,13},{8,14},{9,15},... | collective-permute-start | bytes 294920 | tf_op jit(solution)/shard_map/ppermute | solution.py:387
  81.0 7.7 %collective-permute-start.40 = (bf16[12,16,256]{2,1,0:T(8,128)(2,1)S(1)}, bf16[12,16,256]{2,1,0:T(8,128)(2,1)S(1)}, u32[]{:S(2)}, u32[]{:S(2)}) collective-permute-start(bf16[12,16,256]{2,1,0:T(8,128)(2,1)S(1)} %get-tuple-element.94), channel_id=1, source_target_pairs={{0,10},{1,11},{2,12},{3,13},{4,14},{5,15},{6,0},{7,1},{8,2},{9,3},... | collective-permute-start | bytes 294920 | tf_op jit(solution)/shard_map/ppermute | solution.py:387
  81.0 12.3 %collective-permute-start.41 = (bf16[12,16,256]{2,1,0:T(8,128)(2,1)S(1)}, bf16[12,16,256]{2,1,0:T(8,128)(2,1)S(1)}, u32[]{:S(2)}, u32[]{:S(2)}) collective-permute-start(bf16[12,16,256]{2,1,0:T(8,128)(2,1)S(1)} %get-tuple-element.95), channel_id=1, source_target_pairs={{0,8},{1,9},{2,10},{3,11},{4,12},{5,13},{6,14},{7,15},{8,0},{9,1},... | collective-permute-start | bytes 294920 | tf_op jit(solution)/shard_map/ppermute | solution.py:387
  113.4 14.4 %all-to-all-start.4 = ((f32[8,24,256]{2,1,0:T(8,128)}), f32[8,24,256]{2,1,0:T(8,128)S(1)}, u32[]{:S(2)}, u32[]{:S(2)}) async-start(f32[8,24,256]{2,1,0:T(8,128)} %broadcast_in_dim.67), calls=%async_computation.4 | async-start | bytes 393216 | tf_op jit(solution)/shard_map/all_to_all | solution.py:304
  128.6 15.8 %all-to-all-start.5 = ((bf16[32,24,256]{2,1,0:T(8,128)(2,1)}), bf16[32,24,256]{2,1,0:T(8,128)(2,1)S(1)}, u32[]{:S(2)}, u32[]{:S(2)}) async-start(bf16[32,24,256]{2,1,0:T(8,128)(2,1)} %broadcast_in_dim.68), calls=%async_computation.5 | async-start | bytes 786432 | tf_op jit(solution)/shard_map/all_to_all | solution.py:304
  (5 other events, 180.6 us)

commit v4 on v3

--- a/solution.py
+++ b/solution.py
@@ -12,7 +12,6 @@
 VMEM = pl.BlockSpec(memory_space=pltpu.VMEM)
 SMEM = pl.BlockSpec(memory_space=pltpu.SMEM)
 HBM = pl.BlockSpec(memory_space=pltpu.HBM)
-ANY = pl.BlockSpec(memory_space=pl.ANY)
 CHIPS = 8
 CORES = 2
 ROWS = 16
@@ -59,22 +58,27 @@
     return jnp.where(code < BLOCKS, one, two)
 
 
-def pick_kernel(each, found_ref, gathered_ref, own_ref, low_ref, high_ref, list_ref):
+def pick_kernel(each, found_ref, other_ref, gathered_ref, other_out_ref, low_ref, high_ref, list_ref, other_list):
+    half = low_ref.shape[0]
+
+    def chosen(found, codes, slot):
+        code = codes[slot]
+        s = jnp.maximum(found[jnp.maximum(code, 0)], 0)
+        block = gathered_ref[source(code, s, each)]
+        return jnp.where(code >= 0, block, jnp.zeros_like(block))
+
     compact(found_ref, list_ref)
-    half = low_ref.shape[0]
-    for slot in range(own_ref.shape[0]):
-        code = list_ref[slot]
-        s = jnp.maximum(found_ref[jnp.maximum(code, 0)], 0)
-        block = gathered_ref[source(code, s, each)]
-        block = jnp.where(code >= 0, block, jnp.zeros_like(block))
-        own_ref[slot] = block
+    compact(other_ref, other_list)
+    for slot in range(2 * half):
+        block = chosen(found_ref, list_ref, slot)
         if slot < half:
             low_ref[slot] = block
         else:
             high_ref[slot - half] = block
-
-
-def pick(slots, each, found, gathered):
+        other_out_ref[slot] = chosen(other_ref, other_list, slot)
+
+
+def pick(slots, each, found, other, gathered):
     tail = gathered.shape[1:]
     half = jax.ShapeDtypeStruct((slots // 2,) + tail, BF16)
     return pl.pallas_call(
@@ -83,18 +87,19 @@
             jax.ShapeDtypeStruct((slots,) + tail, BF16), half, half,
             jax.ShapeDtypeStruct((LIST,), jnp.int32),
         ),
-        in_specs=[SMEM, VMEM],
+        in_specs=[SMEM, SMEM, VMEM],
         out_specs=(VMEM, VMEM, VMEM, SMEM),
+        scratch_shapes=[pltpu.SMEM((LIST,), jnp.int32)],
         compiler_params=params(),
         name="pick",
-    )(found, gathered)
+    )(found, other, gathered)
 
 
 def product_kernel(rows_ref, cols_ref, here_ref, region_ref, *refs):
     low_refs, high_refs = refs[:SIDE], refs[SIDE:2 * SIDE]
-    keep_ref, send_ref, list_ref, region, wide, turned, narrow, panel, total, region_sem, sem = refs[2 * SIDE:]
+    keep_ref, send_ref, list_ref, region, wide, turned, panel, total, region_sem = refs[2 * SIDE:]
     width = region.shape[1]
-    slots = narrow.shape[0]
+    slots = keep_ref.shape[1]
     half = slots // 2
     core, depth, x, y = here_ref[0], here_ref[1], here_ref[2], here_ref[3]
     compact(rows_ref, list_ref)
@@ -106,18 +111,6 @@
         slot = list_ref[2 * BLOCKS + code]
         return slot, (slot >= 0) & (slot < slots)
 
-    copies = []
-    for i, (low, high) in enumerate(zip(low_refs, high_refs)):
-        for j in range(SIDE):
-            for side, ref in enumerate((low, high)):
-                dx, dy = (j, i) if side == 0 else (i, j)
-                row = lax.rem(y + SIDE - dy, SIDE) * SIDE + lax.rem(x + SIDE - dx, SIDE)
-                place = pl.ds(pl.multiple_of(row * ROWS, ROWS), ROWS)
-                copies.append(pltpu.make_async_copy(
-                    ref.at[j], narrow.at[pl.ds(side * half, half), place, :], sem.at[len(copies)]
-                ))
-    for copy in copies:
-        copy.start()
     for at in range(BLOCKS):
         pl.when(slot_of(at)[1])(region_copy(at).start)
     panel[...] = jnp.zeros(panel.shape, BF16)
@@ -127,14 +120,23 @@
             keep_ref[:, slot] = jnp.zeros((CHIPS, ROWS, width), F32)
             send_ref[:, slot] = jnp.zeros((CHIPS, ROWS, width), BF16)
 
-    for copy in copies:
-        copy.wait()
+    rows = [[[None, None] for _ in range(SIDE)] for _ in range(SIDE)]
+    for i in range(SIDE):
+        for j in range(SIDE):
+            for side, (dx, dy) in enumerate(((j, i), (i, j))):
+                row = lax.rem(y + SIDE - dy, SIDE) * SIDE + lax.rem(x + SIDE - dx, SIDE)
+                rows[i][j][side] = row * ROWS
     for slot in range(slots):
         code = cols_ref[slot]
+        side, local = divmod(slot, half)
+        refs_here = (low_refs, high_refs)[side]
 
         @pl.when(code >= 0)
         def _():
-            panel[pl.ds(pl.multiple_of(code * width, width), width), :] = narrow[slot]
+            for i in range(SIDE):
+                for j in range(SIDE):
+                    place = pl.multiple_of(code * width + rows[i][j][side], ROWS)
+                    panel[pl.ds(place, ROWS), :] = refs_here[i][j, local]
 
     deep = BLOCKS * width
 
@@ -178,59 +180,102 @@
             jax.ShapeDtypeStruct(shape, F32), jax.ShapeDtypeStruct(shape, BF16),
             jax.ShapeDtypeStruct((LIST,), jnp.int32),
         ),
-        in_specs=[SMEM, SMEM, SMEM, HBM] + [ANY] * (2 * SIDE),
+        in_specs=[SMEM, SMEM, SMEM, HBM] + [VMEM] * (2 * SIDE),
         out_specs=(VMEM, VMEM, SMEM),
         scratch_shapes=[
             pltpu.VMEM((blocks, width, blocks, width), BF16),
             pltpu.VMEM((width // LANES, width * blocks, LANES), F32),
             pltpu.VMEM((width, blocks * width), BF16),
-            pltpu.VMEM((slots, width, width), BF16),
             pltpu.VMEM((2 * blocks * width, width), BF16),
             pltpu.VMEM((CHIPS, CORES, ROWS, width), F32),
             pltpu.SemaphoreType.DMA((blocks,)),
-            pltpu.SemaphoreType.DMA((2 * SIDE * SIDE,)),
         ],
         compiler_params=params(48),
+        cost_estimate=pl.CostEstimate(
+            flops=2 * slots * blocks * width**3, bytes_accessed=2 * region.size, transcendentals=0
+        ),
         name="product",
     )(rows, cols, here, region, *lows, *highs)
 
 
-def pair_kernel(keep_ref, got_ref, *out_refs):
-    for d, out_ref in enumerate(out_refs):
-        out_ref[...] = (keep_ref[d] + got_ref[d].astype(F32)).astype(BF16)
+UP = (3, 1)
+DOWN = (4, 6)
+ON = (2, 5, 7)
+
+
+def pair_kernel(keep_ref, got_ref, own_ref, up_ref, down_ref, on_ref):
+    def share(d):
+        return keep_ref[d] + got_ref[d].astype(F32)
+
+    own_ref[...] = share(0)
+    for out_ref, ways in ((up_ref, UP), (down_ref, DOWN), (on_ref, ON)):
+        for i, d in enumerate(ways):
+            out_ref[i] = share(d).astype(out_ref.dtype)
 
 
 def pair(keep, got):
-    share = jax.ShapeDtypeStruct(keep.shape[1:], BF16)
+    share = keep.shape[1:]
     return pl.pallas_call(
         pair_kernel,
-        out_shape=(share,) * CHIPS,
+        out_shape=(
+            jax.ShapeDtypeStruct(share, F32),
+            jax.ShapeDtypeStruct((len(UP),) + share, BF16),
+            jax.ShapeDtypeStruct((len(DOWN),) + share, BF16),
+            jax.ShapeDtypeStruct((len(ON),) + share, F32),
+        ),
         in_specs=[VMEM, VMEM],
-        out_specs=(VMEM,) * CHIPS,
+        out_specs=(VMEM,) * 4,
         compiler_params=params(),
         name="pair",
     )(keep, got)
 
 
+def merge_kernel(on_ref, up_ref, down_ref, *out_refs):
+    for i, (out_ref, came) in enumerate(zip(out_refs, (up_ref.at[0], down_ref.at[0], down_ref.at[1]))):
+        out_ref[...] = (on_ref[i] + came[...].astype(F32)).astype(BF16)
+
+
+def merge(on, up, down):
+    share = jax.ShapeDtypeStruct(on.shape[1:], BF16)
+    return pl.pallas_call(
+        merge_kernel,
+        out_shape=(share,) * len(ON),
+        in_specs=[VMEM] * 3,
+        out_specs=(VMEM,) * len(ON),
+        compiler_params=params(),
+        name="merge",
+    )(on, up, down)
+
+
+def sum_along_z(keep, got):
+    own, up, down, on = pair(keep, got)
+    up = lax.ppermute(up, "pcol", along_z(1))
+    down = lax.ppermute(down, "pcol", along_z(CHIPS - 1))
+    on = merge(on, up, down)
+    came = [lax.ppermute(on[i], "pcol", along_z(ON[i])) for i in (1, 2, 0)]
+    return [own, up] + came
+
+
 def across(a, b):
     return lax.dot_general(a, b, (((0,), (0,)), ((), ())), preferred_element_type=F32)
 
 
 def columns_kernel(list_ref, found_ref, rows_ref, link_ref, *refs):
-    parts = refs[:CHIPS]
-    one_ref, two_ref, sums_ref, sums, rows = refs[CHIPS:]
+    own_ref, up_ref = refs[:2]
+    came_refs = refs[2:2 + len(ON)]
+    one_ref, two_ref, sums_ref, sums, rows = refs[2 + len(ON):]
     blocks, share, width = one_ref.shape
     deep = blocks * share
     rows[...] = jnp.zeros(rows.shape, BF16)
     sums[...] = jnp.zeros(sums.shape, F32)
-    for slot in range(parts[0].shape[0]):
+    for slot in range(own_ref.shape[0]):
         code = list_ref[slot]
 
         @pl.when(code >= 0)
         def _():
-            total = parts[0][slot].astype(F32)
-            for part in parts[1:]:
-                total = total + part[slot].astype(F32)
+            total = own_ref[slot] + up_ref[1, slot].astype(F32)
+            for came in came_refs:
+                total = total + came[slot].astype(F32)
             place = pl.ds(pl.multiple_of(code * share, share), share)
             sums[place] = -total
             rows[place] = rows_ref[slot]
@@ -256,7 +301,7 @@
     return pl.pallas_call(
         columns_kernel,
         out_shape=(column, column, jax.ShapeDtypeStruct((3 * width, width), BF16)),
-        in_specs=[SMEM, SMEM, VMEM, VMEM] + [VMEM] * CHIPS,
+        in_specs=[SMEM, SMEM, VMEM, VMEM] + [VMEM] * (2 + len(ON)),
         out_specs=(VMEM, VMEM, VMEM),
         scratch_shapes=[
             pltpu.VMEM((2 * BLOCKS * share, width), F32),
@@ -310,12 +355,12 @@
         [p * cols_grid + z * CORES + c for p in range(rows_grid) for c in range(CORES)]
         for z in range(CHIPS)
     ]
-    lines = [[z * CORES + c for z in range(CHIPS)] for c in range(CORES)]
     ways = rows_grid * CORES
     height, width = sums.shape
     share = height // ways
     pieces = swap_axes(sums.reshape(ways, share, width), both, planes)
     piece = jnp.sum(pieces.astype(F32), axis=0)
+    lines = [[z * CORES + c for z in range(CHIPS)] for c in range(CORES)]
     pieces = swap_axes(jnp.broadcast_to(piece, (CHIPS, share, width)), "pcol", lines)
     piece = jnp.sum(pieces, axis=0).astype(BF16)
     pieces = swap_axes(jnp.broadcast_to(piece, (ways, share, width)), both, planes)
@@ -367,24 +412,24 @@
     each = tuple(panel.shape[0] for panel in panels)
     found_cols = places(steps * cols_grid + q, pattern_one, pattern_two)
     found_rows = places(steps * rows_grid + p, pattern_one, pattern_two)
+    found_other = places(steps * rows_grid + (q - p) % rows_grid, pattern_one, pattern_two)
     mine = jnp.concatenate(
         [lax.dynamic_slice_in_dim(panel, p * ROWS, ROWS, 1) for panel in panels], axis=0
     )
     gathered = lax.all_gather(mine, "pcol", axis=0, tiled=True)
 
-    def invert(slots, gathered, found_cols, found_rows, region, link, inv_one, inv_two):
-        own, low, high, col_list = pick(slots, each, found_cols, gathered)
-        transpose = [
-            (a * cols_grid + b, b * cols_grid + a) for a in range(rows_grid) for b in range(cols_grid)
+    def invert(slots, gathered, found_cols, found_other, found_rows, region, link, inv_one, inv_two):
+        other, low, high, col_list = pick(slots, each, found_cols, found_other, gathered)
+        moves = [
+            (a * cols_grid + b, (b - a) % rows_grid * cols_grid + a)
+            for a in range(rows_grid) for b in range(cols_grid)
         ]
-        rows = lax.ppermute(own, ("prow", "pcol"), transpose)
+        rows = lax.ppermute(other, ("prow", "pcol"), moves)
         lows, highs = spread_plane(low, high)
         keep, give, row_list = product(slots, found_rows, col_list, here, region, lows, highs)
+        give, rows = lax.optimization_barrier((give, rows))
         got = lax.ppermute(give, "pcol", [(i, i ^ 1) for i in range(cols_grid)])
-        shares = pair(keep, got)
-        parts = [shares[0]]
-        for d in (1, 7, 2, 6, 3, 5, 4):
-            parts.append(lax.ppermute(shares[d], "pcol", along_z(d)))
+        parts = sum_along_z(keep, got)
         column_one, column_two, sums = columns(row_list, found_rows, parts, rows, link)
         sums = sum_everywhere(sums, rows_grid, cols_grid)
         diagonal_one, cross_two, diagonal_two = diagonals(sums, link, inv_one, inv_two)
@@ -396,7 +441,7 @@
         for pattern in (pattern_one, pattern_two)
     )
     fits = jnp.all(members <= FEW)
-    given = (gathered, found_cols, found_rows, inverse_region, link_block, inv_diag_one, inv_diag_two)
+    given = (gathered, found_cols, found_other, found_rows, inverse_region, link_block, inv_diag_one, inv_diag_two)
     return lax.cond(
         fits,
         lambda outs, *given: outs,

time: 146 us -> 139 us (0.952)
  starting transfers between devices: 47.7 us -> 43 us
  waiting for transfers between devices: 39.5 us -> 35.1 us
  blocking collectives: 41.3 us -> 43.3 us
    ppermute x12, waiting for transfers between devices: 10.4 us -> 3.08 us  [around(): moved[d] = lax.ppermute(value, 'prow', turn(d))]
    ppermute x8 -> x6, starting transfers between devices: 19.9 us -> 16.7 us  [the longest x1 7.41 us: invert(): rows = lax.ppermute(other, ('prow', 'pcol'), moves)]
    all_to_all x1, blocking collectives: 17.8 us -> 19.9 us  [swap_axes(): lax.all_to_all(value, axes, 0, 0, axis_index_groups=groups, tiled=True)]
    ppermute x1, waiting for transfers between devices: 0.01 us -> 1.91 us  [invert(): got = lax.ppermute(give, 'pcol', [(i, i ^ 1) for i in range(cols_grid)])]
    ppermute x1, starting transfers between devices: 3.99 us -> 2.45 us  [invert(): got = lax.ppermute(give, 'pcol', [(i, i ^ 1) for i in range(cols_grid)])]
    ppermute x8 -> x6, waiting for transfers between devices: 10.9 us -> 12 us  [the longest x3 6.94 us: sum_along_z(): came = [lax.ppermute(on[i], 'pcol', along_z(ON[i])) for i in (1, 2, 0)]]
  transfers between devices with their start and end apart: 23 -> 21, of which waited for: 11 -> 9; matrix products, arithmetic and copies ran while one was open for 1% -> 1% of each run, Pallas kernels for 0% -> 4%
where the time goes in v4:
time: 139 us
  blocking collectives  43.3 us (31%)
  starting transfers between devices  43 us (31%)
  waiting for transfers between devices  35.1 us (25%)
  Pallas kernels  10.1 us (7%)
  other arithmetic  3.11 us (2%)
  local copies, waits for them, and re-layouts  2.46 us (2%)
  between operations  1.55 us (1%)
    all_gather x1, blocking collectives, shards(): gathered = lax.all_gather(mine, 'pcol', axis=0, tiled=True)  23.5 us
    all_to_all x1, blocking collectives, swap_axes(): lax.all_to_all(value, axes, 0, 0, axis_index_groups=groups, tiled=True)  19.9 us
    all_to_all x2, waiting for transfers between devices, swap_axes(): lax.all_to_all(value, axes, 0, 0, axis_index_groups=groups, tiled=True)  18.1 us
    ppermute x12, starting transfers between devices, around(): moved[d] = lax.ppermute(value, 'prow', turn(d))  13.9 us
    all_to_all x2, starting transfers between devices, swap_axes(): lax.all_to_all(value, axes, 0, 0, axis_index_groups=groups, tiled=True)  9.92 us
    ppermute x1, starting transfers between devices, invert(): rows = lax.ppermute(other, ('prow', 'pcol'), moves)  7.41 us
    ppermute x3, waiting for transfers between devices, sum_along_z(): came = [lax.ppermute(on[i], 'pcol', along_z(ON[i])) for i in (1, 2, 0)]  6.94 us
    pallas_call x1, Pallas kernels, product(): pl.pallas_call(product_kernel, out_shape=(jax.ShapeDtypeStruct(shape, F32...  5.53 us
  transfers between devices with their start and end apart: 21, of which 9 were waited for; matrix products, arithmetic and copies ran while one was open for 1% of the time, Pallas kernels for 4%

profile of v4, /device:TPU:1, one launch (start us, length us, event | category | flops | bytes accessed | tf_op | source)
XLA Modules:
  0.0 138.7 jit_solution(17746415698900684222)
XLA Ops:
  1.7 23.5 %all_gather.3.gathered_ref = bf16[96,16,256]{2,1,0:T(8,128)(2,1)S(1)} all-gather(bf16[6,16,256]{2,1,0:T(8,128)(2,1)S(1)} %pad_maximum_fusion.4), channel_id=1, replica_groups=mesh['prow'=16,'pcol'=16] {'pcol'}, dimensions={0}, use_global_device_ids=true | all-gather | bytes 835584 | tf_op jit(solution)/shard_map/all_gather | solution.py:419
  27.1 1.4 %pick.3 = (bf16[12,16,256]{2,1,0:T(8,128)(2,1)S(1)}, bf16[6,16,256]{2,1,0:T(8,128)(2,1)S(1)}, bf16[6,16,256]{2,1,0:T(8,128)(2,1)S(1)}, s32[33]{0:T(128)S(1)}) custom-call(s32[16]{0:T(128)S(1)} %pad_add_fusion.found_ref, s32[16]{0:T(128)S(1)} %pad_add_fusion.1.other_ref, bf16[96,16,256]{2,1,0:T(8,128)(2,1)S(1)} %all_gather.3.gathered_ref), custom_call_target="tpu_custom_call" | custom-call | tf_op jit(solution)/shard_map/pick/pallas_call | solution.py:84
  28.5 2.8 %collective-permute-start.27 = (bf16[6,16,256]{2,1,0:T(8,128)(2,1)S(1)}, bf16[6,16,256]{2,1,0:T(8,128)(2,1)S(1)}, u32[]{:S(2)}, u32[]{:S(2)}) collective-permute-start(bf16[6,16,256]{2,1,0:T(8,128)(2,1)S(1)} %get-tuple-element.88), channel_id=1, source_target_pairs={{0,192},{16,208},{32,224},{48,240},{64,0},{80,16},{96,32},{112,48}... | collective-permute-start | bytes 147464 | tf_op jit(solution)/shard_map/ppermute | solution.py:386
  32.4 2.5 %collective-permute-start.21 = (bf16[6,16,256]{2,1,0:T(8,128)(2,1)S(1)}, bf16[6,16,256]{2,1,0:T(8,128)(2,1)S(1)}, u32[]{:S(2)}, u32[]{:S(2)}) collective-permute-start(bf16[6,16,256]{2,1,0:T(8,128)(2,1)S(1)} %get-tuple-element.87), channel_id=1, source_target_pairs={{0,48},{16,0},{32,16},{48,32},{64,112},{80,64},{96,80},{112,96},{1... | collective-permute-start | bytes 147464 | tf_op jit(solution)/shard_map/ppermute | solution.py:386
  36.8 2.6 %collective-permute-start.30 = (bf16[4,6,16,256]{3,2,1,0:T(8,128)(2,1)S(1)}, bf16[4,6,16,256]{3,2,1,0:T(8,128)(2,1)S(1)}, u32[]{:S(2)}, u32[]{:S(2)}) collective-permute-start(bf16[4,6,16,256]{3,2,1,0:T(8,128)(2,1)S(1)} %pad_maximum_fusion.3.refs_4_), channel_id=1, source_target_pairs={{0,48},{16,0},{32,16},{48,32},{64,112},{80,64},{96,80},{112,96},{1... | collective-permute-start | bytes 589832 | tf_op jit(solution)/shard_map/ppermute | solution.py:386
  40.5 1.4 %collective-permute-start.24 = (bf16[4,6,16,256]{3,2,1,0:T(8,128)(2,1)S(1)}, bf16[4,6,16,256]{3,2,1,0:T(8,128)(2,1)S(1)}, u32[]{:S(2)}, u32[]{:S(2)}) collective-permute-start(bf16[4,6,16,256]{3,2,1,0:T(8,128)(2,1)S(1)} %pad_maximum_fusion.2.refs_0_), channel_id=1, source_target_pairs={{0,192},{16,208},{32,224},{48,240},{64,0},{80,16},{96,32},{112,48}... | collective-permute-start | bytes 589832 | tf_op jit(solution)/shard_map/ppermute | solution.py:386
  41.9 1.4 %collective-permute-start.23 = (bf16[4,6,16,256]{3,2,1,0:T(8,128)(2,1)S(1)}, bf16[4,6,16,256]{3,2,1,0:T(8,128)(2,1)S(1)}, u32[]{:S(2)}, u32[]{:S(2)}) collective-permute-start(bf16[4,6,16,256]{3,2,1,0:T(8,128)(2,1)S(1)} %pad_maximum_fusion.2.refs_0_), channel_id=1, source_target_pairs={{0,128},{16,144},{32,160},{48,176},{64,192},{80,208},{96,224},{112... | collective-permute-start | bytes 589832 | tf_op jit(solution)/shard_map/ppermute | solution.py:386
  43.8 1.9 %collective-permute-done.29.refs_6_ = bf16[4,6,16,256]{3,2,1,0:T(8,128)(2,1)S(1)} collective-permute-done((bf16[4,6,16,256]{3,2,1,0:T(8,128)(2,1)S(1)}, bf16[4,6,16,256]{3,2,1,0:T(8,128)(2,1)S(1)}, u32[]{:S(2)}, u32[]{:S(2)}) %collective-permute-start.29) | collective-permute-done | bytes 196640 | tf_op jit(solution)/shard_map/ppermute | solution.py:386
  45.8 7.4 %collective-permute-start.31 = (bf16[12,16,256]{2,1,0:T(8,128)(2,1)S(1)}, bf16[12,16,256]{2,1,0:T(8,128)(2,1)S(1)}, u32[]{:S(2)}, u32[]{:S(2)}) collective-permute-start(bf16[12,16,256]{2,1,0:T(8,128)(2,1)S(1)} %get-tuple-element.91), channel_id=1, source_target_pairs={{0,0},{1,16},{2,32},{3,48},{4,64},{5,80},{6,96},{7,112},{8,128},{9... | collective-permute-start | bytes 294920 | tf_op jit(solution)/shard_map/ppermute | solution.py:427
  53.2 5.5 %product.3 = (f32[8,12,16,256]{3,2,1,0:T(8,128)S(1)}, bf16[8,12,16,256]{3,2,1,0:T(8,128)(2,1)S(1)}, s32[33]{0:T(128)S(1)}) custom-call(s32[16]{0:T(128)S(1)} %pad_add_fusion.2.rows_ref.found_ref, s32[33]{0:T(128)S(1)} %get-tuple-element.86.cols_ref, s32[4]{0:T(128)S(1)} %pad_add_fusion.3.here_ref, bf16[8,256,8,256]{3,2,1,0:T(8,128)(2,1)} %region_ref.1, ...), custom_call_target="tpu_custom_call" | custom-call | flops 3221225472 | bytes 8388608 | tf_op jit(solution)/shard_map/product/pallas_call | solution.py:177
  58.8 2.4 %collective-permute-start.32 = (bf16[8,12,16,256]{3,2,1,0:T(8,128)(2,1)S(1)}, bf16[8,12,16,256]{3,2,1,0:T(8,128)(2,1)S(1)}, u32[]{:S(2)}, u32[]{:S(2)}) collective-permute-start(bf16[8,12,16,256]{3,2,1,0:T(8,128)(2,1)S(1)} %get-tuple-element.94), channel_id=1, source_target_pairs={{0,1},{1,0},{2,3},{3,2},{4,5},{5,4},{6,7},{7,6},{8,9},{9,8},{10,11... | collective-permute-start | bytes 2359304 | tf_op jit(solution)/shard_map/ppermute | solution.py:431
  61.2 1.9 %collective-permute-done.32.got_ref = bf16[8,12,16,256]{3,2,1,0:T(8,128)(2,1)S(1)} collective-permute-done((bf16[8,12,16,256]{3,2,1,0:T(8,128)(2,1)S(1)}, bf16[8,12,16,256]{3,2,1,0:T(8,128)(2,1)S(1)}, u32[]{:S(2)}, u32[]{:S(2)}) %collective-permute-start.32) | collective-permute-done | bytes 786464 | tf_op jit(solution)/shard_map/ppermute | solution.py:431
  64.5 3.5 %collective-permute-start.34 = (bf16[2,12,16,256]{3,2,1,0:T(8,128)(2,1)S(1)}, bf16[2,12,16,256]{3,2,1,0:T(8,128)(2,1)S(1)}, u32[]{:S(2)}, u32[]{:S(2)}) collective-permute-start(bf16[2,12,16,256]{3,2,1,0:T(8,128)(2,1)S(1)} %get-tuple-element.98), channel_id=1, source_target_pairs={{0,14},{1,15},{2,0},{3,1},{4,2},{5,3},{6,4},{7,5},{8,6},{9,7},{10,... | collective-permute-start | bytes 589832 | tf_op jit(solution)/shard_map/ppermute | solution.py:253
  68.0 5.1 %collective-permute-done.33.up_ref.refs_1_ = bf16[2,12,16,256]{3,2,1,0:T(8,128)(2,1)S(1)} collective-permute-done((bf16[2,12,16,256]{3,2,1,0:T(8,128)(2,1)S(1)}, bf16[2,12,16,256]{3,2,1,0:T(8,128)(2,1)S(1)}, u32[]{:S(2)}, u32[]{:S(2)}) %collective-permute-start.33) | collective-permute-done | bytes 196640 | tf_op jit(solution)/shard_map/ppermute | solution.py:252
  73.2 2.2 %collective-permute-start.35 = (bf16[12,16,256]{2,1,0:T(8,128)(2,1)S(1)}, bf16[12,16,256]{2,1,0:T(8,128)(2,1)S(1)}, u32[]{:S(2)}, u32[]{:S(2)}) collective-permute-start(bf16[12,16,256]{2,1,0:T(8,128)(2,1)S(1)} %get-tuple-element.99), channel_id=1, source_target_pairs={{0,10},{1,11},{2,12},{3,13},{4,14},{5,15},{6,0},{7,1},{8,2},{9,3},... | collective-permute-start | bytes 294920 | tf_op jit(solution)/shard_map/ppermute | solution.py:255
  77.8 4.9 %collective-permute-done.35.refs_2_ = bf16[12,16,256]{2,1,0:T(8,128)(2,1)S(1)} collective-permute-done((bf16[12,16,256]{2,1,0:T(8,128)(2,1)S(1)}, bf16[12,16,256]{2,1,0:T(8,128)(2,1)S(1)}, u32[]{:S(2)}, u32[]{:S(2)}) %collective-permute-start.35) | collective-permute-done | bytes 98336 | tf_op jit(solution)/shard_map/ppermute | solution.py:255
  82.7 2.0 %collective-permute-done.36.refs_3_ = bf16[12,16,256]{2,1,0:T(8,128)(2,1)S(1)} collective-permute-done((bf16[12,16,256]{2,1,0:T(8,128)(2,1)S(1)}, bf16[12,16,256]{2,1,0:T(8,128)(2,1)S(1)}, u32[]{:S(2)}, u32[]{:S(2)}) %collective-permute-start.36) | collective-permute-done | bytes 98336 | tf_op jit(solution)/shard_map/ppermute | solution.py:255
  84.7 1.5 %columns.3 = (bf16[8,16,256]{2,1,0:T(8,128)(2,1)}, bf16[8,16,256]{2,1,0:T(8,128)(2,1)}, bf16[768,256]{1,0:T(8,128)(2,1)S(1)}) custom-call(s32[33]{0:T(128)S(1)} %get-tuple-element.89.list_ref, s32[16]{0:T(128)S(1)} %pad_add_fusion.2.rows_ref.found_ref, bf16[12,16,256]{2,1,0:T(8,128)(2,1)S(1)} %collective-permute-done.31.rows_ref, ...), custom_call_target="tpu_custom_call" | custom-call | tf_op jit(solution)/shard_map/columns/pallas_call | solution.py:301
  86.2 19.9 %all_to_all.30 = bf16[32,24,256]{2,1,0:T(8,128)(2,1)S(1)} all-to-all(bf16[32,24,256]{2,1,0:T(8,128)(2,1)S(1)} %bitcast.30), channel_id=1, replica_groups={{0,1,16,17,32,33,48,49,64,65,80,81,96,97,112,113,128,129,144,145,160,16..., dimensions={0} | all-to-all | bytes 786432 | tf_op jit(solution)/shard_map/all_to_all | solution.py:349
  106.8 4.3 %all-to-all-start.4 = ((f32[8,24,256]{2,1,0:T(8,128)}), f32[8,24,256]{2,1,0:T(8,128)S(1)}, u32[]{:S(2)}, u32[]{:S(2)}) async-start(f32[8,24,256]{2,1,0:T(8,128)} %broadcast_in_dim.85), calls=%async_computation.4 | async-start | bytes 393216 | tf_op jit(solution)/shard_map/all_to_all | solution.py:349
  111.2 9.4 %all-to-all-done.4 = f32[8,24,256]{2,1,0:T(8,128)S(1)} async-done(((f32[8,24,256]{2,1,0:T(8,128)}), f32[8,24,256]{2,1,0:T(8,128)S(1)}, u32[]{:S(2)}, u32[]{:S(2)}) %all-to-all-start.4) | async-done | bytes 196640 | tf_op jit(solution)/shard_map/all_to_all | solution.py:349
  121.4 5.6 %all-to-all-start.5 = ((bf16[32,24,256]{2,1,0:T(8,128)(2,1)}), bf16[32,24,256]{2,1,0:T(8,128)(2,1)S(1)}, u32[]{:S(2)}, u32[]{:S(2)}) async-start(bf16[32,24,256]{2,1,0:T(8,128)(2,1)} %broadcast_in_dim.86), calls=%async_computation.5 | async-start | bytes 786432 | tf_op jit(solution)/shard_map/all_to_all | solution.py:349
  128.6 8.7 %all-to-all-done.5 = bf16[32,24,256]{2,1,0:T(8,128)(2,1)S(1)} async-done(((bf16[32,24,256]{2,1,0:T(8,128)(2,1)}), bf16[32,24,256]{2,1,0:T(8,128)(2,1)S(1)}, u32[]{:S(2)}, u32[]{:S(2)}) %all-to-all-start.5) | async-done | bytes 393248 | tf_op jit(solution)/shard_map/all_to_all | solution.py:349
  137.2 1.5 %diagonals.3 = (f32[256,256]{1,0:T(8,128)}, f32[256,256]{1,0:T(8,128)}, f32[256,256]{1,0:T(8,128)}) custom-call(bf16[768,256]{1,0:T(8,128)(2,1)S(1)} %bitcast.27, bf16[256,256]{1,0:T(8,128)(2,1)S(1)} %copy-done.1, f32[256,256]{1,0:T(8,128)S(1)} %copy-done.2, f32[256,256]{1,0:T(8,128)S(1)} %copy-done.3), custom_call_target="tpu_custom_call" | custom-call | tf_op jit(solution)/shard_map/diagonals/pallas_call | solution.py:338
  (67 shorter events, 13.8 us)
Async XLA Ops:
  28.5 6.9 %collective-permute-start.27 = (bf16[6,16,256]{2,1,0:T(8,128)(2,1)S(1)}, bf16[6,16,256]{2,1,0:T(8,128)(2,1)S(1)}, u32[]{:S(2)}, u32[]{:S(2)}) collective-permute-start(bf16[6,16,256]{2,1,0:T(8,128)(2,1)S(1)} %get-tuple-element.88), channel_id=1, source_target_pairs={{0,192},{16,208},{32,224},{48,240},{64,0},{80,16},{96,32},{112,48}... | collective-permute-start | bytes 147464 | tf_op jit(solution)/shard_map/ppermute | solution.py:386
  31.3 4.7 %collective-permute-start.26 = (bf16[6,16,256]{2,1,0:T(8,128)(2,1)S(1)}, bf16[6,16,256]{2,1,0:T(8,128)(2,1)S(1)}, u32[]{:S(2)}, u32[]{:S(2)}) collective-permute-start(bf16[6,16,256]{2,1,0:T(8,128)(2,1)S(1)} %get-tuple-element.88), channel_id=1, source_target_pairs={{0,128},{16,144},{32,160},{48,176},{64,192},{80,208},{96,224},{112... | collective-permute-start | bytes 147464 | tf_op jit(solution)/shard_map/ppermute | solution.py:386
  31.7 5.1 %collective-permute-start.25 = (bf16[6,16,256]{2,1,0:T(8,128)(2,1)S(1)}, bf16[6,16,256]{2,1,0:T(8,128)(2,1)S(1)}, u32[]{:S(2)}, u32[]{:S(2)}) collective-permute-start(bf16[6,16,256]{2,1,0:T(8,128)(2,1)S(1)} %get-tuple-element.88), channel_id=1, source_target_pairs={{0,64},{16,80},{32,96},{48,112},{64,128},{80,144},{96,160},{112,17... | collective-permute-start | bytes 147464 | tf_op jit(solution)/shard_map/ppermute | solution.py:386
  32.4 7.5 %collective-permute-start.21 = (bf16[6,16,256]{2,1,0:T(8,128)(2,1)S(1)}, bf16[6,16,256]{2,1,0:T(8,128)(2,1)S(1)}, u32[]{:S(2)}, u32[]{:S(2)}) collective-permute-start(bf16[6,16,256]{2,1,0:T(8,128)(2,1)S(1)} %get-tuple-element.87), channel_id=1, source_target_pairs={{0,48},{16,0},{32,16},{48,32},{64,112},{80,64},{96,80},{112,96},{1... | collective-permute-start | bytes 147464 | tf_op jit(solution)/shard_map/ppermute | solution.py:386
  34.8 5.6 %collective-permute-start.20 = (bf16[6,16,256]{2,1,0:T(8,128)(2,1)S(1)}, bf16[6,16,256]{2,1,0:T(8,128)(2,1)S(1)}, u32[]{:S(2)}, u32[]{:S(2)}) collective-permute-start(bf16[6,16,256]{2,1,0:T(8,128)(2,1)S(1)} %get-tuple-element.87), channel_id=1, source_target_pairs={{0,32},{16,48},{32,0},{48,16},{64,96},{80,112},{96,64},{112,80},{1... | collective-permute-start | bytes 147464 | tf_op jit(solution)/shard_map/ppermute | solution.py:386
  35.4 5.1 %collective-permute-start.19 = (bf16[6,16,256]{2,1,0:T(8,128)(2,1)S(1)}, bf16[6,16,256]{2,1,0:T(8,128)(2,1)S(1)}, u32[]{:S(2)}, u32[]{:S(2)}) collective-permute-start(bf16[6,16,256]{2,1,0:T(8,128)(2,1)S(1)} %get-tuple-element.87), channel_id=1, source_target_pairs={{0,16},{16,32},{32,48},{48,0},{64,80},{80,96},{96,112},{112,64},{1... | collective-permute-start | bytes 147464 | tf_op jit(solution)/shard_map/ppermute | solution.py:386
  36.8 6.9 %collective-permute-start.30 = (bf16[4,6,16,256]{3,2,1,0:T(8,128)(2,1)S(1)}, bf16[4,6,16,256]{3,2,1,0:T(8,128)(2,1)S(1)}, u32[]{:S(2)}, u32[]{:S(2)}) collective-permute-start(bf16[4,6,16,256]{3,2,1,0:T(8,128)(2,1)S(1)} %pad_maximum_fusion.3.refs_4_), channel_id=1, source_target_pairs={{0,48},{16,0},{32,16},{48,32},{64,112},{80,64},{96,80},{112,96},{1... | collective-permute-start | bytes 589832 | tf_op jit(solution)/shard_map/ppermute | solution.py:386
  39.3 6.4 %collective-permute-start.29 = (bf16[4,6,16,256]{3,2,1,0:T(8,128)(2,1)S(1)}, bf16[4,6,16,256]{3,2,1,0:T(8,128)(2,1)S(1)}, u32[]{:S(2)}, u32[]{:S(2)}) collective-permute-start(bf16[4,6,16,256]{3,2,1,0:T(8,128)(2,1)S(1)} %pad_maximum_fusion.3.refs_4_), channel_id=1, source_target_pairs={{0,32},{16,48},{32,0},{48,16},{64,96},{80,112},{96,64},{112,80},{1... | collective-permute-start | bytes 589832 | tf_op jit(solution)/shard_map/ppermute | solution.py:386
  39.9 13.3 %collective-permute-start.28 = (bf16[4,6,16,256]{3,2,1,0:T(8,128)(2,1)S(1)}, bf16[4,6,16,256]{3,2,1,0:T(8,128)(2,1)S(1)}, u32[]{:S(2)}, u32[]{:S(2)}) collective-permute-start(bf16[4,6,16,256]{3,2,1,0:T(8,128)(2,1)S(1)} %pad_maximum_fusion.3.refs_4_), channel_id=1, source_target_pairs={{0,16},{16,32},{32,48},{48,0},{64,80},{80,96},{96,112},{112,64},{1... | collective-permute-start | bytes 589832 | tf_op jit(solution)/shard_map/ppermute | solution.py:386
  40.5 12.7 %collective-permute-start.24 = (bf16[4,6,16,256]{3,2,1,0:T(8,128)(2,1)S(1)}, bf16[4,6,16,256]{3,2,1,0:T(8,128)(2,1)S(1)}, u32[]{:S(2)}, u32[]{:S(2)}) collective-permute-start(bf16[4,6,16,256]{3,2,1,0:T(8,128)(2,1)S(1)} %pad_maximum_fusion.2.refs_0_), channel_id=1, source_target_pairs={{0,192},{16,208},{32,224},{48,240},{64,0},{80,16},{96,32},{112,48}... | collective-permute-start | bytes 589832 | tf_op jit(solution)/shard_map/ppermute | solution.py:386
  41.9 11.3 %collective-permute-start.23 = (bf16[4,6,16,256]{3,2,1,0:T(8,128)(2,1)S(1)}, bf16[4,6,16,256]{3,2,1,0:T(8,128)(2,1)S(1)}, u32[]{:S(2)}, u32[]{:S(2)}) collective-permute-start(bf16[4,6,16,256]{3,2,1,0:T(8,128)(2,1)S(1)} %pad_maximum_fusion.2.refs_0_), channel_id=1, source_target_pairs={{0,128},{16,144},{32,160},{48,176},{64,192},{80,208},{96,224},{112... | collective-permute-start | bytes 589832 | tf_op jit(solution)/shard_map/ppermute | solution.py:386
  43.7 9.5 %collective-permute-start.22 = (bf16[4,6,16,256]{3,2,1,0:T(8,128)(2,1)S(1)}, bf16[4,6,16,256]{3,2,1,0:T(8,128)(2,1)S(1)}, u32[]{:S(2)}, u32[]{:S(2)}) collective-permute-start(bf16[4,6,16,256]{3,2,1,0:T(8,128)(2,1)S(1)} %pad_maximum_fusion.2.refs_0_), channel_id=1, source_target_pairs={{0,64},{16,80},{32,96},{48,112},{64,128},{80,144},{96,160},{112,17... | collective-permute-start | bytes 589832 | tf_op jit(solution)/shard_map/ppermute | solution.py:386
  45.8 13.0 %collective-permute-start.31 = (bf16[12,16,256]{2,1,0:T(8,128)(2,1)S(1)}, bf16[12,16,256]{2,1,0:T(8,128)(2,1)S(1)}, u32[]{:S(2)}, u32[]{:S(2)}) collective-permute-start(bf16[12,16,256]{2,1,0:T(8,128)(2,1)S(1)} %get-tuple-element.91), channel_id=1, source_target_pairs={{0,0},{1,16},{2,32},{3,48},{4,64},{5,80},{6,96},{7,112},{8,128},{9... | collective-permute-start | bytes 294920 | tf_op jit(solution)/shard_map/ppermute | solution.py:427
  58.8 4.4 %collective-permute-start.32 = (bf16[8,12,16,256]{3,2,1,0:T(8,128)(2,1)S(1)}, bf16[8,12,16,256]{3,2,1,0:T(8,128)(2,1)S(1)}, u32[]{:S(2)}, u32[]{:S(2)}) collective-permute-start(bf16[8,12,16,256]{3,2,1,0:T(8,128)(2,1)S(1)} %get-tuple-element.94), channel_id=1, source_target_pairs={{0,1},{1,0},{2,3},{3,2},{4,5},{5,4},{6,7},{7,6},{8,9},{9,8},{10,11... | collective-permute-start | bytes 2359304 | tf_op jit(solution)/shard_map/ppermute | solution.py:431
  63.3 9.8 %collective-permute-start.33 = (bf16[2,12,16,256]{3,2,1,0:T(8,128)(2,1)S(1)}, bf16[2,12,16,256]{3,2,1,0:T(8,128)(2,1)S(1)}, u32[]{:S(2)}, u32[]{:S(2)}) collective-permute-start(bf16[2,12,16,256]{3,2,1,0:T(8,128)(2,1)S(1)} %get-tuple-element.96), channel_id=1, source_target_pairs={{0,2},{1,3},{2,4},{3,5},{4,6},{5,7},{6,8},{7,9},{8,10},{9,11},{10,... | collective-permute-start | bytes 589832 | tf_op jit(solution)/shard_map/ppermute | solution.py:252
  64.5 8.6 %collective-permute-start.34 = (bf16[2,12,16,256]{3,2,1,0:T(8,128)(2,1)S(1)}, bf16[2,12,16,256]{3,2,1,0:T(8,128)(2,1)S(1)}, u32[]{:S(2)}, u32[]{:S(2)}) collective-permute-start(bf16[2,12,16,256]{3,2,1,0:T(8,128)(2,1)S(1)} %get-tuple-element.98), channel_id=1, source_target_pairs={{0,14},{1,15},{2,0},{3,1},{4,2},{5,3},{6,4},{7,5},{8,6},{9,7},{10,... | collective-permute-start | bytes 589832 | tf_op jit(solution)/shard_map/ppermute | solution.py:253
  73.1 53.9 %copy-start.5 = (s32[32]{0:T(128)S(1)}, s32[32]{0:T(128)}, u32[]{:S(2)}) copy-start(s32[32]{0:T(128)} %param.17) | copy-start | bytes 388
  73.2 64.1 %copy-start.2 = (f32[256,256]{1,0:T(8,128)S(1)}, f32[256,256]{1,0:T(8,128)}, u32[]{:S(2)}) copy-start(f32[256,256]{1,0:T(8,128)} %inv_one_ref.1) | copy-start | bytes 786436
  73.2 64.1 %copy-start.3 = (f32[256,256]{1,0:T(8,128)S(1)}, f32[256,256]{1,0:T(8,128)}, u32[]{:S(2)}) copy-start(f32[256,256]{1,0:T(8,128)} %inv_two_ref.1) | copy-start | bytes 786436
  73.2 9.5 %collective-permute-start.35 = (bf16[12,16,256]{2,1,0:T(8,128)(2,1)S(1)}, bf16[12,16,256]{2,1,0:T(8,128)(2,1)S(1)}, u32[]{:S(2)}, u32[]{:S(2)}) collective-permute-start(bf16[12,16,256]{2,1,0:T(8,128)(2,1)S(1)} %get-tuple-element.99), channel_id=1, source_target_pairs={{0,10},{1,11},{2,12},{3,13},{4,14},{5,15},{6,0},{7,1},{8,2},{9,3},... | collective-permute-start | bytes 294920 | tf_op jit(solution)/shard_map/ppermute | solution.py:255
  75.4 9.3 %collective-permute-start.36 = (bf16[12,16,256]{2,1,0:T(8,128)(2,1)S(1)}, bf16[12,16,256]{2,1,0:T(8,128)(2,1)S(1)}, u32[]{:S(2)}, u32[]{:S(2)}) collective-permute-start(bf16[12,16,256]{2,1,0:T(8,128)(2,1)S(1)} %get-tuple-element.100), channel_id=1, source_target_pairs={{0,14},{1,15},{2,0},{3,1},{4,2},{5,3},{6,4},{7,5},{8,6},{9,7},{10,... | collective-permute-start | bytes 294920 | tf_op jit(solution)/shard_map/ppermute | solution.py:255
  76.5 8.3 %collective-permute-start.37 = (bf16[12,16,256]{2,1,0:T(8,128)(2,1)S(1)}, bf16[12,16,256]{2,1,0:T(8,128)(2,1)S(1)}, u32[]{:S(2)}, u32[]{:S(2)}) collective-permute-start(bf16[12,16,256]{2,1,0:T(8,128)(2,1)S(1)} %get-tuple-element.101), channel_id=1, source_target_pairs={{0,4},{1,5},{2,6},{3,7},{4,8},{5,9},{6,10},{7,11},{8,12},{9,13},{1... | collective-permute-start | bytes 294920 | tf_op jit(solution)/shard_map/ppermute | solution.py:255
  106.8 13.8 %all-to-all-start.4 = ((f32[8,24,256]{2,1,0:T(8,128)}), f32[8,24,256]{2,1,0:T(8,128)S(1)}, u32[]{:S(2)}, u32[]{:S(2)}) async-start(f32[8,24,256]{2,1,0:T(8,128)} %broadcast_in_dim.85), calls=%async_computation.4 | async-start | bytes 393216 | tf_op jit(solution)/shard_map/all_to_all | solution.py:349
  121.4 15.8 %all-to-all-start.5 = ((bf16[32,24,256]{2,1,0:T(8,128)(2,1)}), bf16[32,24,256]{2,1,0:T(8,128)(2,1)S(1)}, u32[]{:S(2)}, u32[]{:S(2)}) async-start(bf16[32,24,256]{2,1,0:T(8,128)(2,1)} %broadcast_in_dim.86), calls=%async_computation.5 | async-start | bytes 786432 | tf_op jit(solution)/shard_map/all_to_all | solution.py:349
  (3 other events, 74.9 us)

commit v5 on v4

--- a/solution.py
+++ b/solution.py
@@ -50,6 +50,7 @@
 
 SIDE = 4
 FEW = 12
+AHEAD = 3
 
 
 def source(code, s, each):
@@ -111,8 +112,12 @@
         slot = list_ref[2 * BLOCKS + code]
         return slot, (slot >= 0) & (slot < slots)
 
-    for at in range(BLOCKS):
-        pl.when(slot_of(at)[1])(region_copy(at).start)
+    def fetch(u):
+        at = list_ref[jnp.minimum(u, BLOCKS - 1)]
+        pl.when((u < BLOCKS) & (at >= 0) & (at < BLOCKS))(lambda: region_copy(at).start())
+
+    for u in range(AHEAD):
+        fetch(u)
     panel[...] = jnp.zeros(panel.shape, BF16)
     for slot in range(slots):
         @pl.when(list_ref[slot] < 0)
@@ -148,12 +153,14 @@
             keep_ref[d, slot] = total[z, core]
             send_ref[d, slot] = total[z, 1 - core].astype(BF16)
 
-    def step(at, carry):
-        first, present = slot_of(at)
-        second, both = slot_of(BLOCKS + at)
+    def step(u, carry):
+        at = list_ref[u]
+        present = (at >= 0) & (at < BLOCKS)
+        second, both = slot_of(BLOCKS + jnp.where(present, at, 0))
 
         @pl.when(present)
         def _():
+            fetch(u + AHEAD)
             region_copy(at).wait()
             for h in range(width // LANES):
                 part = region[at, :, :, pl.ds(h * LANES, LANES)]
@@ -163,7 +170,7 @@
                     turned[:, pl.ds(c * width + h * LANES, LANES)] = wide[
                         h, pl.ds(c, width, stride=BLOCKS), :
                     ].astype(BF16)
-            multiply(0, first)
+            multiply(0, u)
             pl.when(both)(lambda: multiply(1, second))
 
         return carry
@@ -247,13 +254,14 @@
     )(on, up, down)
 
 
-def sum_along_z(keep, got):
+def sum_along_z(keep, got, fits):
     own, up, down, on = pair(keep, got)
     up = lax.ppermute(up, "pcol", along_z(1))
     down = lax.ppermute(down, "pcol", along_z(CHIPS - 1))
+    up, fits = lax.optimization_barrier((up, fits))
     on = merge(on, up, down)
     came = [lax.ppermute(on[i], "pcol", along_z(ON[i])) for i in (1, 2, 0)]
-    return [own, up] + came
+    return [own, up] + came, fits
 
 
 def across(a, b):
@@ -345,6 +353,25 @@
     )(sums, link, inv_one, inv_two)
 
 
+def fold_kernel(pieces_ref, out_ref):
+    total = pieces_ref[0].astype(F32)
+    for i in range(1, pieces_ref.shape[0]):
+        total = total + pieces_ref[i].astype(F32)
+    for i in range(out_ref.shape[0]):
+        out_ref[i] = total.astype(out_ref.dtype)
+
+
+def fold(pieces, copies, dtype):
+    return pl.pallas_call(
+        fold_kernel,
+        out_shape=jax.ShapeDtypeStruct((copies,) + pieces.shape[1:], dtype),
+        in_specs=[VMEM],
+        out_specs=VMEM,
+        compiler_params=params(),
+        name="fold",
+    )(pieces)
+
+
 def swap_axes(value, axes, groups=None):
     return lax.all_to_all(value, axes, 0, 0, axis_index_groups=groups, tiled=True)
 
@@ -359,11 +386,9 @@
     height, width = sums.shape
     share = height // ways
     pieces = swap_axes(sums.reshape(ways, share, width), both, planes)
-    piece = jnp.sum(pieces.astype(F32), axis=0)
     lines = [[z * CORES + c for z in range(CHIPS)] for c in range(CORES)]
-    pieces = swap_axes(jnp.broadcast_to(piece, (CHIPS, share, width)), "pcol", lines)
-    piece = jnp.sum(pieces, axis=0).astype(BF16)
-    pieces = swap_axes(jnp.broadcast_to(piece, (ways, share, width)), both, planes)
+    pieces = swap_axes(fold(pieces, CHIPS, F32), "pcol", lines)
+    pieces = swap_axes(fold(pieces, ways, BF16), both, planes)
     return pieces.reshape(height, width)
 
 
@@ -378,7 +403,7 @@
 
 
 def spread_plane(low, high):
-    hops = (1, SIDE - 1) + tuple(range(2, SIDE - 1))
+    hops = tuple(range(2, SIDE - 1)) + (1, SIDE - 1)
 
     def around(value, turn):
         moved = {0: value}
@@ -410,6 +435,8 @@
     steps = jnp.arange(BLOCKS, dtype=jnp.int32)
     panels = [panel.reshape(-1, width, width) for panel in (panel_one, panel_two)]
     each = tuple(panel.shape[0] for panel in panels)
+    whole = lax.optimization_barrier(jnp.concatenate([pattern_one, pattern_two]))
+    pattern_one, pattern_two = whole[:pattern_one.shape[0]], whole[pattern_one.shape[0]:]
     found_cols = places(steps * cols_grid + q, pattern_one, pattern_two)
     found_rows = places(steps * rows_grid + p, pattern_one, pattern_two)
     found_other = places(steps * rows_grid + (q - p) % rows_grid, pattern_one, pattern_two)
@@ -418,7 +445,13 @@
     )
     gathered = lax.all_gather(mine, "pcol", axis=0, tiled=True)
 
-    def invert(slots, gathered, found_cols, found_other, found_rows, region, link, inv_one, inv_two):
+    classes = jnp.arange(rows_grid, dtype=jnp.int32)[:, None]
+    members = sum(
+        jnp.sum((lax.rem(pattern, rows_grid)[None, :] == classes).astype(jnp.int32), axis=1)
+        for pattern in (pattern_one, pattern_two)
+    )
+    fits = jnp.all(members <= FEW)
+    def invert(slots, fits, gathered, found_cols, found_other, found_rows, region, link, inv_one, inv_two):
         other, low, high, col_list = pick(slots, each, found_cols, found_other, gathered)
         moves = [
             (a * cols_grid + b, (b - a) % rows_grid * cols_grid + a)
@@ -429,24 +462,19 @@
         keep, give, row_list = product(slots, found_rows, col_list, here, region, lows, highs)
         give, rows = lax.optimization_barrier((give, rows))
         got = lax.ppermute(give, "pcol", [(i, i ^ 1) for i in range(cols_grid)])
-        parts = sum_along_z(keep, got)
+        parts, fits = sum_along_z(keep, got, fits)
         column_one, column_two, sums = columns(row_list, found_rows, parts, rows, link)
         sums = sum_everywhere(sums, rows_grid, cols_grid)
         diagonal_one, cross_two, diagonal_two = diagonals(sums, link, inv_one, inv_two)
-        return (column_one, diagonal_one, column_two, cross_two, diagonal_two)
-
-    classes = jnp.arange(rows_grid, dtype=jnp.int32)[:, None]
-    members = sum(
-        jnp.sum((lax.rem(pattern, rows_grid)[None, :] == classes).astype(jnp.int32), axis=1)
-        for pattern in (pattern_one, pattern_two)
-    )
-    fits = jnp.all(members <= FEW)
+        return (column_one, diagonal_one, column_two, cross_two, diagonal_two), fits
+
     given = (gathered, found_cols, found_other, found_rows, inverse_region, link_block, inv_diag_one, inv_diag_two)
+    outs, fits = invert(FEW, fits, *given)
     return lax.cond(
         fits,
         lambda outs, *given: outs,
-        lambda outs, *given: invert(2 * BLOCKS, *given),
-        invert(FEW, *given), *given,
+        lambda outs, *given: invert(2 * BLOCKS, fits, *given)[0],
+        outs, *given,
     )
 
 

time: 139 us -> 137 us (0.986)
  blocking collectives: 43.3 us -> 56.9 us
  waiting for transfers between devices: 35.1 us -> 25.6 us
  starting transfers between devices: 43 us -> 38.4 us
  local copies, waits for them, and re-layouts: 2.46 us -> 0.75 us
  Pallas kernels: 10.1 us -> 11.5 us
    all_to_all x1 -> x2, blocking collectives: 19.9 us -> 33.4 us  [swap_axes(): lax.all_to_all(value, axes, 0, 0, axis_index_groups=groups, tiled=True)]
    all_to_all x2 -> x1, waiting for transfers between devices: 18.1 us -> 9.58 us  [swap_axes(): lax.all_to_all(value, axes, 0, 0, axis_index_groups=groups, tiled=True)]
    all_to_all x2 -> x1, starting transfers between devices: 9.92 us -> 5.58 us  [swap_axes(): lax.all_to_all(value, axes, 0, 0, axis_index_groups=groups, tiled=True)]
    broadcast_in_dim x2 -> x0, local copies, waits for them, and re-layouts: 1.48 us -> none  [the longest x1 0.78 us: sum_everywhere(): jnp.broadcast_to(piece, (ways, share, width))]
  transfers between devices with their start and end apart: 21 -> 20, of which waited for: 9 -> 8; matrix products, arithmetic and copies ran while one was open for 1% -> 1% of each run, Pallas kernels for 4% -> 4%
where the time goes in v5:
time: 137 us
  blocking collectives  56.9 us (42%)
  starting transfers between devices  38.4 us (28%)
  waiting for transfers between devices  25.6 us (19%)
  Pallas kernels  11.5 us (8%)
  other arithmetic  2.58 us (2%)
  between operations  1.5 us (1%)
    all_to_all x2, blocking collectives, swap_axes(): lax.all_to_all(value, axes, 0, 0, axis_index_groups=groups, tiled=True)  33.4 us
    all_gather x1, blocking collectives, shards(): gathered = lax.all_gather(mine, 'pcol', axis=0, tiled=True)  23.5 us
    ppermute x12, starting transfers between devices, around(): moved[d] = lax.ppermute(value, 'prow', turn(d))  13.9 us
    all_to_all x1, waiting for transfers between devices, swap_axes(): lax.all_to_all(value, axes, 0, 0, axis_index_groups=groups, tiled=True)  9.58 us
    ppermute x1, starting transfers between devices, invert(): rows = lax.ppermute(other, ('prow', 'pcol'), moves)  7.41 us
    ppermute x3, waiting for transfers between devices, sum_along_z(): came = [lax.ppermute(on[i], 'pcol', along_z(ON[i])) for i in (1, 2, 0)]  6.84 us
    pallas_call x1, Pallas kernels, product(): pl.pallas_call(product_kernel, out_shape=(jax.ShapeDtypeStruct(shape, F32...  5.98 us
    all_to_all x1, starting transfers between devices, swap_axes(): lax.all_to_all(value, axes, 0, 0, axis_index_groups=groups, tiled=True)  5.58 us
  transfers between devices with their start and end apart: 20, of which 8 were waited for; matrix products, arithmetic and copies ran while one was open for 1% of the time, Pallas kernels for 4%

profile of v5, /device:TPU:1, one launch (start us, length us, event | category | flops | bytes accessed | tf_op | source)
XLA Modules:
  0.0 137.1 jit_solution(12665903694678839614)
XLA Ops:
  2.3 23.5 %all_gather.3.gathered_ref = bf16[96,16,256]{2,1,0:T(8,128)(2,1)S(1)} all-gather(bf16[6,16,256]{2,1,0:T(8,128)(2,1)S(1)} %pad_maximum_fusion.4), channel_id=1, replica_groups=mesh['prow'=16,'pcol'=16] {'pcol'}, dimensions={0}, use_global_device_ids=true | all-gather | bytes 835584 | tf_op jit(solution)/shard_map/all_gather | solution.py:446
  26.4 1.4 %pick.3 = (bf16[12,16,256]{2,1,0:T(8,128)(2,1)S(1)}, bf16[6,16,256]{2,1,0:T(8,128)(2,1)S(1)}, bf16[6,16,256]{2,1,0:T(8,128)(2,1)S(1)}, s32[33]{0:T(128)S(1)}) custom-call(s32[16]{0:T(128)S(1)} %pad_add_fusion.2.found_ref, s32[16]{0:T(128)S(1)} %pad_add_fusion.3.other_ref, bf16[96,16,256]{2,1,0:T(8,128)(2,1)S(1)} %all_gather.3.gathered_ref), custom_call_target="tpu_custom_call" | custom-call | tf_op jit(solution)/shard_map/pick/pallas_call | solution.py:85
  27.8 2.8 %collective-permute-start.27 = (bf16[6,16,256]{2,1,0:T(8,128)(2,1)S(1)}, bf16[6,16,256]{2,1,0:T(8,128)(2,1)S(1)}, u32[]{:S(2)}, u32[]{:S(2)}) collective-permute-start(bf16[6,16,256]{2,1,0:T(8,128)(2,1)S(1)} %get-tuple-element.91), channel_id=1, source_target_pairs={{0,192},{16,208},{32,224},{48,240},{64,0},{80,16},{96,32},{112,48}... | collective-permute-start | bytes 147464 | tf_op jit(solution)/shard_map/ppermute | solution.py:411
  31.7 2.5 %collective-permute-start.21 = (bf16[6,16,256]{2,1,0:T(8,128)(2,1)S(1)}, bf16[6,16,256]{2,1,0:T(8,128)(2,1)S(1)}, u32[]{:S(2)}, u32[]{:S(2)}) collective-permute-start(bf16[6,16,256]{2,1,0:T(8,128)(2,1)S(1)} %get-tuple-element.90), channel_id=1, source_target_pairs={{0,48},{16,0},{32,16},{48,32},{64,112},{80,64},{96,80},{112,96},{1... | collective-permute-start | bytes 147464 | tf_op jit(solution)/shard_map/ppermute | solution.py:411
  36.1 2.6 %collective-permute-start.30 = (bf16[4,6,16,256]{3,2,1,0:T(8,128)(2,1)S(1)}, bf16[4,6,16,256]{3,2,1,0:T(8,128)(2,1)S(1)}, u32[]{:S(2)}, u32[]{:S(2)}) collective-permute-start(bf16[4,6,16,256]{3,2,1,0:T(8,128)(2,1)S(1)} %pad_maximum_fusion.3.refs_4_), channel_id=1, source_target_pairs={{0,48},{16,0},{32,16},{48,32},{64,112},{80,64},{96,80},{112,96},{1... | collective-permute-start | bytes 589832 | tf_op jit(solution)/shard_map/ppermute | solution.py:411
  39.8 1.4 %collective-permute-start.24 = (bf16[4,6,16,256]{3,2,1,0:T(8,128)(2,1)S(1)}, bf16[4,6,16,256]{3,2,1,0:T(8,128)(2,1)S(1)}, u32[]{:S(2)}, u32[]{:S(2)}) collective-permute-start(bf16[4,6,16,256]{3,2,1,0:T(8,128)(2,1)S(1)} %pad_maximum_fusion.2.refs_0_), channel_id=1, source_target_pairs={{0,192},{16,208},{32,224},{48,240},{64,0},{80,16},{96,32},{112,48}... | collective-permute-start | bytes 589832 | tf_op jit(solution)/shard_map/ppermute | solution.py:411
  41.2 1.4 %collective-permute-start.23 = (bf16[4,6,16,256]{3,2,1,0:T(8,128)(2,1)S(1)}, bf16[4,6,16,256]{3,2,1,0:T(8,128)(2,1)S(1)}, u32[]{:S(2)}, u32[]{:S(2)}) collective-permute-start(bf16[4,6,16,256]{3,2,1,0:T(8,128)(2,1)S(1)} %pad_maximum_fusion.2.refs_0_), channel_id=1, source_target_pairs={{0,128},{16,144},{32,160},{48,176},{64,192},{80,208},{96,224},{112... | collective-permute-start | bytes 589832 | tf_op jit(solution)/shard_map/ppermute | solution.py:411
  43.2 1.9 %collective-permute-done.29.refs_6_ = bf16[4,6,16,256]{3,2,1,0:T(8,128)(2,1)S(1)} collective-permute-done((bf16[4,6,16,256]{3,2,1,0:T(8,128)(2,1)S(1)}, bf16[4,6,16,256]{3,2,1,0:T(8,128)(2,1)S(1)}, u32[]{:S(2)}, u32[]{:S(2)}) %collective-permute-start.29) | collective-permute-done | bytes 196640 | tf_op jit(solution)/shard_map/ppermute | solution.py:411
  45.1 7.4 %collective-permute-start.31 = (bf16[12,16,256]{2,1,0:T(8,128)(2,1)S(1)}, bf16[12,16,256]{2,1,0:T(8,128)(2,1)S(1)}, u32[]{:S(2)}, u32[]{:S(2)}) collective-permute-start(bf16[12,16,256]{2,1,0:T(8,128)(2,1)S(1)} %get-tuple-element.94), channel_id=1, source_target_pairs={{0,0},{1,16},{2,32},{3,48},{4,64},{5,80},{6,96},{7,112},{8,128},{9... | collective-permute-start | bytes 294920 | tf_op jit(solution)/shard_map/ppermute | solution.py:460
  52.5 6.0 %product.3 = (f32[8,12,16,256]{3,2,1,0:T(8,128)S(1)}, bf16[8,12,16,256]{3,2,1,0:T(8,128)(2,1)S(1)}, s32[33]{0:T(128)S(1)}) custom-call(s32[16]{0:T(128)S(1)} %pad_add_fusion.1.rows_ref.found_ref, s32[33]{0:T(128)S(1)} %get-tuple-element.89.cols_ref, s32[4]{0:T(128)S(1)} %pad_add_fusion.4.here_ref, bf16[8,256,8,256]{3,2,1,0:T(8,128)(2,1)} %region_ref.1, ...), custom_call_target="tpu_custom_call" | custom-call | flops 3221225472 | bytes 8388608 | tf_op jit(solution)/shard_map/product/pallas_call | solution.py:184
  58.6 2.4 %collective-permute-start.32 = (bf16[8,12,16,256]{3,2,1,0:T(8,128)(2,1)S(1)}, bf16[8,12,16,256]{3,2,1,0:T(8,128)(2,1)S(1)}, u32[]{:S(2)}, u32[]{:S(2)}) collective-permute-start(bf16[8,12,16,256]{3,2,1,0:T(8,128)(2,1)S(1)} %get-tuple-element.95), channel_id=1, source_target_pairs={{0,1},{1,0},{2,3},{3,2},{4,5},{5,4},{6,7},{7,6},{8,9},{9,8},{10,11... | collective-permute-start | bytes 2359304 | tf_op jit(solution)/shard_map/ppermute | solution.py:464
  61.1 1.8 %collective-permute-done.32.got_ref = bf16[8,12,16,256]{3,2,1,0:T(8,128)(2,1)S(1)} collective-permute-done((bf16[8,12,16,256]{3,2,1,0:T(8,128)(2,1)S(1)}, bf16[8,12,16,256]{3,2,1,0:T(8,128)(2,1)S(1)}, u32[]{:S(2)}, u32[]{:S(2)}) %collective-permute-start.32) | collective-permute-done | bytes 786464 | tf_op jit(solution)/shard_map/ppermute | solution.py:464
  63.0 1.2 collective-permute-start.33
  64.2 3.1 %collective-permute-start.34 = (bf16[2,12,16,256]{3,2,1,0:T(8,128)(2,1)S(1)}, bf16[2,12,16,256]{3,2,1,0:T(8,128)(2,1)S(1)}, u32[]{:S(2)}, u32[]{:S(2)}) collective-permute-start(bf16[2,12,16,256]{3,2,1,0:T(8,128)(2,1)S(1)} %get-tuple-element.103), channel_id=1, source_target_pairs={{0,14},{1,15},{2,0},{3,1},{4,2},{5,3},{6,4},{7,5},{8,6},{9,7},{10,... | collective-permute-start | bytes 589832 | tf_op jit(solution)/shard_map/ppermute | solution.py:260
  68.1 4.3 %collective-permute-done.33.up_ref.refs_1_ = bf16[2,12,16,256]{3,2,1,0:T(8,128)(2,1)S(1)} collective-permute-done((bf16[2,12,16,256]{3,2,1,0:T(8,128)(2,1)S(1)}, bf16[2,12,16,256]{3,2,1,0:T(8,128)(2,1)S(1)}, u32[]{:S(2)}, u32[]{:S(2)}) %collective-permute-start.33) | collective-permute-done | bytes 196640 | tf_op jit(solution)/shard_map/ppermute | solution.py:259
  72.5 2.6 %collective-permute-start.35 = (bf16[12,16,256]{2,1,0:T(8,128)(2,1)S(1)}, bf16[12,16,256]{2,1,0:T(8,128)(2,1)S(1)}, u32[]{:S(2)}, u32[]{:S(2)}) collective-permute-start(bf16[12,16,256]{2,1,0:T(8,128)(2,1)S(1)} %get-tuple-element.104), channel_id=1, source_target_pairs={{0,10},{1,11},{2,12},{3,13},{4,14},{5,15},{6,0},{7,1},{8,2},{9,3},... | collective-permute-start | bytes 294920 | tf_op jit(solution)/shard_map/ppermute | solution.py:263
  77.2 5.3 %collective-permute-done.35.refs_2_ = bf16[12,16,256]{2,1,0:T(8,128)(2,1)S(1)} collective-permute-done((bf16[12,16,256]{2,1,0:T(8,128)(2,1)S(1)}, bf16[12,16,256]{2,1,0:T(8,128)(2,1)S(1)}, u32[]{:S(2)}, u32[]{:S(2)}) %collective-permute-start.35) | collective-permute-done | bytes 98336 | tf_op jit(solution)/shard_map/ppermute | solution.py:263
  82.5 1.5 %collective-permute-done.36.refs_3_ = bf16[12,16,256]{2,1,0:T(8,128)(2,1)S(1)} collective-permute-done((bf16[12,16,256]{2,1,0:T(8,128)(2,1)S(1)}, bf16[12,16,256]{2,1,0:T(8,128)(2,1)S(1)}, u32[]{:S(2)}, u32[]{:S(2)}) %collective-permute-start.36) | collective-permute-done | bytes 98336 | tf_op jit(solution)/shard_map/ppermute | solution.py:263
  84.0 1.5 %columns.3 = (bf16[8,16,256]{2,1,0:T(8,128)(2,1)}, bf16[8,16,256]{2,1,0:T(8,128)(2,1)}, bf16[768,256]{1,0:T(8,128)(2,1)S(1)}) custom-call(s32[33]{0:T(128)S(1)} %get-tuple-element.98.list_ref, s32[16]{0:T(128)S(1)} %pad_add_fusion.1.rows_ref.found_ref, bf16[12,16,256]{2,1,0:T(8,128)(2,1)S(1)} %collective-permute-done.31.rows_ref, ...), custom_call_target="tpu_custom_call" | custom-call | tf_op jit(solution)/shard_map/columns/pallas_call | solution.py:309
  85.5 19.8 %all_to_all.30.pieces_ref = bf16[32,24,256]{2,1,0:T(8,128)(2,1)S(1)} all-to-all(bf16[32,24,256]{2,1,0:T(8,128)(2,1)S(1)} %bitcast.30), channel_id=1, replica_groups={{0,1,16,17,32,33,48,49,64,65,80,81,96,97,112,113,128,129,144,145,160,16..., dimensions={0} | all-to-all | bytes 786432 | tf_op jit(solution)/shard_map/all_to_all | solution.py:376
  105.4 13.6 %all_to_all.31.pieces_ref = f32[8,24,256]{2,1,0:T(8,128)S(1)} all-to-all(f32[8,24,256]{2,1,0:T(8,128)S(1)} %fold.6), channel_id=1, replica_groups={{0,2,4,6,8,10,12,14},{1,3,5,7,9,11,13,15},{16,18,20,22,24,26,28,30},{17..., dimensions={0} | all-to-all | bytes 393216 | tf_op jit(solution)/shard_map/all_to_all | solution.py:376
  119.8 5.6 %all-to-all-start.5 = ((bf16[32,24,256]{2,1,0:T(8,128)(2,1)}), bf16[32,24,256]{2,1,0:T(8,128)(2,1)S(1)}, u32[]{:S(2)}, u32[]{:S(2)}) async-start(bf16[32,24,256]{2,1,0:T(8,128)(2,1)} %fold.7), calls=%async_computation.5 | async-start | bytes 786432 | tf_op jit(solution)/shard_map/all_to_all | solution.py:376
  126.0 9.6 %all-to-all-done.5 = bf16[32,24,256]{2,1,0:T(8,128)(2,1)S(1)} async-done(((bf16[32,24,256]{2,1,0:T(8,128)(2,1)}), bf16[32,24,256]{2,1,0:T(8,128)(2,1)S(1)}, u32[]{:S(2)}, u32[]{:S(2)}) %all-to-all-start.5) | async-done | bytes 393248 | tf_op jit(solution)/shard_map/all_to_all | solution.py:376
  135.6 1.5 %diagonals.3 = (f32[256,256]{1,0:T(8,128)}, f32[256,256]{1,0:T(8,128)}, f32[256,256]{1,0:T(8,128)}) custom-call(bf16[768,256]{1,0:T(8,128)(2,1)S(1)} %bitcast.27, bf16[256,256]{1,0:T(8,128)(2,1)S(1)} %copy-done.1, f32[256,256]{1,0:T(8,128)S(1)} %copy-done.2, f32[256,256]{1,0:T(8,128)S(1)} %copy-done.3), custom_call_target="tpu_custom_call" | custom-call | tf_op jit(solution)/shard_map/diagonals/pallas_call | solution.py:346
  (61 shorter events, 10.9 us)
Async XLA Ops:
  0.6 1.7 %copy-start = (bf16[1024,256]{1,0:T(8,128)(2,1)S(1)}, bf16[1024,256]{1,0:T(8,128)(2,1)}, u32[]{:S(2)}) copy-start(bf16[1024,256]{1,0:T(8,128)(2,1)} %param.11) | copy-start | bytes 1572868
  27.8 6.9 %collective-permute-start.27 = (bf16[6,16,256]{2,1,0:T(8,128)(2,1)S(1)}, bf16[6,16,256]{2,1,0:T(8,128)(2,1)S(1)}, u32[]{:S(2)}, u32[]{:S(2)}) collective-permute-start(bf16[6,16,256]{2,1,0:T(8,128)(2,1)S(1)} %get-tuple-element.91), channel_id=1, source_target_pairs={{0,192},{16,208},{32,224},{48,240},{64,0},{80,16},{96,32},{112,48}... | collective-permute-start | bytes 147464 | tf_op jit(solution)/shard_map/ppermute | solution.py:411
  30.7 4.7 %collective-permute-start.26 = (bf16[6,16,256]{2,1,0:T(8,128)(2,1)S(1)}, bf16[6,16,256]{2,1,0:T(8,128)(2,1)S(1)}, u32[]{:S(2)}, u32[]{:S(2)}) collective-permute-start(bf16[6,16,256]{2,1,0:T(8,128)(2,1)S(1)} %get-tuple-element.91), channel_id=1, source_target_pairs={{0,128},{16,144},{32,160},{48,176},{64,192},{80,208},{96,224},{112... | collective-permute-start | bytes 147464 | tf_op jit(solution)/shard_map/ppermute | solution.py:411
  31.0 5.1 %collective-permute-start.25 = (bf16[6,16,256]{2,1,0:T(8,128)(2,1)S(1)}, bf16[6,16,256]{2,1,0:T(8,128)(2,1)S(1)}, u32[]{:S(2)}, u32[]{:S(2)}) collective-permute-start(bf16[6,16,256]{2,1,0:T(8,128)(2,1)S(1)} %get-tuple-element.91), channel_id=1, source_target_pairs={{0,64},{16,80},{32,96},{48,112},{64,128},{80,144},{96,160},{112,17... | collective-permute-start | bytes 147464 | tf_op jit(solution)/shard_map/ppermute | solution.py:411
  31.7 7.5 %collective-permute-start.21 = (bf16[6,16,256]{2,1,0:T(8,128)(2,1)S(1)}, bf16[6,16,256]{2,1,0:T(8,128)(2,1)S(1)}, u32[]{:S(2)}, u32[]{:S(2)}) collective-permute-start(bf16[6,16,256]{2,1,0:T(8,128)(2,1)S(1)} %get-tuple-element.90), channel_id=1, source_target_pairs={{0,48},{16,0},{32,16},{48,32},{64,112},{80,64},{96,80},{112,96},{1... | collective-permute-start | bytes 147464 | tf_op jit(solution)/shard_map/ppermute | solution.py:411
  34.2 5.6 %collective-permute-start.20 = (bf16[6,16,256]{2,1,0:T(8,128)(2,1)S(1)}, bf16[6,16,256]{2,1,0:T(8,128)(2,1)S(1)}, u32[]{:S(2)}, u32[]{:S(2)}) collective-permute-start(bf16[6,16,256]{2,1,0:T(8,128)(2,1)S(1)} %get-tuple-element.90), channel_id=1, source_target_pairs={{0,32},{16,48},{32,0},{48,16},{64,96},{80,112},{96,64},{112,80},{1... | collective-permute-start | bytes 147464 | tf_op jit(solution)/shard_map/ppermute | solution.py:411
  34.7 5.1 %collective-permute-start.19 = (bf16[6,16,256]{2,1,0:T(8,128)(2,1)S(1)}, bf16[6,16,256]{2,1,0:T(8,128)(2,1)S(1)}, u32[]{:S(2)}, u32[]{:S(2)}) collective-permute-start(bf16[6,16,256]{2,1,0:T(8,128)(2,1)S(1)} %get-tuple-element.90), channel_id=1, source_target_pairs={{0,16},{16,32},{32,48},{48,0},{64,80},{80,96},{96,112},{112,64},{1... | collective-permute-start | bytes 147464 | tf_op jit(solution)/shard_map/ppermute | solution.py:411
  36.1 6.9 %collective-permute-start.30 = (bf16[4,6,16,256]{3,2,1,0:T(8,128)(2,1)S(1)}, bf16[4,6,16,256]{3,2,1,0:T(8,128)(2,1)S(1)}, u32[]{:S(2)}, u32[]{:S(2)}) collective-permute-start(bf16[4,6,16,256]{3,2,1,0:T(8,128)(2,1)S(1)} %pad_maximum_fusion.3.refs_4_), channel_id=1, source_target_pairs={{0,48},{16,0},{32,16},{48,32},{64,112},{80,64},{96,80},{112,96},{1... | collective-permute-start | bytes 589832 | tf_op jit(solution)/shard_map/ppermute | solution.py:411
  38.7 6.4 %collective-permute-start.29 = (bf16[4,6,16,256]{3,2,1,0:T(8,128)(2,1)S(1)}, bf16[4,6,16,256]{3,2,1,0:T(8,128)(2,1)S(1)}, u32[]{:S(2)}, u32[]{:S(2)}) collective-permute-start(bf16[4,6,16,256]{3,2,1,0:T(8,128)(2,1)S(1)} %pad_maximum_fusion.3.refs_4_), channel_id=1, source_target_pairs={{0,32},{16,48},{32,0},{48,16},{64,96},{80,112},{96,64},{112,80},{1... | collective-permute-start | bytes 589832 | tf_op jit(solution)/shard_map/ppermute | solution.py:411
  39.2 13.3 %collective-permute-start.28 = (bf16[4,6,16,256]{3,2,1,0:T(8,128)(2,1)S(1)}, bf16[4,6,16,256]{3,2,1,0:T(8,128)(2,1)S(1)}, u32[]{:S(2)}, u32[]{:S(2)}) collective-permute-start(bf16[4,6,16,256]{3,2,1,0:T(8,128)(2,1)S(1)} %pad_maximum_fusion.3.refs_4_), channel_id=1, source_target_pairs={{0,16},{16,32},{32,48},{48,0},{64,80},{80,96},{96,112},{112,64},{1... | collective-permute-start | bytes 589832 | tf_op jit(solution)/shard_map/ppermute | solution.py:411
  39.8 12.7 %collective-permute-start.24 = (bf16[4,6,16,256]{3,2,1,0:T(8,128)(2,1)S(1)}, bf16[4,6,16,256]{3,2,1,0:T(8,128)(2,1)S(1)}, u32[]{:S(2)}, u32[]{:S(2)}) collective-permute-start(bf16[4,6,16,256]{3,2,1,0:T(8,128)(2,1)S(1)} %pad_maximum_fusion.2.refs_0_), channel_id=1, source_target_pairs={{0,192},{16,208},{32,224},{48,240},{64,0},{80,16},{96,32},{112,48}... | collective-permute-start | bytes 589832 | tf_op jit(solution)/shard_map/ppermute | solution.py:411
  41.2 11.3 %collective-permute-start.23 = (bf16[4,6,16,256]{3,2,1,0:T(8,128)(2,1)S(1)}, bf16[4,6,16,256]{3,2,1,0:T(8,128)(2,1)S(1)}, u32[]{:S(2)}, u32[]{:S(2)}) collective-permute-start(bf16[4,6,16,256]{3,2,1,0:T(8,128)(2,1)S(1)} %pad_maximum_fusion.2.refs_0_), channel_id=1, source_target_pairs={{0,128},{16,144},{32,160},{48,176},{64,192},{80,208},{96,224},{112... | collective-permute-start | bytes 589832 | tf_op jit(solution)/shard_map/ppermute | solution.py:411
  43.0 9.5 %collective-permute-start.22 = (bf16[4,6,16,256]{3,2,1,0:T(8,128)(2,1)S(1)}, bf16[4,6,16,256]{3,2,1,0:T(8,128)(2,1)S(1)}, u32[]{:S(2)}, u32[]{:S(2)}) collective-permute-start(bf16[4,6,16,256]{3,2,1,0:T(8,128)(2,1)S(1)} %pad_maximum_fusion.2.refs_0_), channel_id=1, source_target_pairs={{0,64},{16,80},{32,96},{48,112},{64,128},{80,144},{96,160},{112,17... | collective-permute-start | bytes 589832 | tf_op jit(solution)/shard_map/ppermute | solution.py:411
  45.1 13.5 %collective-permute-start.31 = (bf16[12,16,256]{2,1,0:T(8,128)(2,1)S(1)}, bf16[12,16,256]{2,1,0:T(8,128)(2,1)S(1)}, u32[]{:S(2)}, u32[]{:S(2)}) collective-permute-start(bf16[12,16,256]{2,1,0:T(8,128)(2,1)S(1)} %get-tuple-element.94), channel_id=1, source_target_pairs={{0,0},{1,16},{2,32},{3,48},{4,64},{5,80},{6,96},{7,112},{8,128},{9... | collective-permute-start | bytes 294920 | tf_op jit(solution)/shard_map/ppermute | solution.py:460
  58.5 25.5 %copy-start.1 = (bf16[256,256]{1,0:T(8,128)(2,1)S(1)}, bf16[256,256]{1,0:T(8,128)(2,1)}, u32[]{:S(2)}) copy-start(bf16[256,256]{1,0:T(8,128)(2,1)} %link_ref.3) | copy-start | bytes 393220
  58.6 4.4 %collective-permute-start.32 = (bf16[8,12,16,256]{3,2,1,0:T(8,128)(2,1)S(1)}, bf16[8,12,16,256]{3,2,1,0:T(8,128)(2,1)S(1)}, u32[]{:S(2)}, u32[]{:S(2)}) collective-permute-start(bf16[8,12,16,256]{3,2,1,0:T(8,128)(2,1)S(1)} %get-tuple-element.95), channel_id=1, source_target_pairs={{0,1},{1,0},{2,3},{3,2},{4,5},{5,4},{6,7},{7,6},{8,9},{9,8},{10,11... | collective-permute-start | bytes 2359304 | tf_op jit(solution)/shard_map/ppermute | solution.py:464
  63.0 9.4 %collective-permute-start.33 = (bf16[2,12,16,256]{3,2,1,0:T(8,128)(2,1)S(1)}, bf16[2,12,16,256]{3,2,1,0:T(8,128)(2,1)S(1)}, u32[]{:S(2)}, u32[]{:S(2)}) collective-permute-start(bf16[2,12,16,256]{3,2,1,0:T(8,128)(2,1)S(1)} %get-tuple-element.96), channel_id=1, source_target_pairs={{0,2},{1,3},{2,4},{3,5},{4,6},{5,7},{6,8},{7,9},{8,10},{9,11},{10,... | collective-permute-start | bytes 589832 | tf_op jit(solution)/shard_map/ppermute | solution.py:259
  64.2 8.2 %collective-permute-start.34 = (bf16[2,12,16,256]{3,2,1,0:T(8,128)(2,1)S(1)}, bf16[2,12,16,256]{3,2,1,0:T(8,128)(2,1)S(1)}, u32[]{:S(2)}, u32[]{:S(2)}) collective-permute-start(bf16[2,12,16,256]{3,2,1,0:T(8,128)(2,1)S(1)} %get-tuple-element.103), channel_id=1, source_target_pairs={{0,14},{1,15},{2,0},{3,1},{4,2},{5,3},{6,4},{7,5},{8,6},{9,7},{10,... | collective-permute-start | bytes 589832 | tf_op jit(solution)/shard_map/ppermute | solution.py:260
  72.5 63.1 %copy-start.2 = (f32[256,256]{1,0:T(8,128)S(1)}, f32[256,256]{1,0:T(8,128)}, u32[]{:S(2)}) copy-start(f32[256,256]{1,0:T(8,128)} %inv_one_ref.1) | copy-start | bytes 786436
  72.5 63.1 %copy-start.3 = (f32[256,256]{1,0:T(8,128)S(1)}, f32[256,256]{1,0:T(8,128)}, u32[]{:S(2)}) copy-start(f32[256,256]{1,0:T(8,128)} %inv_two_ref.1) | copy-start | bytes 786436
  72.5 10.0 %collective-permute-start.35 = (bf16[12,16,256]{2,1,0:T(8,128)(2,1)S(1)}, bf16[12,16,256]{2,1,0:T(8,128)(2,1)S(1)}, u32[]{:S(2)}, u32[]{:S(2)}) collective-permute-start(bf16[12,16,256]{2,1,0:T(8,128)(2,1)S(1)} %get-tuple-element.104), channel_id=1, source_target_pairs={{0,10},{1,11},{2,12},{3,13},{4,14},{5,15},{6,0},{7,1},{8,2},{9,3},... | collective-permute-start | bytes 294920 | tf_op jit(solution)/shard_map/ppermute | solution.py:263
  75.1 8.9 %collective-permute-start.36 = (bf16[12,16,256]{2,1,0:T(8,128)(2,1)S(1)}, bf16[12,16,256]{2,1,0:T(8,128)(2,1)S(1)}, u32[]{:S(2)}, u32[]{:S(2)}) collective-permute-start(bf16[12,16,256]{2,1,0:T(8,128)(2,1)S(1)} %get-tuple-element.105), channel_id=1, source_target_pairs={{0,14},{1,15},{2,0},{3,1},{4,2},{5,3},{6,4},{7,5},{8,6},{9,7},{10,... | collective-permute-start | bytes 294920 | tf_op jit(solution)/shard_map/ppermute | solution.py:263
  76.2 7.8 %collective-permute-start.37 = (bf16[12,16,256]{2,1,0:T(8,128)(2,1)S(1)}, bf16[12,16,256]{2,1,0:T(8,128)(2,1)S(1)}, u32[]{:S(2)}, u32[]{:S(2)}) collective-permute-start(bf16[12,16,256]{2,1,0:T(8,128)(2,1)S(1)} %get-tuple-element.106), channel_id=1, source_target_pairs={{0,4},{1,5},{2,6},{3,7},{4,8},{5,9},{6,10},{7,11},{8,12},{9,13},{1... | collective-permute-start | bytes 294920 | tf_op jit(solution)/shard_map/ppermute | solution.py:263
  119.8 15.8 %all-to-all-start.5 = ((bf16[32,24,256]{2,1,0:T(8,128)(2,1)}), bf16[32,24,256]{2,1,0:T(8,128)(2,1)S(1)}, u32[]{:S(2)}, u32[]{:S(2)}) async-start(bf16[32,24,256]{2,1,0:T(8,128)(2,1)} %fold.7), calls=%async_computation.5 | async-start | bytes 786432 | tf_op jit(solution)/shard_map/all_to_all | solution.py:376
